TPU v7x, 32 devices: a whole 2x2x4 slice. The times are simulated.
32 devices in a mesh: dp: 8 (over y, x, core), mp: 4 (over z).
Axes of the slice: x: 2, y: 2, z: 4, core: 2. Of those that a mesh axis runs over, the one named last changes fastest.
Arguments:
- residual_in: float32 [8192, 1024], P(('dp', 'mp')), may hold values from -60 to 60
- cotangent: float32 [8192, 1024], P(('dp', 'mp')), may hold values from -6 to 6
- expert_ids: int32 [8192, 8], P(('dp', 'mp')), may hold values from 0 to 31, all different within a row; in each aligned block of 256 rows (0 to 255, 256 to 511, ...) at most 80 rows name the same one
- attn_gain: float32 [1024], P(('dp', 'mp')), may hold values from 0.5 to 1.5
- query_w: float32 [1024, 1024], P('dp', 'mp'), may hold values from -0.1875 to 0.1875
- key_value_weight: float32 [1024, 1024], P('dp', 'mp'), may hold values from -0.1875 to 0.1875
- output_w: float32 [1024, 1024], P('mp', 'dp'), may hold values from -3 to 3
- moe_gain: float32 [1024], P(('dp', 'mp')), may hold values from 0.5 to 1.5
- router_w: float32 [1024, 32], P(('dp', 'mp')), may hold values from -0.09375 to 0.09375
- gateup_w: float32 [32, 2, 512, 1024], P('dp', None, 'mp'), may hold values from -0.1875 to 0.1875
- down_w: float32 [32, 512, 1024], P('dp', 'mp'), may hold values from -2 to 2
- attn_gain_mean: float32 [1024], P(('dp', 'mp')), may hold values from -384 to 384
- attn_gain_var: float32 [1024], P(('dp', 'mp')), may hold values from 491.52 to 49152
- query_mean: float32 [1024, 1024], P('dp', 'mp'), may hold values from -320 to 320
- query_var: float32 [1024, 1024], P('dp', 'mp'), may hold values from 327.68 to 32768
- key_value_first_moment: float32 [1024, 1024], P('dp', 'mp'), may hold values from -320 to 320
- key_value_second_moment: float32 [1024, 1024], P('dp', 'mp'), may hold values from 327.68 to 32768
- output_mean: float32 [1024, 1024], P('mp', 'dp'), may hold values from -64 to 64
- output_var: float32 [1024, 1024], P('mp', 'dp'), may hold values from 13.1072 to 1310.72
- moe_gain_mean: float32 [1024], P(('dp', 'mp')), may hold values from -256 to 256
- moe_gain_var: float32 [1024], P(('dp', 'mp')), may hold values from 163.84 to 16384
- router_mean: float32 [1024, 32], P(('dp', 'mp')), may hold values from -640 to 640
- router_var: float32 [1024, 32], P(('dp', 'mp')), may hold values from 1310.72 to 131072
- gateup_mean: float32 [32, 2, 512, 1024], P('dp', None, 'mp'), may hold values from -16 to 16
- gateup_var: float32 [32, 2, 512, 1024], P('dp', None, 'mp'), may hold values from 0.8192 to 81.92
- down_mean: float32 [32, 512, 1024], P('dp', 'mp'), may hold values from -1 to 1
- down_var: float32 [32, 512, 1024], P('dp', 'mp'), may hold values from 0.00458752 to 0.458752
Outputs:
- block_out: float32 [8192, 1024], P(('dp', 'mp'))
- input_grad: float32 [8192, 1024], P(('dp', 'mp'))
- attn_gain_grad: float32 [1024], P(('dp', 'mp'))
- attn_gain_new: float32 [1024], P(('dp', 'mp'))
- attn_gain_mean_new: float32 [1024], P(('dp', 'mp'))
- attn_gain_var_new: float32 [1024], P(('dp', 'mp'))
- query_grad: float32 [1024, 1024], P('dp', 'mp')
- query_new: float32 [1024, 1024], P('dp', 'mp')
- query_mean_new: float32 [1024, 1024], P('dp', 'mp')
- query_var_new: float32 [1024, 1024], P('dp', 'mp')
- keyval_grad: float32 [1024, 1024], P('dp', 'mp')
- keyval_new: float32 [1024, 1024], P('dp', 'mp')
- keyval_mean_new: float32 [1024, 1024], P('dp', 'mp')
- keyval_var_new: float32 [1024, 1024], P('dp', 'mp')
- output_grad: float32 [1024, 1024], P('mp', 'dp')
- output_new: float32 [1024, 1024], P('mp', 'dp')
- output_mean_new: float32 [1024, 1024], P('mp', 'dp')
- output_var_new: float32 [1024, 1024], P('mp', 'dp')
- moe_gain_grad: float32 [1024], P(('dp', 'mp'))
- moe_gain_new: float32 [1024], P(('dp', 'mp'))
- moe_gain_mean_new: float32 [1024], P(('dp', 'mp'))
- moe_gain_var_new: float32 [1024], P(('dp', 'mp'))
- router_grad: float32 [1024, 32], P(('dp', 'mp'))
- router_new: float32 [1024, 32], P(('dp', 'mp'))
- router_mean_new: float32 [1024, 32], P(('dp', 'mp'))
- router_var_new: float32 [1024, 32], P(('dp', 'mp'))
- gateup_grad: float32 [32, 2, 512, 1024], P('dp', None, 'mp')
- gateup_new: float32 [32, 2, 512, 1024], P('dp', None, 'mp')
- gateup_mean_new: float32 [32, 2, 512, 1024], P('dp', None, 'mp')
- gateup_var_new: float32 [32, 2, 512, 1024], P('dp', None, 'mp')
- down_grad: float32 [32, 512, 1024], P('dp', 'mp')
- down_new: float32 [32, 512, 1024], P('dp', 'mp')
- down_mean_new: float32 [32, 512, 1024], P('dp', 'mp')
- down_var_new: float32 [32, 512, 1024], P('dp', 'mp')
Inputs may be any that keep to these rules, and one draw needn't show every extreme that they name: `expert_ids`: the 8 experts of a row differ. Among the 256 rows of one device (aligned blocks of rows) no expert is named more than 80 times, a bound that some block reaches.
All inputs are finite; a program needn't handle non-finite values.
Results may differ from a plain program's by a relative error of at most 0.02.
Values may be sent and summed in bfloat16 or wider, within the bound.
A program may use at most 256 MiB of HBM per device.

v0:
```python
import math

import jax
import jax.numpy as jnp
from jax import lax
from jax.sharding import PartitionSpec as P

MODEL_WIDTH = 1024
QUERY_HEADS = 16
KEY_VALUE_HEADS = 8
HEAD_SIZE = 64
EXPERTS = 32
TOPK = 8
SEQUENCE_TOKENS = 512
STEP = 3
CAP = 80


NORM_EPS = 1e-06


def apply_rotary_embedding(value, direction):
    length = value.shape[1]
    width = value.shape[-1]
    half_width = width // 2
    position = jnp.arange(length, dtype=jnp.float32)
    frequency = jnp.exp(
        -math.log(10000.0) * jnp.arange(half_width, dtype=jnp.float32) * 2.0 / width
    )
    angles = position[:, None] * frequency[None, :]
    cosine = jnp.cos(angles)[:, None, :]
    sine_val = direction * jnp.sin(angles)[:, None, :]
    front = value[..., :half_width]
    rear = value[..., half_width:]
    return jnp.concatenate([front * cosine - rear * sine_val, rear * cosine + front * sine_val], -1)


def causal_mask(length):
    index = jnp.arange(length, dtype=jnp.int32)
    return index[:, None] >= index[None, :]


def rows_gather(value):
    return lax.all_gather(value, "mp", axis=0, tiled=True)


def rows_sum(value):
    return lax.psum_scatter(value, "mp", scatter_dimension=0, tiled=True)


def to_owner(buffer):
    return lax.all_to_all(buffer, "dp", split_axis=0, concat_axis=1, tiled=True)


def from_owner(buffer):
    return lax.all_to_all(buffer, "dp", split_axis=1, concat_axis=0, tiled=True)


def adamw(weight, gradient, moment_one, moment_two, rate_val, decay_val):
    first_new = 0.9 * moment_one + 0.1 * gradient
    second_new = 0.95 * moment_two + 0.05 * gradient * gradient
    first_hat = first_new / (1.0 - 0.9**STEP)
    second_hat = second_new / (1.0 - 0.95**STEP)
    weight_new = weight - rate_val * (
        first_hat / (jnp.sqrt(second_hat) + 1e-08) + decay_val * weight
    )
    return (gradient, weight_new, first_new, second_new)


def local(
    residual_in,
    cotangent,
    expert_ids,
    attn_gain,
    query_w,
    key_value_weight,
    output_w,
    moe_gain,
    router_w,
    gateup_w,
    down_w,
    attn_gain_mean,
    attn_gain_var,
    query_mean,
    query_var,
    key_value_first_moment,
    key_value_second_moment,
    output_mean,
    output_var,
    moe_gain_mean,
    moe_gain_var,
    router_mean,
    router_var,
    gateup_mean,
    gateup_var,
    down_mean,
    down_var,
):
    gain_one, gain_two, router_full = (
        lax.all_gather(attn_gain, ("dp", "mp"), axis=0, tiled=True),
        lax.all_gather(moe_gain, ("dp", "mp"), axis=0, tiled=True),
        lax.all_gather(router_w, ("dp", "mp"), axis=0, tiled=True),
    )
    query_part, keyval_part, output_part = (
        lax.all_gather(query_w.astype(jnp.bfloat16), "dp", axis=0, tiled=True),
        lax.all_gather(key_value_weight.astype(jnp.bfloat16), "dp", axis=0, tiled=True),
        lax.all_gather(output_w.astype(jnp.bfloat16), "dp", axis=1, tiled=True),
    )
    gateup_full, down_full = (
        lax.all_gather(gateup_w.astype(jnp.bfloat16), "mp", axis=2, tiled=True),
        lax.all_gather(down_w.astype(jnp.bfloat16), "mp", axis=1, tiled=True),
    )
    router_low = router_full.astype(jnp.bfloat16)
    rows_own = residual_in.shape[0]
    inv_one = lax.rsqrt(jnp.mean(residual_in * residual_in, -1, keepdims=True) + NORM_EPS)
    first_normed_input = (residual_in * inv_one * gain_one).astype(jnp.bfloat16)
    normed_all = rows_gather(first_normed_input)
    total_rows = normed_all.shape[0]
    sequence_count = total_rows // SEQUENCE_TOKENS
    queries_per_group = QUERY_HEADS // KEY_VALUE_HEADS
    heads_kv = keyval_part.shape[1] // (2 * HEAD_SIZE)
    score_scale = 1.0 / math.sqrt(HEAD_SIZE)
    causal = causal_mask(SEQUENCE_TOKENS)
    query_linear = jnp.dot(normed_all, query_part, preferred_element_type=jnp.float32)
    key_value_linear = jnp.dot(normed_all, keyval_part, preferred_element_type=jnp.float32).reshape(
        sequence_count, SEQUENCE_TOKENS, heads_kv, 2, HEAD_SIZE
    )
    query_rows = (
        apply_rotary_embedding(
            query_linear.reshape(
                sequence_count, SEQUENCE_TOKENS, heads_kv * queries_per_group, HEAD_SIZE
            ),
            1.0,
        )
        .astype(jnp.bfloat16)
        .reshape(sequence_count, SEQUENCE_TOKENS, heads_kv, queries_per_group, HEAD_SIZE)
    )
    keys_rot = apply_rotary_embedding(key_value_linear[:, :, :, 0], 1.0).astype(jnp.bfloat16)
    values = key_value_linear[:, :, :, 1].astype(jnp.bfloat16)
    raw_scores = (
        jnp.einsum("nqkgd,nskd->nkgqs", query_rows, keys_rot, preferred_element_type=jnp.float32)
        * score_scale
    )
    exp_scores = jnp.where(causal, jnp.exp(jnp.where(causal, raw_scores, 0.0)), 0.0)
    row_total = jnp.sum(exp_scores, -1, keepdims=True)
    log_total = jnp.log(row_total)
    attn_probs = (exp_scores / row_total).astype(jnp.bfloat16)
    context = (
        jnp.einsum("nkgqs,nskd->nqkgd", attn_probs, values, preferred_element_type=jnp.float32)
        .astype(jnp.bfloat16)
        .reshape(total_rows, -1)
    )
    attn_out = rows_sum(jnp.dot(context, output_part, preferred_element_type=jnp.float32))
    hidden = residual_in + attn_out
    inv_two = lax.rsqrt(jnp.mean(hidden * hidden, -1, keepdims=True) + NORM_EPS)
    normed_two = (hidden * inv_two * gain_two).astype(jnp.bfloat16)
    logits = jnp.dot(normed_two, router_low, preferred_element_type=jnp.float32)
    exp_logits = jnp.exp(logits)
    router_probs = exp_logits / jnp.sum(exp_logits, -1, keepdims=True)
    expert_range = jnp.arange(EXPERTS, dtype=jnp.int32)
    onehot = (expert_ids[:, :, None] == expert_range[None, None, :]).astype(jnp.int32)
    onehot_float = onehot.astype(jnp.float32)
    picked = jnp.sum(onehot_float * router_probs[:, None, :], -1)
    chosen = jnp.sum(onehot, 1)
    before = jnp.cumsum(chosen, 0) - chosen
    slot_index = jnp.sum(onehot * before[:, None, :], -1)
    flat_slot = (expert_ids * CAP + slot_index).reshape(-1)
    token_index = jnp.repeat(jnp.arange(rows_own, dtype=jnp.int32), TOPK)
    source = jnp.full((EXPERTS * CAP,), rows_own, jnp.int32).at[flat_slot].set(token_index)
    padded = jnp.concatenate([normed_two, jnp.zeros((1, MODEL_WIDTH), jnp.bfloat16)], 0)
    dispatch = padded[source].reshape(EXPERTS, CAP, MODEL_WIDTH)
    received = to_owner(dispatch)
    gate_up = jnp.einsum(
        "erd,ecfd->ercf", received, gateup_full, preferred_element_type=jnp.float32
    )
    gate_val = gate_up[:, :, 0]
    up_val = gate_up[:, :, 1]
    sigmoid_val = jax.nn.sigmoid(gate_val)
    silu_val = gate_val * sigmoid_val
    activation = (silu_val * up_val).astype(jnp.bfloat16)
    expert_out = jnp.einsum(
        "erf,efd->erd", activation, down_full, preferred_element_type=jnp.float32
    ).astype(jnp.bfloat16)
    returned = from_owner(expert_out).reshape(EXPERTS * CAP, MODEL_WIDTH)
    picked_rows = returned[flat_slot].reshape(rows_own, TOPK, MODEL_WIDTH)
    mixture = jnp.sum(picked[:, :, None] * picked_rows, 1)
    block_out = hidden + mixture
    gate_dot = jnp.sum(cotangent[:, None, :] * picked_rows, -1)
    grad_rows = (picked[:, :, None] * cotangent[:, None, :]).astype(jnp.bfloat16)
    grad_buffer = (
        jnp.zeros((EXPERTS * CAP, MODEL_WIDTH), jnp.bfloat16)
        .at[flat_slot]
        .set(grad_rows.reshape(-1, MODEL_WIDTH))
        .reshape(EXPERTS, CAP, MODEL_WIDTH)
    )
    grad_recv = to_owner(grad_buffer)
    grad_act = jnp.einsum("erd,efd->erf", grad_recv, down_full, preferred_element_type=jnp.float32)
    grad_down = jnp.einsum(
        "erf,erd->efd", activation, grad_recv, preferred_element_type=jnp.float32
    )
    grad_gate = grad_act * up_val * sigmoid_val * (1.0 + gate_val * (1.0 - sigmoid_val))
    grad_up = grad_act * silu_val
    grad_pair = jnp.stack([grad_gate, grad_up], 2).astype(jnp.bfloat16)
    grad_slots = jnp.einsum(
        "ercf,ecfd->erd", grad_pair, gateup_full, preferred_element_type=jnp.float32
    ).astype(jnp.bfloat16)
    grad_gateup = jnp.einsum(
        "ercf,erd->ecfd", grad_pair, received, preferred_element_type=jnp.float32
    )
    returned_grad = from_owner(grad_slots).reshape(EXPERTS * CAP, MODEL_WIDTH)
    grad_normed_two = jnp.sum(
        returned_grad[flat_slot].reshape(rows_own, TOPK, MODEL_WIDTH), 1, dtype=jnp.float32
    )
    grad_probs = jnp.sum(onehot_float * gate_dot[:, :, None], 1)
    grad_logits = (
        router_probs * (grad_probs - jnp.sum(router_probs * grad_probs, -1, keepdims=True))
    ).astype(jnp.bfloat16)
    grad_normed_two = grad_normed_two + jnp.einsum(
        "te,de->td", grad_logits, router_low, preferred_element_type=jnp.float32
    )
    grad_router = jnp.einsum(
        "td,te->de", normed_two, grad_logits, preferred_element_type=jnp.float32
    )
    scaled_two = gain_two * grad_normed_two
    grad_hidden = (
        cotangent
        + inv_two * scaled_two
        - hidden * inv_two**3 * jnp.mean(scaled_two * hidden, -1, keepdims=True)
    )
    grad_gain_two = jnp.sum(grad_normed_two * hidden * inv_two, 0)
    grad_attn = grad_hidden.astype(jnp.bfloat16)
    grad_attn_all = rows_gather(grad_attn)
    grad_ctx = jnp.einsum(
        "td,cd->tc", grad_attn_all, output_part, preferred_element_type=jnp.float32
    ).astype(jnp.bfloat16)
    grad_output = jnp.einsum(
        "tc,td->cd", context, grad_attn_all, preferred_element_type=jnp.float32
    )
    grad_ctx = grad_ctx.reshape(
        sequence_count, SEQUENCE_TOKENS, heads_kv, queries_per_group, HEAD_SIZE
    )
    scores_again = (
        jnp.einsum("nqkgd,nskd->nkgqs", query_rows, keys_rot, preferred_element_type=jnp.float32)
        * score_scale
    )
    probs_float = jnp.where(causal, jnp.exp(jnp.where(causal, scores_again - log_total, 0.0)), 0.0)
    probs_low = probs_float.astype(jnp.bfloat16)
    grad_p = jnp.einsum("nqkgd,nskd->nkgqs", grad_ctx, values, preferred_element_type=jnp.float32)
    delta_sum = jnp.sum(probs_float * grad_p, -1, keepdims=True)
    grad_s = (probs_float * (grad_p - delta_sum)).astype(jnp.bfloat16)
    grad_q = (
        jnp.einsum("nkgqs,nskd->nqkgd", grad_s, keys_rot, preferred_element_type=jnp.float32)
        * score_scale
    )
    grad_k = (
        jnp.einsum("nkgqs,nqkgd->nskd", grad_s, query_rows, preferred_element_type=jnp.float32)
        * score_scale
    )
    grad_v = jnp.einsum(
        "nkgqs,nqkgd->nskd", probs_low, grad_ctx, preferred_element_type=jnp.float32
    )
    grad_q_lin = (
        apply_rotary_embedding(
            grad_q.reshape(
                sequence_count, SEQUENCE_TOKENS, heads_kv * queries_per_group, HEAD_SIZE
            ),
            -1.0,
        )
        .astype(jnp.bfloat16)
        .reshape(total_rows, -1)
    )
    grad_kv_lin = (
        jnp.stack([apply_rotary_embedding(grad_k, -1.0), grad_v], 3)
        .astype(jnp.bfloat16)
        .reshape(total_rows, -1)
    )
    grad_normed_part = jnp.einsum(
        "tc,dc->td", grad_q_lin, query_part, preferred_element_type=jnp.float32
    ) + jnp.einsum("tc,dc->td", grad_kv_lin, keyval_part, preferred_element_type=jnp.float32)
    grad_normed_one = rows_sum(grad_normed_part)
    grad_query = jnp.einsum("td,tc->dc", normed_all, grad_q_lin, preferred_element_type=jnp.float32)
    grad_keyval = jnp.einsum(
        "td,tc->dc", normed_all, grad_kv_lin, preferred_element_type=jnp.float32
    )
    scaled_one = gain_one * grad_normed_one
    input_grad = (
        grad_hidden
        + inv_one * scaled_one
        - residual_in * inv_one**3 * jnp.mean(scaled_one * residual_in, -1, keepdims=True)
    )
    grad_gain_one = jnp.sum(grad_normed_one * residual_in * inv_one, 0)
    gain_one_grad, gain_two_grad, router_grad = (
        lax.psum_scatter(grad_gain_one, ("dp", "mp"), scatter_dimension=0, tiled=True),
        lax.psum_scatter(grad_gain_two, ("dp", "mp"), scatter_dimension=0, tiled=True),
        lax.psum_scatter(grad_router, ("dp", "mp"), scatter_dimension=0, tiled=True),
    )
    query_grad, keyval_grad, output_grad = (
        lax.psum_scatter(grad_query, "dp", scatter_dimension=0, tiled=True),
        lax.psum_scatter(grad_keyval, "dp", scatter_dimension=0, tiled=True),
        lax.psum_scatter(grad_output, "dp", scatter_dimension=1, tiled=True),
    )
    gateup_grad, down_grad = (
        lax.psum_scatter(
            grad_gateup.astype(jnp.bfloat16), "mp", scatter_dimension=2, tiled=True
        ).astype(jnp.float32),
        lax.psum_scatter(
            grad_down.astype(jnp.bfloat16), "mp", scatter_dimension=1, tiled=True
        ).astype(jnp.float32),
    )
    matrix_rate = 0.2 / math.sqrt(MODEL_WIDTH)
    gain_one_all = adamw(attn_gain, gain_one_grad, attn_gain_mean, attn_gain_var, 0.1, 0.0)
    query_all = adamw(query_w, query_grad, query_mean, query_var, matrix_rate, 0.1)
    keyval_all = adamw(
        key_value_weight,
        keyval_grad,
        key_value_first_moment,
        key_value_second_moment,
        matrix_rate,
        0.1,
    )
    output_all = adamw(output_w, output_grad, output_mean, output_var, 0.1, 0.1)
    gain_two_all = adamw(moe_gain, gain_two_grad, moe_gain_mean, moe_gain_var, 0.1, 0.0)
    router_all = adamw(router_w, router_grad, router_mean, router_var, matrix_rate, 0.1)
    gateup_all = adamw(gateup_w, gateup_grad, gateup_mean, gateup_var, matrix_rate, 0.1)
    down_all = adamw(down_w, down_grad, down_mean, down_var, 0.07, 0.1)
    return (
        block_out,
        input_grad,
        gain_one_all[0],
        gain_one_all[1],
        gain_one_all[2],
        gain_one_all[3],
        query_all[0],
        query_all[1],
        query_all[2],
        query_all[3],
        keyval_all[0],
        keyval_all[1],
        keyval_all[2],
        keyval_all[3],
        output_all[0],
        output_all[1],
        output_all[2],
        output_all[3],
        gain_two_all[0],
        gain_two_all[1],
        gain_two_all[2],
        gain_two_all[3],
        router_all[0],
        router_all[1],
        router_all[2],
        router_all[3],
        gateup_all[0],
        gateup_all[1],
        gateup_all[2],
        gateup_all[3],
        down_all[0],
        down_all[1],
        down_all[2],
        down_all[3],
    )


def solution(mesh):
    in_specs = (
        P(("dp", "mp"), None),
        P(("dp", "mp"), None),
        P(("dp", "mp"), None),
        P(("dp", "mp")),
        P("dp", "mp"),
        P("dp", "mp"),
        P("mp", "dp"),
        P(("dp", "mp")),
        P(("dp", "mp"), None),
        P("dp", None, "mp", None),
        P("dp", "mp", None),
        P(("dp", "mp")),
        P(("dp", "mp")),
        P("dp", "mp"),
        P("dp", "mp"),
        P("dp", "mp"),
        P("dp", "mp"),
        P("mp", "dp"),
        P("mp", "dp"),
        P(("dp", "mp")),
        P(("dp", "mp")),
        P(("dp", "mp"), None),
        P(("dp", "mp"), None),
        P("dp", None, "mp", None),
        P("dp", None, "mp", None),
        P("dp", "mp", None),
        P("dp", "mp", None),
    )
    out_specs = (
        P(("dp", "mp"), None),
        P(("dp", "mp"), None),
        P(("dp", "mp")),
        P(("dp", "mp")),
        P(("dp", "mp")),
        P(("dp", "mp")),
        P("dp", "mp"),
        P("dp", "mp"),
        P("dp", "mp"),
        P("dp", "mp"),
        P("dp", "mp"),
        P("dp", "mp"),
        P("dp", "mp"),
        P("dp", "mp"),
        P("mp", "dp"),
        P("mp", "dp"),
        P("mp", "dp"),
        P("mp", "dp"),
        P(("dp", "mp")),
        P(("dp", "mp")),
        P(("dp", "mp")),
        P(("dp", "mp")),
        P(("dp", "mp"), None),
        P(("dp", "mp"), None),
        P(("dp", "mp"), None),
        P(("dp", "mp"), None),
        P("dp", None, "mp", None),
        P("dp", None, "mp", None),
        P("dp", None, "mp", None),
        P("dp", None, "mp", None),
        P("dp", "mp", None),
        P("dp", "mp", None),
        P("dp", "mp", None),
        P("dp", "mp", None),
    )
    return jax.shard_map(local, mesh=mesh, in_specs=in_specs, out_specs=out_specs, check_vma=False)
```

profile of v0, /device:TPU:0, one launch (start us, length us, event | category | flops | bytes accessed | tf_op | source)
XLA Modules:
  0.0 1253.8 jit_solution(5876413164302833801)
XLA Ops:
  10.9 42.1 %all-reduce.6 = (f32[1024]{0:T(1024)S(1)}, f32[1024]{0:T(1024)S(1)}) all-reduce(f32[1024]{0:T(1024)S(1)} %dynamic-update-slice, f32[1024]{0:T(1024)S(1)} %dynamic-update-slice.1), channel_id=1, replica_groups=mesh['dp'=8,'mp'=4] {'dp','mp'}, use_global_device_ids=true, to_apply=%add.1 | all-reduce | flops 2048 | bytes 16384
  77.5 11.2 all_gather.34
  89.7 11.3 all-gather.5.cloned.1.call-done
  139.5 61.0 %reduce-scatter.9.cloned.1.call-done = f32[256,1024]{1,0:T(8,128)} async-done(((f32[1024,1024]{1,0:T(8,128)}), f32[256,1024]{1,0:T(8,128)}) %reduce-scatter.9.cloned.1.call-update) | async-done | bytes 1048592 | tf_op jit(solution)/shard_map/reduce_scatter | solution.py:48
  219.2 82.8 %all_gather.36 = bf16[1024,32]{1,0:T(8,128)(2,1)S(1)} all-gather(bf16[32,32]{1,0:T(8,128)(2,1)S(1)} %convert.92), channel_id=1, replica_groups=mesh['dp'=8,'mp'=4] {'dp','mp'}, dimensions={0}, use_global_device_ids=true | all-gather | bytes 67584 | tf_op jit(solution)/shard_map/all_gather | solution.py:102
  303.2 14.0 %scatter_custom_fusion.1 = bf16[2560,1024]{1,0:T(8,128)(2,1)} fusion(s32[2048]{0:T(1024)} %bitcast.253, f32[256,1024]{1,0:T(8,128)S(1)} %copy-done.5, f32[2048]{0:T(1024)S(1)} %mul.780, bf16[]{:T(256)} %constant.31.clone.1), kind=kCustom, calls=%fused_computation.41 | custom fusion | flops 4194304 | bytes 6300160 | tf_op jit(solution)/shard_map/scatter | solution.py:193
  327.7 54.7 %all-to-all-done.2 = bf16[32,80,1024]{2,1,0:T(8,128)(2,1)} async-done(((bf16[32,80,1024]{2,1,0:T(8,128)(2,1)}), bf16[32,80,1024]{2,1,0:T(8,128)(2,1)}, u32[]{:S(2)}, u32[]{:S(2)}) %all-to-all-start.2) | async-done | bytes 5242912 | tf_op jit(solution)/shard_map/all_to_all | solution.py:52
  388.1 12.1 fusion.87
  400.2 39.2 %all-gather.9.cloned.1.call-done = bf16[4,512,1024]{2,1,0:T(8,128)(2,1)} async-done(((bf16[4,128,1024]{2,1,0:T(8,128)(2,1)}), bf16[4,512,1024]{2,1,0:T(8,128)(2,1)}) %all-gather.9.cloned.1.call-update) | async-done | bytes 4194320 | tf_op jit(solution)/shard_map/all_gather | solution.py:111
  450.3 11.3 bitcast_convert_fusion
  484.9 48.2 %all-to-all-done.3 = bf16[4,640,1024]{2,0,1:T(4,128)(2,1)} async-done(((bf16[4,640,1024]{2,0,1:T(4,128)(2,1)}), bf16[4,640,1024]{2,0,1:T(4,128)(2,1)}, u32[]{:S(2)}, u32[]{:S(2)}) %all-to-all-start.3) | async-done | bytes 5242912 | tf_op jit(solution)/shard_map/all_to_all | solution.py:56
  545.8 14.1 %gather_fusion.2 = bf16[2048,1024]{1,0:T(8,128)(2,1)} fusion(bf16[2560,1024]{1,0:T(8,128)(2,1)} %bitcast.230, s32[2048]{0:T(1024)S(1)} %broadcast_clamp_fusion), kind=kCustom, calls=%fused_computation.2 | custom fusion | bytes 8396800 | tf_op jit(solution)/shard_map/gather | solution.py:212
  566.3 31.9 %all-to-all-done.1 = bf16[4,640,1024]{2,0,1:T(4,128)(2,1)} async-done(((bf16[4,640,1024]{2,0,1:T(4,128)(2,1)}), bf16[4,640,1024]{2,0,1:T(4,128)(2,1)}, u32[]{:S(2)}, u32[]{:S(2)}) %all-to-all-start.1) | async-done | bytes 5242912 | tf_op jit(solution)/shard_map/all_to_all | solution.py:56
  604.9 14.1 %gather_fusion.1 = bf16[2048,1024]{1,0:T(8,128)(2,1)} fusion(bf16[2560,1024]{1,0:T(8,128)(2,1)} %bitcast.229, s32[2048]{0:T(1024)S(1)} %broadcast_clamp_fusion), kind=kCustom, calls=%fused_computation.1 | custom fusion | bytes 8396800 | tf_op jit(solution)/shard_map/gather | solution.py:185
  644.0 31.5 %all-gather.11.cloned.1.call-done = bf16[1024,1024]{1,0:T(8,128)(2,1)} async-done(((bf16[256,1024]{1,0:T(8,128)(2,1)}), bf16[1024,1024]{1,0:T(8,128)(2,1)}) %all-gather.11.cloned.1.call-update) | async-done | bytes 2097168 | tf_op jit(solution)/shard_map/all_gather | solution.py:44
  717.2 11.9 convolution_convert_fusion
  729.1 82.4 %reduce-scatter.19.cloned.1.call-done = f32[32,32]{1,0:T(8,128)} async-done(((f32[1024,32]{1,0:T(8,128)}), f32[32,32]{1,0:T(8,128)}) %reduce-scatter.19.cloned.1.call-update) | async-done | bytes 4112 | tf_op jit(solution)/shard_map/reduce_scatter | solution.py:295
  812.9 74.3 %reduce-scatter.23.cloned.1.call-done = bf16[4,128,1024]{2,1,0:T(8,128)(2,1)} async-done(((bf16[4,512,1024]{2,1,0:T(8,128)(2,1)}), bf16[4,128,1024]{2,1,0:T(8,128)(2,1)}) %reduce-scatter.23.cloned.1.call-update) | async-done | bytes 1048592 | tf_op jit(solution)/shard_map/reduce_scatter | solution.py:306
  893.9 34.6 %reduce-scatter.13.cloned.1.call-done = f32[128,256]{1,0:T(8,128)} async-done(((f32[1024,256]{1,0:T(8,128)}), f32[128,256]{1,0:T(8,128)}) %reduce-scatter.13.cloned.1.call-update) | async-done | bytes 131088 | tf_op jit(solution)/shard_map/reduce_scatter | solution.py:298
  930.3 38.3 %reduce-scatter.15.cloned.1.call-done = f32[128,256]{1,0:T(8,128)} async-done(((f32[1024,256]{1,0:T(8,128)}), f32[128,256]{1,0:T(8,128)}) %reduce-scatter.15.cloned.1.call-update) | async-done | bytes 131088 | tf_op jit(solution)/shard_map/reduce_scatter | solution.py:299
  970.4 38.2 %reduce-scatter.17.cloned.1.call-done = f32[256,128]{1,0:T(8,128)} async-done(((f32[256,1024]{1,0:T(8,128)}), f32[256,128]{1,0:T(8,128)}) %reduce-scatter.17.cloned.1.call-update) | async-done | bytes 131088 | tf_op jit(solution)/shard_map/reduce_scatter | solution.py:300
  1010.4 77.9 %reduce-scatter.11.cloned.1.call-done = f32[256,1024]{1,0:T(8,128)} async-done(((f32[1024,1024]{1,0:T(8,128)}), f32[256,1024]{1,0:T(8,128)}) %reduce-scatter.11.cloned.1.call-update) | async-done | bytes 1048592 | tf_op jit(solution)/shard_map/reduce_scatter | solution.py:48
  1089.9 43.5 %all-reduce.5 = (f32[1024]{0:T(1024)S(1)}, f32[1024]{0:T(1024)S(1)}) all-reduce(f32[1024]{0:T(1024)S(1)} %get-tuple-element.38, f32[1024]{0:T(1024)S(1)} %copy-done.50), channel_id=4, replica_groups=mesh['dp'=8,'mp'=4] {'dp','mp'}, use_global_device_ids=true, to_apply=%region_22.23.clone | all-reduce | flops 2048 | bytes 16384
  1136.5 100.1 %reduce-scatter.21.cloned.1.call-done = bf16[4,2,128,1024]{3,2,1,0:T(8,128)(2,1)} async-done(((bf16[4,2,512,1024]{3,2,1,0:T(8,128)(2,1)}), bf16[4,2,128,1024]{3,2,1,0:T(8,128)(2,1)}) %reduce-scatter.21.cloned.1.call-update) | async-done | bytes 2097168 | tf_op jit(solution)/shard_map/reduce_scatter | solution.py:303
  (277 shorter events, 257.7 us)
Async XLA Ops:
  7.2 93.9 %all-gather.5.cloned.1.call-start = ((), (), s32[]{:S(2)}) async-start(), calls=%async_computation.12 | async-start | bytes 2621440 | tf_op jit(solution)/shard_map/all_gather | solution.py:44
  55.2 145.3 %reduce-scatter.9.cloned.1.call-start = ((), (), s32[]{:S(2)}) async-start(), calls=%async_computation.13 | async-start | bytes 5242880 | tf_op jit(solution)/shard_map/reduce_scatter | solution.py:48
  124.8 263.3 %all-gather.7.cloned.1.call-start = ((), (), s32[]{:S(2)}) async-start(), calls=%async_computation.14 | async-start | bytes 10485760 | tf_op jit(solution)/shard_map/all_gather | solution.py:110
  211.5 105.7 %all-to-all-start = ((bf16[32,80,1024]{2,1,0:T(8,128)(2,1)}), bf16[32,80,1024]{2,1,0:T(8,128)(2,1)}, u32[]{:S(2)}, u32[]{:S(2)}) async-start(bf16[32,80,1024]{2,1,0:T(8,128)(2,1)} %bitcast.231), calls=%async_computation.1 | async-start | bytes 10485760 | tf_op jit(solution)/shard_map/all_to_all | solution.py:52
  216.2 223.2 %all-gather.9.cloned.1.call-start = ((), (), s32[]{:S(2)}) async-start(), calls=%async_computation.15 | async-start | bytes 5242880 | tf_op jit(solution)/shard_map/all_gather | solution.py:111
  317.2 65.2 %all-to-all-start.2 = ((bf16[32,80,1024]{2,1,0:T(8,128)(2,1)}), bf16[32,80,1024]{2,1,0:T(8,128)(2,1)}, u32[]{:S(2)}, u32[]{:S(2)}) async-start(bf16[32,80,1024]{2,1,0:T(8,128)(2,1)} %bitcast.232), calls=%async_computation.3 | async-start | bytes 10485760 | tf_op jit(solution)/shard_map/all_to_all | solution.py:52
  468.1 65.0 %all-to-all-start.3 = ((bf16[4,640,1024]{2,0,1:T(4,128)(2,1)}), bf16[4,640,1024]{2,0,1:T(4,128)(2,1)}, u32[]{:S(2)}, u32[]{:S(2)}) async-start(bf16[4,640,1024]{2,0,1:T(4,128)(2,1)} %copy.199), calls=%async_computation.4 | async-start | bytes 10485760 | tf_op jit(solution)/shard_map/all_to_all | solution.py:56
  533.1 65.1 %all-to-all-start.1 = ((bf16[4,640,1024]{2,0,1:T(4,128)(2,1)}), bf16[4,640,1024]{2,0,1:T(4,128)(2,1)}, u32[]{:S(2)}, u32[]{:S(2)}) async-start(bf16[4,640,1024]{2,0,1:T(4,128)(2,1)} %copy.194), calls=%async_computation.2 | async-start | bytes 10485760 | tf_op jit(solution)/shard_map/all_to_all | solution.py:56
  537.8 137.7 %all-gather.11.cloned.1.call-start = ((), (), s32[]{:S(2)}) async-start(), calls=%async_computation.16 | async-start | bytes 2621440 | tf_op jit(solution)/shard_map/all_gather | solution.py:44
  632.7 178.8 %reduce-scatter.19.cloned.1.call-start = ((), (), s32[]{:S(2)}) async-start(), calls=%async_computation.21 | async-start | bytes 540672 | tf_op jit(solution)/shard_map/reduce_scatter | solution.py:295
  634.0 253.2 %reduce-scatter.23.cloned.1.call-start = ((), (), s32[]{:S(2)}) async-start(), calls=%async_computation.23 | async-start | bytes 5242880 | tf_op jit(solution)/shard_map/reduce_scatter | solution.py:306
  643.3 285.1 %reduce-scatter.13.cloned.1.call-start = ((), (), s32[]{:S(2)}) async-start(), calls=%async_computation.18 | async-start | bytes 1179648 | tf_op jit(solution)/shard_map/reduce_scatter | solution.py:298
  695.1 273.5 %reduce-scatter.15.cloned.1.call-start = ((), (), s32[]{:S(2)}) async-start(), calls=%async_computation.19 | async-start | bytes 1179648 | tf_op jit(solution)/shard_map/reduce_scatter | solution.py:299
  708.3 300.2 %reduce-scatter.17.cloned.1.call-start = ((), (), s32[]{:S(2)}) async-start(), calls=%async_computation.20 | async-start | bytes 1179648 | tf_op jit(solution)/shard_map/reduce_scatter | solution.py:300
  711.8 376.6 %reduce-scatter.11.cloned.1.call-start = ((), (), s32[]{:S(2)}) async-start(), calls=%async_computation.17 | async-start | bytes 5242880 | tf_op jit(solution)/shard_map/reduce_scatter | solution.py:48
  715.5 521.1 %reduce-scatter.21.cloned.1.call-start = ((), (), s32[]{:S(2)}) async-start(), calls=%async_computation.22 | async-start | bytes 10485760 | tf_op jit(solution)/shard_map/reduce_scatter | solution.py:303
  812.9 275.5 %copy-start.4 = (f32[256,1024]{1,0:T(8,128)S(1)}, f32[256,1024]{1,0:T(8,128)}, u32[]{:S(2)}) copy-start(f32[256,1024]{1,0:T(8,128)} %param.27) | copy-start | bytes 3145732
  812.9 275.5 %copy-start.42 = (f32[1024]{0:T(1024)S(1)}, f32[1024]{0:T(1024)}, u32[]{:S(2)}) copy-start(f32[1024]{0:T(1024)} %copy-done.41) | copy-start | bytes 12292
  812.9 275.5 %copy-start.47 = (f32[256]{0:T(256)S(1)}, f32[256]{0:T(256)}, u32[]{:S(2)}) copy-start(f32[256]{0:T(256)} %copy-done.46) | copy-start | bytes 3076
  893.8 239.5 %copy-start.57 = (f32[32]{0:T(128)S(1)}, f32[32]{0:T(128)}, u32[]{:S(2)}) copy-start(f32[32]{0:T(128)} %param.30) | copy-start | bytes 388
  893.8 239.5 %copy-start.58 = (f32[32]{0:T(128)S(1)}, f32[32]{0:T(128)}, u32[]{:S(2)}) copy-start(f32[32]{0:T(128)} %param.34) | copy-start | bytes 388
  893.8 239.5 %copy-start.59 = (f32[32]{0:T(128)S(1)}, f32[32]{0:T(128)}, u32[]{:S(2)}) copy-start(f32[32]{0:T(128)} %param.46) | copy-start | bytes 388
  893.8 240.2 %copy-start.16 = (f32[256,1024]{1,0:T(8,128)S(1)}, f32[256,1024]{1,0:T(8,128)}, u32[]{:S(2)}) copy-start(f32[256,1024]{1,0:T(8,128)} %get-tuple-element.73) | copy-start | bytes 3145732
  893.8 240.2 %copy-start.56 = (f32[256]{0:T(256)S(1)}, f32[256]{0:T(256)}, u32[]{:S(2)}) copy-start(f32[256]{0:T(256)} %get-tuple-element.90) | copy-start | bytes 3076
  (59 other events, 2552.8 us)
Sparse Core Ops, SparseCore 0:
  55.3 45.7 all-gather.4
  124.9 75.4 reduce-scatter.8
  202.7 155.2 all-gather.6
  360.1 79.2 all-gather.8
  632.8 42.6 all-gather.10
  678.3 133.1 reduce-scatter.18
  814.4 72.7 reduce-scatter.22
  891.9 36.5 reduce-scatter.12
  932.5 36.0 reduce-scatter.14
  972.5 36.0 reduce-scatter.16
  1011.6 76.7 reduce-scatter.10
  1090.6 145.9 reduce-scatter.20
where the time goes:
time: 1260 us; the launch traced here: 1250 us
  waiting for transfers between devices  724 us (57%)
  blocking collectives  199 us (16%)
  matrix products  108 us (9%)
  local copies, waits for them, and re-layouts  103 us (8%)
  other arithmetic  84.4 us (7%)
  starting transfers between devices  20.4 us (2%)
  between operations  15.5 us (1%)
    reduce_scatter x2, waiting for transfers between devices, rows_sum(): return lax.psum_scatter(value, 'mp', scatter_dimension=0, tiled=True)  139 us
    reduce_scatter x1, waiting for transfers between devices, local(): lax.psum_scatter(grad_gateup.astype(jnp.bfloat16), 'mp', scatter_dimensio...  100 us
    unnamed x2, blocking collectives  85.5 us
    all_gather x1, blocking collectives, local(): lax.all_gather(router_w, ('dp', 'mp'), axis=0, tiled=True)  82.8 us
    reduce_scatter x1, waiting for transfers between devices, local(): lax.psum_scatter(grad_router, ('dp', 'mp'), scatter_dimension=0, tiled=True)  82.4 us
    all_to_all x2, waiting for transfers between devices, from_owner(): return lax.all_to_all(buffer, 'dp', split_axis=1, concat_axis=0, tiled=True)  80 us
    reduce_scatter x1, waiting for transfers between devices, local(): lax.psum_scatter(grad_down.astype(jnp.bfloat16), 'mp', scatter_dimension=...  74.3 us
    all_to_all x2, waiting for transfers between devices, to_owner(): return lax.all_to_all(buffer, 'dp', split_axis=0, concat_axis=1, tiled=True)  54.7 us
  transfers between devices with their start and end apart: 16, of which 14 were waited for; matrix products, arithmetic and copies ran while one was open for 15% of the time, Pallas kernels for 0%

commit v1 on v0

v1 whole, which is shorter than its diff:
```python
import functools
import math

import jax
import jax.numpy as jnp
from jax import lax
from jax.experimental import pallas as pl
from jax.experimental.pallas import tpu as pltpu
from jax.sharding import PartitionSpec as P

MODEL_WIDTH = 1024
QUERY_HEADS = 16
KEY_VALUE_HEADS = 8
HEAD_SIZE = 64
EXPERTS = 32
TOPK = 8
SEQUENCE_TOKENS = 512
STEP = 3
CAP = 80

NORM_EPS = 1e-06
MESH = pl.DeviceIdType.MESH
BF16 = jnp.bfloat16
F32 = jnp.float32


def flip(index, mask):
    return index + mask * (1 - 2 * lax.rem(lax.div(index, mask), 2))


def flip_all(index, masks):
    bit = 1
    while bit <= masks:
        if masks & bit:
            index = flip(index, bit)
        bit *= 2
    return index


def bits_of(size):
    return [1 << i for i in range(size.bit_length() - 1)]


def orders_of(n_dp):
    bits = bits_of(n_dp)
    return bits[1:] + bits[:1], bits[1:][::-1] + bits[:1]


def place_of(order, j):
    place = -1
    for at, mask in enumerate(order):
        if j & mask:
            place = at
    return place


def greet(partners):
    barrier = pltpu.get_barrier_semaphore()
    for partner in partners:
        pl.semaphore_signal(barrier, inc=1, device_id=partner, device_id_type=MESH)
    pl.semaphore_wait(barrier, len(partners))


class Copies:
    def __init__(self, send_sems, recv_sems):
        self.send_sems, self.recv_sems = send_sems, recv_sems
        self.used = 0
        self.sent = []

    def slot(self):
        self.used += 1
        return self.used - 1

    def make(self, source, target, device, slot):
        return pltpu.make_async_remote_copy(
            src_ref=source,
            dst_ref=target,
            send_sem=self.send_sems.at[slot],
            recv_sem=self.recv_sems.at[slot],
            device_id=device,
            device_id_type=MESH,
        )

    def start(self, source, target, device, slot):
        copy = self.make(source, target, device, slot)
        copy.start()
        self.sent.append(copy)

    def wait(self, target, device, slot):
        self.make(target, target, device, slot).wait_recv()

    def finish(self):
        for copy in self.sent:
            copy.wait_send()


class TreeGather:
    def __init__(self, copies, order, n_dp, me, source, target):
        self.copies, self.order, self.n_dp, self.me = copies, order, n_dp, me
        self.source, self.target = source, target
        self.slots = {j: copies.slot() for j in range(1, n_dp)}

    def level(self, j):
        return bin(j).count("1")

    def send(self, j):
        dp, mp = self.me
        for mask in self.order[place_of(self.order, j) + 1 :]:
            self.copies.start(
                self.source(j), self.target(j, mask), (flip(dp, mask), mp), self.slots[j ^ mask]
            )

    def receive(self, j):
        self.copies.wait(self.source(j), self.me, self.slots[j])

    def steps(self):
        return sorted(range(1, self.n_dp), key=lambda j: (self.level(j), place_of(self.order, j)))


def run_gathers(trees):
    n_dp = trees[0].n_dp
    for level in range(1, n_dp.bit_length()):
        for tree in trees:
            for j in tree.steps():
                if tree.level(j) == level:
                    tree.receive(j)
                    tree.send(j)


class TreeReduce:
    def __init__(self, copies, order, n_dp, me, block, room, add):
        self.copies, self.order, self.n_dp, self.me = copies, order, n_dp, me
        self.block, self.room, self.add = block, room, add
        self.keys = [
            (j, q) for j in range(n_dp) for q in range(len(order) - 1, place_of(order, j), -1)
        ]
        self.slots = {key: copies.slot() for key in self.keys}

    def number(self, key):
        return self.keys.index(key)

    def send(self, j):
        dp, mp = self.me
        p = place_of(self.order, j)
        last = len(self.order) - 1
        source = self.block(j) if p == last else self.room(self.number((j, last)))
        mask = self.order[p]
        key = (j ^ mask, p)
        self.copies.start(source, self.room(self.number(key)), (flip(dp, mask), mp), self.slots[key])

    def collect(self, j):
        last = len(self.order) - 1
        for q in range(last, place_of(self.order, j), -1):
            here = self.room(self.number((j, q)))
            self.copies.wait(here, self.me, self.slots[(j, q)])
            if q == last:
                self.add(here, self.block(j))
            else:
                self.add(self.room(self.number((j, last))), here)

    def total(self):
        return self.room(self.number((0, len(self.order) - 1)))


def run_reduces(trees):
    n_dp = trees[0].n_dp
    last = len(trees[0].order) - 1
    for tree in trees:
        for j in range(1, n_dp):
            if place_of(tree.order, j) == last:
                tree.send(j)
    for p in range(last - 1, -1, -1):
        for tree in trees:
            for j in range(1, n_dp):
                if place_of(tree.order, j) == p:
                    tree.collect(j)
                    tree.send(j)
    for tree in trees:
        tree.collect(0)


def add_rows(step=16):
    def add(here, other):
        def body(i, carry):
            rows = pl.ds(pl.multiple_of(i * step, step), step)
            total = here[..., rows, :].astype(F32) + other[..., rows, :].astype(F32)
            here[..., rows, :] = total.astype(here.dtype)
            return carry

        lax.fori_loop(0, here.shape[-2] // step, body, 0)

    return add


def hbm():
    return pl.BlockSpec(memory_space=pl.ANY)


def vmem():
    return pl.BlockSpec(memory_space=pltpu.VMEM)


def params(identity, limit=None):
    return pltpu.CompilerParams(
        collective_id=identity, has_side_effects=True, vmem_limit_bytes=limit
    )


def gather_weights(n_dp, n_mp, small, shards):
    half = n_mp // 2
    kinds, rows, cols = shards.shape
    order_a, order_b = orders_of(n_dp)
    n_copies = 2 * (n_mp - 1) + 6 * (n_dp - 1)

    def kernel(small_ref, shard_ref, small_all, full, send_sems, recv_sems, local_sems):
        dp, mp = lax.axis_index("dp"), lax.axis_index("mp")
        me = (dp, mp)
        copies = Copies(send_sems, recv_sems)
        own_small = small_all.at[dp, mp]
        column = pl.multiple_of(mp * cols, cols)
        own_rows = pl.ds(pl.multiple_of(dp * rows, rows), rows)
        own_full = full.at[:, own_rows, pl.ds(column, cols)]
        keep = [
            pltpu.make_async_copy(small_ref, own_small, local_sems.at[0]),
            pltpu.make_async_copy(shard_ref, own_full, local_sems.at[1]),
        ]
        for copy in keep:
            copy.start()
        greet(
            [(flip_all(dp, mask), mp) for mask in bits_of(n_dp)]
            + [(dp, flip_all(mp, k)) for k in range(1, n_mp)]
        )
        near = lax.div(mp, half)
        line = {}
        for k in range(1, n_mp):
            device = (dp, flip_all(mp, k))
            line[k] = (copies.slot(), copies.slot())
            copies.start(small_ref, own_small, device, line[k][0])
            copies.start(shard_ref, own_full, device, line[k][1])

        def small_tree(chunk):
            first = pl.multiple_of(chunk * half, half)

            def ref(j, mask=0):
                return small_all.at[flip_all(dp, j), pl.ds(first, half)]

            return TreeGather(copies, order_a, n_dp, me, ref, ref)

        def tree(chunk, part, order):
            first = pl.multiple_of(chunk * half * cols, half * cols)
            part_rows = rows // 2

            def ref(j, mask=0):
                start = flip_all(dp, j) * rows + part * part_rows
                return full.at[
                    :,
                    pl.ds(pl.multiple_of(start, part_rows), part_rows),
                    pl.ds(first, half * cols),
                ]

            return TreeGather(copies, order, n_dp, me, ref, ref)

        groups = []
        for chunk in (near, 1 - near):
            groups.append(
                [small_tree(chunk), tree(chunk, 0, order_a), tree(chunk, 1, order_b)]
            )
        for copy in keep:
            copy.wait()
        for number, group in enumerate(groups):
            for k in range(1, n_mp) if number else range(1, half):
                if number == 0 or k >= half:
                    other = flip_all(mp, k)
                    copies.wait(small_all.at[dp, other], me, line[k][0])
                    theirs = pl.ds(pl.multiple_of(other * cols, cols), cols)
                    copies.wait(full.at[:, own_rows, theirs], me, line[k][1])
            for one in group:
                one.send(0)
        for level in range(1, n_dp.bit_length()):
            for group in groups:
                for one in group:
                    for j in one.steps():
                        if one.level(j) == level:
                            one.receive(j)
                            one.send(j)
        copies.finish()

    return pl.pallas_call(
        kernel,
        out_shape=(
            jax.ShapeDtypeStruct((n_dp, n_mp) + small.shape, small.dtype),
            jax.ShapeDtypeStruct((kinds, n_dp * rows, n_mp * cols), shards.dtype),
        ),
        in_specs=[hbm(), hbm()],
        out_specs=(hbm(), hbm()),
        scratch_shapes=[
            pltpu.SemaphoreType.DMA((n_copies,)),
            pltpu.SemaphoreType.DMA((n_copies,)),
            pltpu.SemaphoreType.DMA((2,)),
        ],
        compiler_params=params(0),
        name="gather_weights",
    )(small, shards)


def gather_tokens(n_dp, n_mp, identity, rows, table):
    half = n_mp // 2
    tokens = rows.shape[0]
    order_a, order_b = orders_of(n_dp)
    n_copies = 2 + 6 * (n_dp - 1)

    def kernel(rows_ref, table_ref, rows_all, table_all, send_sems, recv_sems, local_sems):
        dp, mp = lax.axis_index("dp"), lax.axis_index("mp")
        me = (dp, mp)
        partner = (dp, flip_all(mp, half))
        copies = Copies(send_sems, recv_sems)
        keep = [
            pltpu.make_async_copy(rows_ref, rows_all.at[0, 0], local_sems.at[0]),
            pltpu.make_async_copy(table_ref, table_all.at[0, 0], local_sems.at[1]),
        ]
        for copy in keep:
            copy.start()
        greet([(flip_all(dp, mask), mp) for mask in bits_of(n_dp)] + [partner])
        across = (copies.slot(), copies.slot())
        copies.start(rows_ref, rows_all.at[1, 0], partner, across[0])
        copies.start(table_ref, table_all.at[1, 0], partner, across[1])

        def row_tree(group, part, order):
            cut = pl.ds(part * (tokens // 2), tokens // 2)
            return TreeGather(
                copies,
                order,
                n_dp,
                me,
                lambda j: rows_all.at[group, j, cut],
                lambda j, mask: rows_all.at[group, j ^ mask, cut],
            )

        def table_tree(group, order):
            return TreeGather(
                copies,
                order,
                n_dp,
                me,
                lambda j: table_all.at[group, j],
                lambda j, mask: table_all.at[group, j ^ mask],
            )

        groups = [
            [row_tree(group, 0, order_a), row_tree(group, 1, order_b), table_tree(group, order_a)]
            for group in range(2)
        ]
        for copy in keep:
            copy.wait()
        for one in groups[0]:
            one.send(0)
        run_gathers(groups[0])
        copies.wait(rows_all.at[1, 0], me, across[0])
        copies.wait(table_all.at[1, 0], me, across[1])
        for one in groups[1]:
            one.send(0)
        run_gathers(groups[1])
        copies.finish()

    return pl.pallas_call(
        kernel,
        out_shape=(
            jax.ShapeDtypeStruct((2, n_dp) + rows.shape, rows.dtype),
            jax.ShapeDtypeStruct((2, n_dp) + table.shape, table.dtype),
        ),
        in_specs=[hbm(), hbm()],
        out_specs=(hbm(), hbm()),
        scratch_shapes=[
            pltpu.SemaphoreType.DMA((n_copies,)),
            pltpu.SemaphoreType.DMA((n_copies,)),
            pltpu.SemaphoreType.DMA((2,)),
        ],
        compiler_params=params(identity),
        name="gather_tokens",
    )(rows, table)


def reduce_tokens(n_dp, n_mp, identity, terms, table=None):
    half = n_mp // 2
    tokens, width = terms.shape[2:]
    order_a, order_b = orders_of(n_dp)
    n_copies = 4 * (n_dp - 1) + 1 + (2 * n_dp - 1 if table is not None else 0)

    def kernel(*refs):
        if table is not None:
            terms_ref, table_ref, out_ref, parts_ref, *refs = refs
        else:
            terms_ref, out_ref, *refs = refs
        rooms, across, send_sems, recv_sems, local_sems = refs
        dp, mp = lax.axis_index("dp"), lax.axis_index("mp")
        me = (dp, mp)
        other = flip_all(mp, half)
        partner = (dp, other)
        copies = Copies(send_sems, recv_sems)
        if table is not None:
            greet(
                [
                    (flip_all(dp, j), other if group else mp)
                    for group in range(2)
                    for j in range(n_dp)
                    if group + j
                ]
            )
        else:
            greet([(flip_all(dp, mask), mp) for mask in bits_of(n_dp)] + [partner])
        kind = lax.div(mp, half)
        parts = {}
        if table is not None:
            keep = pltpu.make_async_copy(
                table_ref.at[0, 0], parts_ref.at[dp, kind], local_sems.at[0]
            )
            keep.start()
            for group in range(2):
                for j in range(n_dp):
                    if group + j:
                        device = (flip_all(dp, j), other if group else mp)
                        parts[group, j] = copies.slot()
                        copies.start(
                            table_ref.at[group, j], parts_ref.at[dp, kind], device, parts[group, j]
                        )

        def tree(group, part, order):
            cut = pl.ds(part * (tokens // 2), tokens // 2)
            return TreeReduce(
                copies,
                order,
                n_dp,
                me,
                lambda j: terms_ref.at[group, j, cut],
                lambda number: rooms.at[group, part, number],
                add_rows(),
            )

        groups = [[tree(group, 0, order_a), tree(group, 1, order_b)] for group in (1, 0)]
        run_reduces(groups[0] + groups[1])
        last = copies.slot()
        mine = [rooms.at[1, part, groups[0][part].number((0, len(order_a) - 1))] for part in (0, 1)]
        own = [rooms.at[0, part, groups[1][part].number((0, len(order_a) - 1))] for part in (0, 1)]
        for part in (0, 1):
            out_ref[pl.ds(part * (tokens // 2), tokens // 2), :] = mine[part][...].astype(F32)
        for part in (0, 1):
            across[0, pl.ds(part * (tokens // 2), tokens // 2), :] = mine[part][...]
        copies.start(across.at[0], across.at[1], partner, last)
        copies.wait(across.at[1], me, last)
        for part in (0, 1):
            cut = pl.ds(part * (tokens // 2), tokens // 2)
            out_ref[cut, :] = own[part][...].astype(F32) + across[1, cut, :].astype(F32)
        if table is not None:
            keep.wait()
            for group in range(2):
                for j in range(n_dp):
                    if group + j:
                        theirs = 1 - kind if group else kind
                        copies.wait(
                            parts_ref.at[flip_all(dp, j), theirs], me, parts[group, j]
                        )
        copies.finish()

    out_shape = [jax.ShapeDtypeStruct((tokens, width), F32)]
    if table is not None:
        out_shape.append(jax.ShapeDtypeStruct((n_dp, 2) + table.shape[2:], table.dtype))
    return pl.pallas_call(
        kernel,
        out_shape=tuple(out_shape),
        in_specs=[vmem()] * (2 if table is not None else 1),
        out_specs=tuple([vmem()] * len(out_shape)),
        scratch_shapes=[
            pltpu.VMEM((2, 2, n_dp - 1, tokens // 2, width), terms.dtype),
            pltpu.VMEM((2, tokens, width), terms.dtype),
            pltpu.SemaphoreType.DMA((n_copies,)),
            pltpu.SemaphoreType.DMA((n_copies,)),
            pltpu.SemaphoreType.DMA((1,)),
        ],
        compiler_params=params(identity, 48 << 20),
        name="reduce_tokens",
    )(*([terms, table] if table is not None else [terms]))


def reduce_weights(n_dp, n_mp, identity, grads, small):
    kinds, rows_all, cols_all = grads.shape
    rows, cols = rows_all // n_dp, cols_all // n_mp
    order_a, order_b = orders_of(n_dp)
    n_copies = 3 * (n_dp - 1) + 2 * (n_mp - 1)
    part_rows = rows // 2

    def kernel(grads_ref, small_ref, out_ref, small_out, rooms, small_rooms, line, small_line, send_sems, recv_sems):
        dp, mp = lax.axis_index("dp"), lax.axis_index("mp")
        me = (dp, mp)
        copies = Copies(send_sems, recv_sems)
        greet(
            [(flip_all(dp, mask), mp) for mask in bits_of(n_dp)]
            + [(dp, flip_all(mp, k)) for k in range(1, n_mp)]
        )

        def tree(part, order):
            def block(j):
                start = flip_all(dp, j) * rows + part * part_rows
                return grads_ref.at[:, pl.ds(pl.multiple_of(start, part_rows), part_rows), :]

            return TreeReduce(
                copies, order, n_dp, me, block, lambda number: rooms.at[part, number], add_rows()
            )

        def add_whole(here, other):
            here[...] = here[...] + other[...]

        trees = [
            TreeReduce(
                copies,
                order_a,
                n_dp,
                me,
                lambda j: small_ref.at[flip_all(dp, j)],
                lambda number: small_rooms.at[number],
                add_whole,
            ),
            tree(0, order_a),
            tree(1, order_b),
        ]
        run_reduces(trees)
        slots = {k: (copies.slot(), copies.slot()) for k in range(1, n_mp)}
        totals = [one.total() for one in trees]

        def columns(who):
            return pl.ds(pl.multiple_of(who * cols, cols), cols)

        for part in (0, 1):
            for k in range(n_mp):
                line[0, k, :, pl.ds(part * part_rows, part_rows), :] = totals[1 + part][
                    :, :, columns(flip_all(mp, k))
                ]
        for k in range(1, n_mp):
            device = (dp, flip_all(mp, k))
            copies.start(totals[0].at[device[1]], small_line.at[k], device, slots[k][0])
            copies.start(line.at[0, k], line.at[1, k], device, slots[k][1])
        small_out[...] = totals[0][mp]
        out_ref[...] = line[0, 0].astype(F32)
        for k in range(1, n_mp):
            copies.wait(small_line.at[k], me, slots[k][0])
            small_out[...] += small_line[k]
            copies.wait(line.at[1, k], me, slots[k][1])
            out_ref[...] += line[1, k].astype(F32)
        copies.finish()

    return pl.pallas_call(
        kernel,
        out_shape=(
            jax.ShapeDtypeStruct((kinds, rows, cols), F32),
            jax.ShapeDtypeStruct(small.shape[2:], F32),
        ),
        in_specs=[vmem(), vmem()],
        out_specs=(vmem(), vmem()),
        scratch_shapes=[
            pltpu.VMEM((2, n_dp - 1, kinds, part_rows, cols_all), grads.dtype),
            pltpu.VMEM((n_dp - 1,) + small.shape[1:], small.dtype),
            pltpu.VMEM((2, n_mp, kinds, rows, cols), grads.dtype),
            pltpu.VMEM((n_mp,) + small.shape[2:], small.dtype),
            pltpu.SemaphoreType.DMA((n_copies,)),
            pltpu.SemaphoreType.DMA((n_copies,)),
        ],
        compiler_params=params(identity, 48 << 20),
        name="reduce_weights",
    )(grads, small)


def rotary_tables(positions):
    half_width = HEAD_SIZE // 2
    frequency = jnp.exp(
        -math.log(10000.0) * jnp.arange(half_width, dtype=F32) * 2.0 / HEAD_SIZE
    )
    angles = positions.astype(F32)[:, None] * frequency[None, :]
    return jnp.cos(angles)[:, None, :], jnp.sin(angles)[:, None, :]


def rotate(value, cosine, sine):
    half_width = value.shape[-1] // 2
    front = value[..., :half_width]
    rear = value[..., half_width:]
    return jnp.concatenate([front * cosine - rear * sine, rear * cosine + front * sine], -1)


def adamw(weight, gradient, moment_one, moment_two, rate_val, decay_val):
    first_new = 0.9 * moment_one + 0.1 * gradient
    second_new = 0.95 * moment_two + 0.05 * gradient * gradient
    first_hat = first_new / (1.0 - 0.9**STEP)
    second_hat = second_new / (1.0 - 0.95**STEP)
    weight_new = weight - rate_val * (
        first_hat / (jnp.sqrt(second_hat) + 1e-08) + decay_val * weight
    )
    return (gradient, weight_new, first_new, second_new)


def local(
    n_dp,
    n_mp,
    residual_in,
    cotangent,
    expert_ids,
    attn_gain,
    query_w,
    key_value_weight,
    output_w,
    moe_gain,
    router_w,
    gateup_w,
    down_w,
    attn_gain_mean,
    attn_gain_var,
    query_mean,
    query_var,
    key_value_first_moment,
    key_value_second_moment,
    output_mean,
    output_var,
    moe_gain_mean,
    moe_gain_var,
    router_mean,
    router_var,
    gateup_mean,
    gateup_var,
    down_mean,
    down_var,
):
    dp, mp = lax.axis_index("dp"), lax.axis_index("mp")
    half = n_mp // 2
    kind = mp // half
    tokens = residual_in.shape[0]
    owned = gateup_w.shape[0]
    shared = owned // 2
    hidden_units = down_w.shape[1]
    flips = [[(i, i ^ k) for i in range(n_mp)] for k in range(n_mp)]

    packed = jnp.concatenate([gateup_w, down_w[:, None]], 1).astype(BF16)
    mine = jnp.where(kind == 0, packed[:shared], packed[shared:])
    theirs = jnp.where(kind == 0, packed[shared:], packed[:shared])
    expert_parts = [mine] + [
        lax.ppermute(mine if k < half else theirs, "mp", flips[k]) for k in range(1, n_mp)
    ]

    expert_range = jnp.arange(EXPERTS, dtype=jnp.int32)
    onehot = (expert_ids[:, :, None] == expert_range[None, None, :]).astype(jnp.int32)
    onehot_float = onehot.astype(F32)
    chosen = jnp.sum(onehot, 1)
    before = jnp.cumsum(chosen, 0) - chosen
    place = jnp.where(chosen > 0, before, -1).T

    own_gain, own_router = attn_gain.shape[0], router_w.shape[0]
    lanes = 128
    small = jnp.zeros((8 + own_router, lanes), F32)
    small = small.at[0, :own_gain].set(attn_gain).at[1, :own_gain].set(moe_gain)
    small = small.at[8:, :EXPERTS].set(router_w)
    shards = jnp.stack([query_w, key_value_weight, output_w.T]).astype(BF16)
    small_all, projections = gather_weights(n_dp, n_mp, small, shards)
    gain_one = small_all[:, :, 0, :own_gain].reshape(-1)
    gain_two = small_all[:, :, 1, :own_gain].reshape(-1)
    router_low = small_all[:, :, 8:, :EXPERTS].reshape(MODEL_WIDTH, EXPERTS).astype(BF16)
    query_full, keyval_full, output_turned = projections[0], projections[1], projections[2]
    cot_low = cotangent.astype(BF16)
    cot_all, place_all = gather_tokens(n_dp, n_mp, 1, cot_low, place)

    inv_one = lax.rsqrt(jnp.mean(residual_in * residual_in, -1, keepdims=True) + NORM_EPS)
    normed_one = (residual_in * inv_one * gain_one).astype(BF16)
    normed_other = lax.ppermute(normed_one, "mp", flips[1])
    per_sequence = SEQUENCE_TOKENS // tokens
    own_positions = (mp % per_sequence) * tokens + jnp.arange(tokens, dtype=jnp.int32)
    other_positions = (flip(mp, 1) % per_sequence) * tokens + jnp.arange(tokens, dtype=jnp.int32)
    key_positions = jnp.concatenate([other_positions, own_positions])
    queries_per_group = QUERY_HEADS // KEY_VALUE_HEADS
    score_scale = 1.0 / math.sqrt(HEAD_SIZE)
    causal = own_positions[:, None] >= key_positions[None, :]
    query_cos, query_sin = rotary_tables(own_positions)
    key_cos, key_sin = rotary_tables(key_positions)
    query_linear = jnp.dot(normed_one, query_full, preferred_element_type=F32)
    keyval_linear = jnp.dot(
        jnp.concatenate([normed_other, normed_one]), keyval_full, preferred_element_type=F32
    ).reshape(2 * tokens, KEY_VALUE_HEADS, 2, HEAD_SIZE)
    query_rows = (
        rotate(query_linear.reshape(tokens, QUERY_HEADS, HEAD_SIZE), query_cos, query_sin)
        .astype(BF16)
        .reshape(tokens, KEY_VALUE_HEADS, queries_per_group, HEAD_SIZE)
    )
    keys_rot = rotate(keyval_linear[:, :, 0], key_cos, key_sin).astype(BF16)
    values = keyval_linear[:, :, 1].astype(BF16)
    raw_scores = (
        jnp.einsum("qkgd,skd->kgqs", query_rows, keys_rot, preferred_element_type=F32) * score_scale
    )
    exp_scores = jnp.where(causal, jnp.exp(jnp.where(causal, raw_scores, 0.0)), 0.0)
    row_total = jnp.sum(exp_scores, -1, keepdims=True)
    log_total = jnp.log(row_total)
    attn_probs = (exp_scores / row_total).astype(BF16)
    context = (
        jnp.einsum("kgqs,skd->qkgd", attn_probs, values, preferred_element_type=F32)
        .astype(BF16)
        .reshape(tokens, -1)
    )
    attn_out = jnp.einsum("tc,dc->td", context, output_turned, preferred_element_type=F32)
    hidden = residual_in + attn_out
    inv_two = lax.rsqrt(jnp.mean(hidden * hidden, -1, keepdims=True) + NORM_EPS)
    normed_two = (hidden * inv_two * gain_two).astype(BF16)
    logits = jnp.dot(normed_two, router_low, preferred_element_type=F32)
    exp_logits = jnp.exp(logits)
    router_probs = exp_logits / jnp.sum(exp_logits, -1, keepdims=True)

    token_all, probs_all = gather_tokens(n_dp, n_mp, 2, normed_two, router_probs.T)
    blocks = 2 * n_dp
    first_expert = dp * owned + kind * shared
    token_all = token_all.reshape(blocks, tokens, MODEL_WIDTH)
    cot_all = cot_all.reshape(blocks, tokens, MODEL_WIDTH)
    own_place = lax.dynamic_slice_in_dim(
        place_all.reshape(blocks, EXPERTS, tokens), first_expert, shared, 1
    )
    own_probs = lax.dynamic_slice_in_dim(
        probs_all.reshape(blocks, EXPERTS, tokens), first_expert, shared, 1
    )
    hit = own_place[:, :, None, :] == jnp.arange(CAP, dtype=jnp.int32)[None, None, :, None]
    pick = hit.astype(BF16)
    weight = jnp.sum(jnp.where(hit, own_probs[:, :, None, :], 0.0), -1)
    weight = weight.transpose(1, 0, 2).reshape(shared, blocks * CAP, 1)

    def slots_of(rows):
        found = jnp.einsum("best,btd->ebsd", pick, rows, preferred_element_type=F32)
        return found.astype(BF16).reshape(shared, blocks * CAP, MODEL_WIDTH)

    def sums_of(slots):
        per_block = slots.reshape(shared, blocks, CAP, MODEL_WIDTH)
        found = jnp.einsum("best,ebsd->btd", pick, per_block, preferred_element_type=F32)
        return found.astype(BF16).reshape(2, n_dp, tokens, MODEL_WIDTH)

    received = slots_of(token_all)
    cot_slots = slots_of(cot_all)
    experts = jnp.stack(expert_parts, 2)
    gateup_full = experts[:, :2].reshape(shared, 2, n_mp * hidden_units, MODEL_WIDTH)
    down_full = experts[:, 2].reshape(shared, n_mp * hidden_units, MODEL_WIDTH)
    gate_up = jnp.einsum("erd,ecfd->ercf", received, gateup_full, preferred_element_type=F32)
    gate_val, up_val = gate_up[:, :, 0], gate_up[:, :, 1]
    sigmoid_val = jax.nn.sigmoid(gate_val)
    silu_val = gate_val * sigmoid_val
    activation = (silu_val * up_val).astype(BF16)
    expert_out = jnp.einsum("erf,efd->erd", activation, down_full, preferred_element_type=F32)
    gate_dot_slots = jnp.sum(cot_slots.astype(F32) * expert_out, -1)
    gate_dot_slots = gate_dot_slots.reshape(shared, blocks, CAP).transpose(1, 0, 2)
    gate_dots = jnp.sum(jnp.where(hit, gate_dot_slots[..., None], 0.0), 2)
    gate_dots = jnp.pad(gate_dots, ((0, 0), (0, 8 - shared), (0, 0)))
    gate_dots = gate_dots.reshape(2, n_dp, 8, tokens)
    mixture_terms = sums_of((weight * expert_out).astype(BF16))
    mixture, gate_parts = reduce_tokens(n_dp, n_mp, 3, mixture_terms, gate_dots)
    block_out = hidden + mixture
    grad_probs = gate_parts[:, :, :shared].reshape(EXPERTS, tokens).T
    grad_rows = (weight * cot_slots.astype(F32)).astype(BF16)
    grad_act = jnp.einsum("erd,efd->erf", grad_rows, down_full, preferred_element_type=F32)
    grad_down = jnp.einsum("erf,erd->efd", activation, grad_rows, preferred_element_type=F32)
    grad_gate = grad_act * up_val * sigmoid_val * (1.0 + gate_val * (1.0 - sigmoid_val))
    grad_up = grad_act * silu_val
    grad_pair = jnp.stack([grad_gate, grad_up], 2).astype(BF16)
    grad_slots = jnp.einsum(
        "ercf,ecfd->erd", grad_pair, gateup_full, preferred_element_type=F32
    ).astype(BF16)
    grad_gateup = jnp.einsum("ercf,erd->ecfd", grad_pair, received, preferred_element_type=F32)
    (grad_normed_two,) = reduce_tokens(n_dp, n_mp, 4, sums_of(grad_slots))

    grad_experts = jnp.concatenate(
        [
            grad_gateup.reshape(shared, 2, n_mp, hidden_units, MODEL_WIDTH),
            grad_down.reshape(shared, 1, n_mp, hidden_units, MODEL_WIDTH),
        ],
        1,
    ).astype(BF16)
    arrived = [grad_experts[:, :, 0]] + [
        lax.ppermute(grad_experts[:, :, k], "mp", flips[k]) for k in range(1, n_mp)
    ]
    near_sum = sum(part.astype(F32) for part in arrived[:half])
    far_sum = sum(part.astype(F32) for part in arrived[half:])
    expert_grad = jnp.where(
        kind == 0,
        jnp.concatenate([near_sum, far_sum], 0),
        jnp.concatenate([far_sum, near_sum], 0),
    )
    gateup_grad, down_grad = expert_grad[:, :2], expert_grad[:, 2]

    grad_probs = jnp.where(chosen > 0, grad_probs, 0.0)
    grad_logits = (
        router_probs * (grad_probs - jnp.sum(router_probs * grad_probs, -1, keepdims=True))
    ).astype(BF16)
    grad_normed_two = grad_normed_two + jnp.einsum(
        "te,de->td", grad_logits, router_low, preferred_element_type=F32
    )
    grad_router = jnp.einsum("td,te->de", normed_two, grad_logits, preferred_element_type=F32)
    scaled_two = gain_two * grad_normed_two
    grad_hidden = (
        cotangent
        + inv_two * scaled_two
        - hidden * inv_two**3 * jnp.mean(scaled_two * hidden, -1, keepdims=True)
    )
    grad_gain_two = jnp.sum(grad_normed_two * hidden * inv_two, 0)

    grad_attn = grad_hidden.astype(BF16)
    grad_ctx = jnp.dot(grad_attn, output_turned, preferred_element_type=F32).astype(BF16)
    grad_output = jnp.einsum("td,tc->dc", grad_attn, context, preferred_element_type=F32)
    grad_ctx = grad_ctx.reshape(tokens, KEY_VALUE_HEADS, queries_per_group, HEAD_SIZE)
    probs_float = jnp.where(causal, jnp.exp(jnp.where(causal, raw_scores - log_total, 0.0)), 0.0)
    grad_p = jnp.einsum("qkgd,skd->kgqs", grad_ctx, values, preferred_element_type=F32)
    delta_sum = jnp.sum(probs_float * grad_p, -1, keepdims=True)
    grad_s = (probs_float * (grad_p - delta_sum)).astype(BF16)
    grad_q = (
        jnp.einsum("kgqs,skd->qkgd", grad_s, keys_rot, preferred_element_type=F32) * score_scale
    )
    grad_k = (
        jnp.einsum("kgqs,qkgd->skd", grad_s, query_rows, preferred_element_type=F32) * score_scale
    )
    grad_v = jnp.einsum("kgqs,qkgd->skd", attn_probs, grad_ctx, preferred_element_type=F32)
    grad_q_lin = (
        rotate(grad_q.reshape(tokens, QUERY_HEADS, HEAD_SIZE), query_cos, -query_sin)
        .astype(BF16)
        .reshape(tokens, -1)
    )
    grad_kv = jnp.stack([rotate(grad_k, key_cos, -key_sin), grad_v], 2).reshape(2 * tokens, -1)
    grad_kv_other = lax.ppermute(grad_kv[:tokens].astype(BF16), "mp", flips[1])
    grad_kv_lin = (grad_kv[tokens:] + grad_kv_other.astype(F32)).astype(BF16)
    grad_normed_one = jnp.einsum(
        "tc,dc->td", grad_q_lin, query_full, preferred_element_type=F32
    ) + jnp.einsum("tc,dc->td", grad_kv_lin, keyval_full, preferred_element_type=F32)
    grad_query = jnp.einsum("td,tc->dc", normed_one, grad_q_lin, preferred_element_type=F32)
    grad_keyval = jnp.einsum("td,tc->dc", normed_one, grad_kv_lin, preferred_element_type=F32)
    scaled_one = gain_one * grad_normed_one
    input_grad = (
        grad_hidden
        + inv_one * scaled_one
        - residual_in * inv_one**3 * jnp.mean(scaled_one * residual_in, -1, keepdims=True)
    )
    grad_gain_one = jnp.sum(grad_normed_one * residual_in * inv_one, 0)

    grads = jnp.stack([grad_query, grad_keyval, grad_output]).astype(BF16)
    small_grads = jnp.zeros((n_dp, n_mp, 8 + own_router, lanes), F32)
    small_grads = small_grads.at[:, :, 0, :own_gain].set(grad_gain_one.reshape(n_dp, n_mp, -1))
    small_grads = small_grads.at[:, :, 1, :own_gain].set(grad_gain_two.reshape(n_dp, n_mp, -1))
    small_grads = small_grads.at[:, :, 8:, :EXPERTS].set(
        grad_router.reshape(n_dp, n_mp, own_router, EXPERTS)
    )
    grads, small_grads = reduce_weights(n_dp, n_mp, 5, grads, small_grads)
    query_grad, keyval_grad, output_grad = grads[0], grads[1], grads[2].T
    gain_one_grad, gain_two_grad = small_grads[0, :own_gain], small_grads[1, :own_gain]
    router_grad = small_grads[8:, :EXPERTS]
    matrix_rate = 0.2 / math.sqrt(MODEL_WIDTH)
    gain_one_all = adamw(attn_gain, gain_one_grad, attn_gain_mean, attn_gain_var, 0.1, 0.0)
    query_all = adamw(query_w, query_grad, query_mean, query_var, matrix_rate, 0.1)
    keyval_all = adamw(
        key_value_weight,
        keyval_grad,
        key_value_first_moment,
        key_value_second_moment,
        matrix_rate,
        0.1,
    )
    output_all = adamw(output_w, output_grad, output_mean, output_var, 0.1, 0.1)
    gain_two_all = adamw(moe_gain, gain_two_grad, moe_gain_mean, moe_gain_var, 0.1, 0.0)
    router_all = adamw(router_w, router_grad, router_mean, router_var, matrix_rate, 0.1)
    gateup_all = adamw(gateup_w, gateup_grad, gateup_mean, gateup_var, matrix_rate, 0.1)
    down_all = adamw(down_w, down_grad, down_mean, down_var, 0.07, 0.1)
    return (
        block_out,
        input_grad,
        gain_one_all[0],
        gain_one_all[1],
        gain_one_all[2],
        gain_one_all[3],
        query_all[0],
        query_all[1],
        query_all[2],
        query_all[3],
        keyval_all[0],
        keyval_all[1],
        keyval_all[2],
        keyval_all[3],
        output_all[0],
        output_all[1],
        output_all[2],
        output_all[3],
        gain_two_all[0],
        gain_two_all[1],
        gain_two_all[2],
        gain_two_all[3],
        router_all[0],
        router_all[1],
        router_all[2],
        router_all[3],
        gateup_all[0],
        gateup_all[1],
        gateup_all[2],
        gateup_all[3],
        down_all[0],
        down_all[1],
        down_all[2],
        down_all[3],
    )


def solution(mesh):
    in_specs = (
        P(("dp", "mp"), None),
        P(("dp", "mp"), None),
        P(("dp", "mp"), None),
        P(("dp", "mp")),
        P("dp", "mp"),
        P("dp", "mp"),
        P("mp", "dp"),
        P(("dp", "mp")),
        P(("dp", "mp"), None),
        P("dp", None, "mp", None),
        P("dp", "mp", None),
        P(("dp", "mp")),
        P(("dp", "mp")),
        P("dp", "mp"),
        P("dp", "mp"),
        P("dp", "mp"),
        P("dp", "mp"),
        P("mp", "dp"),
        P("mp", "dp"),
        P(("dp", "mp")),
        P(("dp", "mp")),
        P(("dp", "mp"), None),
        P(("dp", "mp"), None),
        P("dp", None, "mp", None),
        P("dp", None, "mp", None),
        P("dp", "mp", None),
        P("dp", "mp", None),
    )
    out_specs = (
        P(("dp", "mp"), None),
        P(("dp", "mp"), None),
        P(("dp", "mp")),
        P(("dp", "mp")),
        P(("dp", "mp")),
        P(("dp", "mp")),
        P("dp", "mp"),
        P("dp", "mp"),
        P("dp", "mp"),
        P("dp", "mp"),
        P("dp", "mp"),
        P("dp", "mp"),
        P("dp", "mp"),
        P("dp", "mp"),
        P("mp", "dp"),
        P("mp", "dp"),
        P("mp", "dp"),
        P("mp", "dp"),
        P(("dp", "mp")),
        P(("dp", "mp")),
        P(("dp", "mp")),
        P(("dp", "mp")),
        P(("dp", "mp"), None),
        P(("dp", "mp"), None),
        P(("dp", "mp"), None),
        P(("dp", "mp"), None),
        P("dp", None, "mp", None),
        P("dp", None, "mp", None),
        P("dp", None, "mp", None),
        P("dp", None, "mp", None),
        P("dp", "mp", None),
        P("dp", "mp", None),
        P("dp", "mp", None),
        P("dp", "mp", None),
    )
    step = functools.partial(local, mesh.shape["dp"], mesh.shape["mp"])
    return jax.shard_map(step, mesh=mesh, in_specs=in_specs, out_specs=out_specs, check_vma=False)
```

time: 1260 us -> 900 us (0.71)
  waiting for transfers between devices: 724 us -> 101 us
  Pallas kernels: 0 us -> 497 us
  blocking collectives: 199 us -> 0 us
  local copies, waits for them, and re-layouts: 103 us -> 84.3 us
  other arithmetic: 84.4 us -> 71 us
  between operations: 15.5 us -> 2.74 us
    reduce_scatter x8 -> x0, waiting for transfers between devices: 507 us -> none  [the longest x2 139 us: rows_sum(): return lax.psum_scatter(value, 'mp', scatter_dimension=0, tiled=True)]
    pallas_call x0 -> x6, Pallas kernels: none -> 497 us  [the longest x1 170 us: gather_weights(): pl.pallas_call(kernel, out_shape=(jax.ShapeDtypeStruct((n_dp, n_mp) + sma...]
    all_to_all x4 -> x0, waiting for transfers between devices: 135 us -> none  [the longest x2 80 us: from_owner(): return lax.all_to_all(buffer, 'dp', split_axis=1, concat_axis=0, tiled=True)]
    all_gather x4 -> x0, blocking collectives: 114 us -> none  [the longest x1 82.8 us: local(): lax.all_gather(router_w, ('dp', 'mp'), axis=0, tiled=True)]
    ppermute x0 -> x8, waiting for transfers between devices: none -> 101 us  [the longest x1 101 us: local(): grad_kv_other = lax.ppermute(grad_kv[:tokens].astype(BF16), 'mp', flips[1])]
    unnamed x2 -> x0, blocking collectives: 85.5 us -> none
    all_gather x4 -> x0, waiting for transfers between devices: 82.1 us -> none  [the longest x2 42.9 us: rows_gather(): return lax.all_gather(value, 'mp', axis=0, tiled=True)]
    gather x3 -> x0, local copies, waits for them, and re-layouts: 37 us -> none  [the longest x1 14.1 us: local(): picked_rows = returned[flat_slot].reshape(rows_own, TOPK, MODEL_WIDTH)]
  transfers between devices with their start and end apart: 16 -> 8, of which waited for: 14 -> 1; matrix products, arithmetic and copies ran while one was open for 15% -> 13% of each run, Pallas kernels for 0% -> 40%
where the time goes in v1:
time: 900 us; the launch traced here: 892 us
  Pallas kernels  497 us (55%)
  matrix products  120 us (13%)
  waiting for transfers between devices  101 us (11%)
  local copies, waits for them, and re-layouts  84.3 us (9%)
  other arithmetic  71 us (8%)
  starting transfers between devices  15.1 us (2%)
    pallas_call x1, Pallas kernels, gather_weights(): pl.pallas_call(kernel, out_shape=(jax.ShapeDtypeStruct((n_dp, n_mp) + sma...  170 us
    pallas_call x2, Pallas kernels, reduce_tokens(): pl.pallas_call(kernel, out_shape=tuple(out_shape), in_specs=[vmem()] * (2...  143 us
    pallas_call x2, Pallas kernels, gather_tokens(): pl.pallas_call(kernel, out_shape=(jax.ShapeDtypeStruct((2, n_dp) + rows.s...  128 us
    ppermute x1, waiting for transfers between devices, local(): grad_kv_other = lax.ppermute(grad_kv[:tokens].astype(BF16), 'mp', flips[1])  101 us
    pallas_call x1, Pallas kernels, reduce_weights(): pl.pallas_call(kernel, out_shape=(jax.ShapeDtypeStruct((kinds, rows, cols...  56.7 us
    unnamed x222, local copies, waits for them, and re-layouts  36.5 us
  transfers between devices with their start and end apart: 8, of which 1 were waited for; matrix products, arithmetic and copies ran while one was open for 13% of the time, Pallas kernels for 40%

profile of v1, /device:TPU:0, one launch (start us, length us, event | category | flops | bytes accessed | tf_op | source)
XLA Modules:
  0.0 891.8 jit_solution(12150144340844053734)
XLA Ops:
  12.6 170.1 %gather_weights.1 = (f32[8,4,40,128]{3,2,1,0:T(8,128)}, bf16[3,1024,1024]{2,1,0:T(8,128)(2,1)}) custom-call(f32[40,128]{1,0:T(8,128)} %copy-done.65, bf16[3,128,256]{2,1,0:T(8,128)(2,1)} %pad_maximum_fusion.9.shard_ref), custom_call_target="tpu_custom_call" | custom-call | tf_op jit(solution)/shard_map/gather_weights/pallas_call | solution.py:288
  184.7 5.3 collective-permute-start
  206.6 64.1 %gather_tokens.2 = (bf16[2,8,256,1024]{3,2,1,0:T(8,128)(2,1)}, s32[2,8,32,256]{3,2,1,0:T(8,128)}) custom-call(bf16[256,1024]{1,0:T(8,128)(2,1)} %convert_element_type.150.rows_ref, s32[32,256]{1,0:T(8,128)} %fusion.71.table_ref), custom_call_target="tpu_custom_call" | custom-call | tf_op jit(solution)/shard_map/gather_tokens/pallas_call | solution.py:365
  271.6 8.8 convert_bitcast_fusion
  287.1 10.2 %copy.248 = f32[2,16,80,1024]{3,2,1,0:T(8,128)} copy(f32[2,16,80,1024]{3,2,0,1:T(8,128)} %convert_bitcast_fusion) | data formatting | bytes 20971520 | tf_op jit(solution)/shard_map/convert_element_type | solution.py:745
  319.8 63.7 %gather_tokens.3 = (bf16[2,8,256,1024]{3,2,1,0:T(8,128)(2,1)}, f32[2,8,32,256]{3,2,1,0:T(8,128)}) custom-call(bf16[256,1024]{1,0:T(8,128)(2,1)} %copy-done.14, f32[32,256]{1,0:T(8,128)} %fusion.83.table_ref), custom_call_target="tpu_custom_call" | custom-call | tf_op jit(solution)/shard_map/gather_tokens/pallas_call | solution.py:365
  383.5 7.3 convert_bitcast_fusion.1
  390.7 5.7 copy.242
  407.0 8.4 fusion.94
  421.4 7.1 fusion
  430.4 8.2 fusion.1
  445.8 10.7 %fusion.23 = (bf16[2,1280,1,512]{3,1,0,2:T(8,128)(2,1)}, bf16[2,1280,1,512]{3,1,0,2:T(8,128)(2,1)}) fusion(f32[2,1280,2,512]{3,1,2,0:T(8,128)S(1)} %bitcast.323, bf16[2,1280,1024]{2,1,0:T(8,128)(2,1)} %copy-done.21, bf16[2,512,1024]{2,1,0:T(8,128)(2,1)} %bitcast.326), kind=kOutput, calls=%fused_computation.57 | convolution fusion | flops 2701393920 | bytes 23068672 | tf_op jit(solution)/shard_map/erd,efd->erf/dot_general | solution.py:755
  456.5 10.6 %fusion.19 = bf16[2,2,512,1024]{3,2,1,0:T(8,128)(2,1)} fusion(bf16[2,1280,1024,1]{2,1,3,0:T(8,128)(2,1)} %bitcast.330, bf16[2,1280,1,512]{3,1,0,2:T(8,128)(2,1)} %get-tuple-element.335, bf16[2,1280,1,512]{3,1,0,2:T(8,128)(2,1)} %get-tuple-element.334), kind=kOutput, calls=%fused_computation.52 | convolution fusion | flops 5373427712 | bytes 14680064 | tf_op jit(solution)/shard_map/ercf,erd->ecfd/dot_general | solution.py:763
  467.1 7.5 bitcast_convert_fusion.2
  474.6 5.8 bitcast_convert_fusion.1
  480.5 73.9 %reduce_tokens.2 = (f32[256,1024]{1,0:T(8,128)S(1)}, f32[8,2,8,256]{3,2,1,0:T(8,128)S(1)}) custom-call(bf16[2,8,256,1024]{3,2,1,0:T(8,128)(2,1)} %bitcast.317, f32[2,8,8,256]{3,2,1,0:T(8,128)S(1)} %bitcast.312), custom_call_target="tpu_custom_call" | custom-call | tf_op jit(solution)/shard_map/reduce_tokens/pallas_call | solution.py:467
  555.7 8.2 bitcast_convert_fusion
  564.0 68.8 %reduce_tokens.3 = f32[256,1024]{1,0:T(8,128)S(1)} custom-call(bf16[2,8,256,1024]{3,2,1,0:T(8,128)(2,1)} %bitcast.318), custom_call_target="tpu_custom_call" | custom-call | tf_op jit(solution)/shard_map/reduce_tokens/pallas_call | solution.py:467
  642.5 5.3 fusion.2
  674.1 101.5 %collective-permute-done.4 = bf16[256,1024]{0,1:T(8,128)(2,1)} collective-permute-done((bf16[256,1024]{0,1:T(8,128)(2,1)}, bf16[256,1024]{0,1:T(8,128)(2,1)}, u32[]{:S(2)}, u32[]{:S(2)}) %collective-permute-start.4) | collective-permute-done | bytes 524320 | tf_op jit(solution)/shard_map/ppermute | solution.py:822
  786.4 6.4 pad_maximum_fusion.1.grads_ref
  793.0 56.7 %reduce_weights.1 = (f32[3,128,256]{2,1,0:T(8,128)S(1)}, f32[40,128]{1,0:T(8,128)S(1)}) custom-call(bf16[3,1024,1024]{2,1,0:T(8,128)(2,1)} %pad_maximum_fusion.1.grads_ref, f32[8,4,40,128]{3,2,1,0:T(8,128)S(1)} %scatter.29.small_ref), custom_call_target="tpu_custom_call" | custom-call | tf_op jit(solution)/shard_map/reduce_weights/pallas_call | solution.py:550
  865.9 7.5 multiply_subtract_fusion
  873.4 4.9 copy.275
  (348 shorter events, 162.5 us)
Async XLA Ops:
  3.7 180.1 %copy-start.8 = (f32[256,1024]{1,0:T(8,128)S(1)}, f32[256,1024]{1,0:T(8,128)}, u32[]{:S(2)}) copy-start(f32[256,1024]{1,0:T(8,128)} %param.39) | copy-start | bytes 3145732
  5.1 392.3 %collective-permute-start.2 = (bf16[2,3,128,1024]{3,2,1,0:T(8,128)(2,1)}, bf16[2,3,128,1024]{3,2,1,0:T(8,128)(2,1)}, u32[]{:S(2)}, u32[]{:S(2)}) collective-permute-start(bf16[2,3,128,1024]{3,2,1,0:T(8,128)(2,1)} %get-tuple-element.343), channel_id=1, source_target_pairs={{0,2},{1,3},{2,0},{3,1},{4,6},{5,7},{6,4},{7,5},{8,10},{9,11},{10,... | collective-permute-start | bytes 4718600 | tf_op jit(solution)/shard_map/ppermute | solution.py:642
  9.1 388.2 %collective-permute-start.3 = (bf16[2,3,128,1024]{3,2,1,0:T(8,128)(2,1)}, bf16[2,3,128,1024]{3,2,1,0:T(8,128)(2,1)}, u32[]{:S(2)}, u32[]{:S(2)}) collective-permute-start(bf16[2,3,128,1024]{3,2,1,0:T(8,128)(2,1)} %get-tuple-element.343), channel_id=1, source_target_pairs={{0,3},{1,2},{2,1},{3,0},{4,7},{5,6},{6,5},{7,4},{8,11},{9,10},{10,... | collective-permute-start | bytes 4718600 | tf_op jit(solution)/shard_map/ppermute | solution.py:642
  10.5 174.0 %copy-start.37 = (f32[256,128]{0,1:T(8,128)}, f32[256,128]{0,1:T(8,128)S(1)}, u32[]{:S(2)}) copy-start(f32[256,128]{0,1:T(8,128)S(1)} %copy.235) | copy-start | bytes 393220
  184.7 118.3 %copy-start.19 = (bf16[256,1024]{1,0:T(8,128)(2,1)}, bf16[256,1024]{1,0:T(8,128)(2,1)S(1)}, u32[]{:S(2)}) copy-start(bf16[256,1024]{1,0:T(8,128)(2,1)S(1)} %multiply_convert_fusion.5) | copy-start | bytes 1572868
  184.7 118.3 %collective-permute-start = (bf16[256,1024]{1,0:T(8,128)(2,1)S(1)}, bf16[256,1024]{1,0:T(8,128)(2,1)}, u32[]{:S(2)}, u32[]{:S(2)}) collective-permute-start(bf16[256,1024]{1,0:T(8,128)(2,1)S(1)} %multiply_convert_fusion.5), channel_id=1, source_target_pairs={{0,1},{1,0},{2,3},{3,2},{4,5},{5,4},{6,7},{7,6},{8,9},{9,8},{10,11... | collective-permute-start | bytes 1572872 | tf_op jit(solution)/shard_map/ppermute | solution.py:668
  190.0 207.3 %collective-permute-start.1 = (bf16[2,3,128,1024]{3,2,1,0:T(8,128)(2,1)S(1)}, bf16[2,3,128,1024]{3,2,1,0:T(8,128)(2,1)}, u32[]{:S(2)}, u32[]{:S(2)}) collective-permute-start(bf16[2,3,128,1024]{3,2,1,0:T(8,128)(2,1)S(1)} %get-tuple-element.342), channel_id=1, source_target_pairs={{0,1},{1,0},{2,3},{3,2},{4,5},{5,4},{6,7},{7,6},{8,9},{9,8},{10,11... | collective-permute-start | bytes 4718600 | tf_op jit(solution)/shard_map/ppermute | solution.py:642
  190.1 90.3 %copy-start.85 = (f32[32]{0:T(128)}, f32[32]{0:T(128)S(1)}, u32[]{:S(2)}) copy-start(f32[32]{0:T(128)S(1)} %multiply_exponential_fusion) | copy-start | bytes 388
  480.4 74.0 %copy-start.48 = (s32[256,32]{0,1:T(8,128)S(1)}, s32[256,32]{0,1:T(8,128)}, u32[]{:S(2)}) copy-start(s32[256,32]{0,1:T(8,128)} %copy-done.47) | copy-start | bytes 98308
  480.4 74.0 %copy-start.56 = (f32[256,32]{0,1:T(8,128)S(1)}, f32[256,32]{0,1:T(8,128)}, u32[]{:S(2)}) copy-start(f32[256,32]{0,1:T(8,128)} %copy-done.55) | copy-start | bytes 98308
  480.4 74.0 %copy-start.73 = (f32[256]{0:T(256)S(1)}, f32[256]{0:T(256)}, u32[]{:S(2)}) copy-start(f32[256]{0:T(256)} %copy-done.72) | copy-start | bytes 3076
  480.5 74.1 %copy-start.15 = (bf16[256,1024]{1,0:T(8,128)(2,1)S(1)}, bf16[256,1024]{1,0:T(8,128)(2,1)}, u32[]{:S(2)}) copy-start(bf16[256,1024]{1,0:T(8,128)(2,1)} %copy-done.14) | copy-start | bytes 1572868
  563.9 68.8 %copy-start.13 = (f32[256,1024]{1,0:T(8,128)S(1)}, f32[256,1024]{1,0:T(8,128)}, u32[]{:S(2)}) copy-start(f32[256,1024]{1,0:T(8,128)} %copy-done.12) | copy-start | bytes 3145732
  563.9 68.8 %copy-start.69 = (f32[1024]{0:T(1024)S(1)}, f32[1024]{0:T(1024)}, u32[]{:S(2)}) copy-start(f32[1024]{0:T(1024)} %mul.623) | copy-start | bytes 12292
  563.9 68.8 %copy-start.78 = (f32[256]{0:T(256)S(1)}, f32[256]{0:T(256)}, u32[]{:S(2)}) copy-start(f32[256]{0:T(256)} %copy-done.77) | copy-start | bytes 3076
  563.9 70.0 %copy-start.25 = (f32[256,1024]{1,0:T(8,128)S(1)}, f32[256,1024]{1,0:T(8,128)}, u32[]{:S(2)}) copy-start(f32[256,1024]{1,0:T(8,128)} %param.40) | copy-start | bytes 3145732
  563.9 70.0 %copy-start.84 = (f32[256]{0:T(256)S(1)}, f32[256]{0:T(256)}, u32[]{:S(2)}) copy-start(f32[256]{0:T(256)} %get-tuple-element.374) | copy-start | bytes 3076
  660.3 198.4 %collective-permute-start.5 = (bf16[2,3,128,1024]{3,2,0,1:T(8,128)(2,1)}, bf16[2,3,128,1024]{3,2,0,1:T(8,128)(2,1)}, u32[]{:S(2)}, u32[]{:S(2)}) collective-permute-start(bf16[2,3,128,1024]{3,2,0,1:T(8,128)(2,1)} %get-tuple-element.337), channel_id=1, source_target_pairs={{0,1},{1,0},{2,3},{3,2},{4,5},{5,4},{6,7},{7,6},{8,9},{9,8},{10,11... | collective-permute-start | bytes 4718600 | tf_op jit(solution)/shard_map/ppermute | solution.py:774
  660.3 200.9 %collective-permute-start.6 = (bf16[2,3,128,1024]{3,2,0,1:T(8,128)(2,1)}, bf16[2,3,128,1024]{3,2,0,1:T(8,128)(2,1)}, u32[]{:S(2)}, u32[]{:S(2)}) collective-permute-start(bf16[2,3,128,1024]{3,2,0,1:T(8,128)(2,1)} %get-tuple-element.339), channel_id=1, source_target_pairs={{0,2},{1,3},{2,0},{3,1},{4,6},{5,7},{6,4},{7,5},{8,10},{9,11},{10,... | collective-permute-start | bytes 4718600 | tf_op jit(solution)/shard_map/ppermute | solution.py:774
  663.3 197.9 %collective-permute-start.7 = (bf16[2,3,128,1024]{3,2,0,1:T(8,128)(2,1)}, bf16[2,3,128,1024]{3,2,0,1:T(8,128)(2,1)}, u32[]{:S(2)}, u32[]{:S(2)}) collective-permute-start(bf16[2,3,128,1024]{3,2,0,1:T(8,128)(2,1)} %get-tuple-element.338), channel_id=1, source_target_pairs={{0,3},{1,2},{2,1},{3,0},{4,7},{5,6},{6,5},{7,4},{8,11},{9,10},{10,... | collective-permute-start | bytes 4718600 | tf_op jit(solution)/shard_map/ppermute | solution.py:774
  665.8 109.8 %collective-permute-start.4 = (bf16[256,1024]{0,1:T(8,128)(2,1)}, bf16[256,1024]{0,1:T(8,128)(2,1)}, u32[]{:S(2)}, u32[]{:S(2)}) collective-permute-start(bf16[256,1024]{0,1:T(8,128)(2,1)} %bitcast.86), channel_id=1, source_target_pairs={{0,1},{1,0},{2,3},{3,2},{4,5},{5,4},{6,7},{7,6},{8,9},{9,8},{10,11... | collective-permute-start | bytes 1572872 | tf_op jit(solution)/shard_map/ppermute | solution.py:822
  669.5 106.1 %copy-start.24 = (f32[256,8,2,64]{0,3,2,1:T(8,128)S(1)}, f32[256,8,2,64]{0,3,2,1:T(8,128)}, u32[]{:S(2)}) copy-start(f32[256,8,2,64]{0,3,2,1:T(8,128)} %copy.256) | copy-start | bytes 3145732
  671.6 107.4 %copy-start.71 = (f32[1024]{0:T(1024)S(1)}, f32[1024]{0:T(1024)}, u32[]{:S(2)}) copy-start(f32[1024]{0:T(1024)} %copy-done.70) | copy-start | bytes 12292
  671.6 107.4 %copy-start.80 = (f32[256]{0:T(256)S(1)}, f32[256]{0:T(256)}, u32[]{:S(2)}) copy-start(f32[256]{0:T(256)} %copy-done.79) | copy-start | bytes 3076
  (89 other events, 1497.9 us)

commit v2 on v1

--- a/solution.py
+++ b/solution.py
@@ -303,182 +303,507 @@
     )(small, shards)
 
 
-def gather_tokens(n_dp, n_mp, identity, rows, table):
-    half = n_mp // 2
-    tokens = rows.shape[0]
-    order_a, order_b = orders_of(n_dp)
-    n_copies = 2 + 6 * (n_dp - 1)
-
-    def kernel(rows_ref, table_ref, rows_all, table_all, send_sems, recv_sems, local_sems):
+def gather_tokens(n_dp, groups, identity, rows):
+    n_copies = groups - 1 + 2 * groups * (n_dp - 1)
+
+    def kernel(rows_ref, rows_all, send_sems, recv_sems, local_sem):
         dp, mp = lax.axis_index("dp"), lax.axis_index("mp")
         me = (dp, mp)
-        partner = (dp, flip_all(mp, half))
+        partner = (dp, flip(mp, 1))
         copies = Copies(send_sems, recv_sems)
-        keep = [
-            pltpu.make_async_copy(rows_ref, rows_all.at[0, 0], local_sems.at[0]),
-            pltpu.make_async_copy(table_ref, table_all.at[0, 0], local_sems.at[1]),
-        ]
-        for copy in keep:
-            copy.start()
-        greet([(flip_all(dp, mask), mp) for mask in bits_of(n_dp)] + [partner])
-        across = (copies.slot(), copies.slot())
-        copies.start(rows_ref, rows_all.at[1, 0], partner, across[0])
-        copies.start(table_ref, table_all.at[1, 0], partner, across[1])
-
-        def row_tree(group, part, order):
-            cut = pl.ds(part * (tokens // 2), tokens // 2)
-            return TreeGather(
-                copies,
-                order,
-                n_dp,
-                me,
-                lambda j: rows_all.at[group, j, cut],
-                lambda j, mask: rows_all.at[group, j ^ mask, cut],
-            )
-
-        def table_tree(group, order):
-            return TreeGather(
-                copies,
-                order,
-                n_dp,
-                me,
-                lambda j: table_all.at[group, j],
-                lambda j, mask: table_all.at[group, j ^ mask],
-            )
-
-        groups = [
-            [row_tree(group, 0, order_a), row_tree(group, 1, order_b), table_tree(group, order_a)]
-            for group in range(2)
-        ]
-        for copy in keep:
-            copy.wait()
-        for one in groups[0]:
+        keep = pltpu.make_async_copy(rows_ref, rows_all.at[0, 0], local_sem.at[0])
+        keep.start()
+        greet([(flip_all(dp, mask), mp) for mask in bits_of(n_dp)] + [partner] * (groups - 1))
+        if groups > 1:
+            across = copies.slot()
+            copies.start(rows_ref, rows_all.at[1, 0], partner, across)
+        trees = [row_trees(copies, n_dp, me, rows_all, group) for group in range(groups)]
+        keep.wait()
+        for one in trees[0]:
             one.send(0)
-        run_gathers(groups[0])
-        copies.wait(rows_all.at[1, 0], me, across[0])
-        copies.wait(table_all.at[1, 0], me, across[1])
-        for one in groups[1]:
-            one.send(0)
-        run_gathers(groups[1])
+        if groups > 1:
+            copies.wait(rows_all.at[1, 0], me, across)
+            for one in trees[1]:
+                one.send(0)
+        run_gathers(sum(trees, []))
         copies.finish()
 
     return pl.pallas_call(
         kernel,
-        out_shape=(
-            jax.ShapeDtypeStruct((2, n_dp) + rows.shape, rows.dtype),
-            jax.ShapeDtypeStruct((2, n_dp) + table.shape, table.dtype),
-        ),
-        in_specs=[hbm(), hbm()],
-        out_specs=(hbm(), hbm()),
+        out_shape=jax.ShapeDtypeStruct((groups, n_dp) + rows.shape, rows.dtype),
+        in_specs=[hbm()],
+        out_specs=hbm(),
         scratch_shapes=[
             pltpu.SemaphoreType.DMA((n_copies,)),
             pltpu.SemaphoreType.DMA((n_copies,)),
-            pltpu.SemaphoreType.DMA((2,)),
+            pltpu.SemaphoreType.DMA((1,)),
         ],
         compiler_params=params(identity),
         name="gather_tokens",
-    )(rows, table)
-
-
-def reduce_tokens(n_dp, n_mp, identity, terms, table=None):
-    half = n_mp // 2
-    tokens, width = terms.shape[2:]
-    order_a, order_b = orders_of(n_dp)
-    n_copies = 4 * (n_dp - 1) + 1 + (2 * n_dp - 1 if table is not None else 0)
-
-    def kernel(*refs):
-        if table is not None:
-            terms_ref, table_ref, out_ref, parts_ref, *refs = refs
-        else:
-            terms_ref, out_ref, *refs = refs
-        rooms, across, send_sems, recv_sems, local_sems = refs
-        dp, mp = lax.axis_index("dp"), lax.axis_index("mp")
-        me = (dp, mp)
-        other = flip_all(mp, half)
-        partner = (dp, other)
-        copies = Copies(send_sems, recv_sems)
-        if table is not None:
-            greet(
-                [
-                    (flip_all(dp, j), other if group else mp)
-                    for group in range(2)
-                    for j in range(n_dp)
-                    if group + j
-                ]
-            )
-        else:
-            greet([(flip_all(dp, mask), mp) for mask in bits_of(n_dp)] + [partner])
-        kind = lax.div(mp, half)
-        parts = {}
-        if table is not None:
-            keep = pltpu.make_async_copy(
-                table_ref.at[0, 0], parts_ref.at[dp, kind], local_sems.at[0]
-            )
-            keep.start()
-            for group in range(2):
-                for j in range(n_dp):
-                    if group + j:
-                        device = (flip_all(dp, j), other if group else mp)
-                        parts[group, j] = copies.slot()
-                        copies.start(
-                            table_ref.at[group, j], parts_ref.at[dp, kind], device, parts[group, j]
-                        )
+    )(rows)
+
+
+def row_trees(copies, n_dp, me, rows_all, group):
+    tokens = rows_all.shape[2]
+
+    def tree(part, order):
+        cut = pl.ds(part * (tokens // 2), tokens // 2)
+        return TreeGather(
+            copies,
+            order,
+            n_dp,
+            me,
+            lambda j: rows_all.at[group, j, cut],
+            lambda j, mask: rows_all.at[group, j ^ mask, cut],
+        )
+
+    return [tree(part, order) for part, order in enumerate(orders_of(n_dp))]
+
+
+class TokenReduce:
+    def __init__(self, copies, n_dp, me, terms, rooms, across):
+        dp, mp = me
+        self.copies, self.me, self.across = copies, me, across
+        self.partner = (dp, flip(mp, 1))
+        self.tokens = terms.shape[2]
+        self.n_dp = n_dp
+        self.last = n_dp.bit_length() - 2
+        self.groups = terms.shape[0]
+        self.slot = copies.slot()
 
         def tree(group, part, order):
-            cut = pl.ds(part * (tokens // 2), tokens // 2)
+            cut = pl.ds(part * (self.tokens // 2), self.tokens // 2)
             return TreeReduce(
                 copies,
                 order,
                 n_dp,
                 me,
-                lambda j: terms_ref.at[group, j, cut],
+                lambda j: terms.at[group, j, cut],
                 lambda number: rooms.at[group, part, number],
                 add_rows(),
             )
 
-        groups = [[tree(group, 0, order_a), tree(group, 1, order_b)] for group in (1, 0)]
-        run_reduces(groups[0] + groups[1])
-        last = copies.slot()
-        mine = [rooms.at[1, part, groups[0][part].number((0, len(order_a) - 1))] for part in (0, 1)]
-        own = [rooms.at[0, part, groups[1][part].number((0, len(order_a) - 1))] for part in (0, 1)]
-        for part in (0, 1):
-            out_ref[pl.ds(part * (tokens // 2), tokens // 2), :] = mine[part][...].astype(F32)
-        for part in (0, 1):
-            across[0, pl.ds(part * (tokens // 2), tokens // 2), :] = mine[part][...]
-        copies.start(across.at[0], across.at[1], partner, last)
-        copies.wait(across.at[1], me, last)
-        for part in (0, 1):
-            cut = pl.ds(part * (tokens // 2), tokens // 2)
-            out_ref[cut, :] = own[part][...].astype(F32) + across[1, cut, :].astype(F32)
-        if table is not None:
-            keep.wait()
-            for group in range(2):
-                for j in range(n_dp):
-                    if group + j:
-                        theirs = 1 - kind if group else kind
-                        copies.wait(
-                            parts_ref.at[flip_all(dp, j), theirs], me, parts[group, j]
-                        )
+        self.trees = [
+            [tree(group, part, order) for part, order in enumerate(orders_of(n_dp))]
+            for group in range(self.groups)
+        ]
+
+    def first(self, group, j):
+        for tree in self.trees[group]:
+            tree.send(j)
+
+    def level(self, group, p):
+        if group == self.groups:
+            return
+        for j in range(1, self.n_dp):
+            for tree in self.trees[group]:
+                if place_of(tree.order, j) == p:
+                    tree.collect(j)
+                    tree.send(j)
+
+    def pass_on(self):
+        if self.groups == 1:
+            return
+        for part, tree in enumerate(self.trees[1]):
+            tree.collect(0)
+            cut = pl.ds(part * (self.tokens // 2), self.tokens // 2)
+            self.across[0, cut, :] = tree.total()[...]
+        self.copies.start(self.across.at[0], self.across.at[1], self.partner, self.slot)
+
+    def end(self, out_ref):
+        for tree in self.trees[0]:
+            tree.collect(0)
+        if self.groups > 1:
+            self.copies.wait(self.across.at[1], self.me, self.slot)
+        for part, tree in enumerate(self.trees[0]):
+            cut = pl.ds(part * (self.tokens // 2), self.tokens // 2)
+            total = tree.total()[...].astype(F32)
+            if self.groups > 1:
+                total = total + self.across[1, cut, :].astype(F32)
+            out_ref[cut, :] = total
+
+
+def reduce_rooms(groups, n_dp, tokens, width, dtype):
+    return [
+        pltpu.VMEM((groups, 2, n_dp - 1, tokens // 2, width), dtype),
+        pltpu.VMEM((2, tokens, width), dtype),
+    ]
+
+
+def reduce_tokens(identity, terms):
+    groups, n_dp, tokens, width = terms.shape
+    n_copies = 2 * groups * (n_dp - 1) + 1
+
+    def kernel(terms_ref, out_ref, rooms, across, send_sems, recv_sems):
+        dp, mp = lax.axis_index("dp"), lax.axis_index("mp")
+        me = (dp, mp)
+        copies = Copies(send_sems, recv_sems)
+        greet(
+            [(flip_all(dp, mask), mp) for mask in bits_of(n_dp)]
+            + [(dp, flip(mp, 1))] * (groups - 1)
+        )
+        reduce = TokenReduce(copies, n_dp, me, terms_ref, rooms, across)
+        for group in range(groups)[::-1]:
+            for j in range(1, n_dp, 2):
+                reduce.first(group, j)
+        for p in range(reduce.last - 1, -1, -1):
+            reduce.level(1, p)
+        reduce.pass_on()
+        for p in range(reduce.last - 1, -1, -1):
+            reduce.level(0, p)
+        reduce.end(out_ref)
         copies.finish()
 
-    out_shape = [jax.ShapeDtypeStruct((tokens, width), F32)]
-    if table is not None:
-        out_shape.append(jax.ShapeDtypeStruct((n_dp, 2) + table.shape[2:], table.dtype))
     return pl.pallas_call(
         kernel,
-        out_shape=tuple(out_shape),
-        in_specs=[vmem()] * (2 if table is not None else 1),
-        out_specs=tuple([vmem()] * len(out_shape)),
-        scratch_shapes=[
-            pltpu.VMEM((2, 2, n_dp - 1, tokens // 2, width), terms.dtype),
-            pltpu.VMEM((2, tokens, width), terms.dtype),
+        out_shape=jax.ShapeDtypeStruct((tokens, width), F32),
+        in_specs=[vmem()],
+        out_specs=vmem(),
+        scratch_shapes=reduce_rooms(groups, n_dp, tokens, width, terms.dtype)
+        + [
             pltpu.SemaphoreType.DMA((n_copies,)),
             pltpu.SemaphoreType.DMA((n_copies,)),
-            pltpu.SemaphoreType.DMA((1,)),
         ],
         compiler_params=params(identity, 48 << 20),
         name="reduce_tokens",
-    )(*([terms, table] if table is not None else [terms]))
+    )(terms)
+
+
+def dot(a, b, contract):
+    return lax.dot_general(a, b, ((contract[:1], contract[1:]), ((), ())), preferred_element_type=F32)
+
+
+NN, NT, TN = (1, 0), (1, 1), (0, 0)
+
+
+def run_expert(n_dp, n_mp, groups, identity, index, shared, parts, inputs):
+    first, last = index == 0, index == shared - 1
+    hidden, width = parts[0].shape[1:]
+    units = n_mp * hidden
+    blocks = groups * n_dp
+    slots = blocks * CAP
+    tokens = inputs["rows"].shape[0] if first else inputs["tokens"]
+    per_tile = 4
+    tile = per_tile * CAP
+    low = lambda *shape: jax.ShapeDtypeStruct(shape, BF16)
+    single = lambda *shape: jax.ShapeDtypeStruct(shape, F32)
+
+    arrays, places = {}, {}
+
+    def give(name, value, spec):
+        arrays[name], places[name] = value, spec
+
+    for k in range(n_mp):
+        give(f"part{k}", parts[k], hbm())
+    if first:
+        give("rows", inputs["rows"], hbm())
+        give("own_table", inputs["table"], hbm())
+        give("cots", inputs["cots"], hbm())
+    else:
+        give("tables_in", inputs["tables"], vmem())
+        give("gates_in", inputs["gates"], vmem())
+        give("x_in", inputs["x"][index], vmem())
+        give("c_in", inputs["c"][index], vmem())
+    if last:
+        for i in range(index):
+            give(f"y{i}", inputs["y"][i], vmem())
+            give(f"d{i}", inputs["d"][i], vmem())
+    outs, out_places = {}, {}
+
+    def get(name, shape, spec):
+        outs[name], out_places[name] = shape, spec
+
+    for k in range(n_mp):
+        get(f"grad{k}", low(3, hidden, width), vmem())
+    if first and not last:
+        get("tables", single(blocks, 8, tokens), vmem())
+        for i in range(1, shared):
+            get(f"x{i}", low(slots, width), vmem())
+            get(f"c{i}", low(slots, width), vmem())
+    if not last:
+        get("gates", single(blocks, 8, tokens), vmem())
+        get("y", low(slots, width), vmem())
+        get("d", low(slots, width), vmem())
+    else:
+        get("terms", low(groups, n_dp, tokens, width), hbm())
+        get("gate_parts", single(n_dp, groups, 8, tokens), hbm())
+        get("total", single(tokens, width), vmem())
+    scratch = {
+        "weights": pltpu.VMEM((3, units, width), BF16),
+        "act": pltpu.VMEM((slots, units), BF16),
+        "pair": pltpu.VMEM((slots, 2 * units), BF16),
+        "grad_rows": pltpu.VMEM((slots, width), BF16),
+        "part_sems": pltpu.SemaphoreType.DMA((3 * n_mp,)),
+    }
+    n_copies = 0
+    if first:
+        n_copies += blocks + 2 * groups * (n_dp - 1)
+        scratch["tokens_all"] = pltpu.VMEM((groups, n_dp, tokens, width), BF16)
+        scratch["x_own"] = pltpu.VMEM((slots, width), BF16)
+        scratch["c_own"] = pltpu.VMEM((slots, width), BF16)
+        scratch["cot"] = pltpu.VMEM((2, tokens, width), BF16)
+        scratch["cot_sems"] = pltpu.SemaphoreType.DMA((2,))
+        scratch["keep_sems"] = pltpu.SemaphoreType.DMA((2,))
+        if last:
+            scratch["tables"] = pltpu.VMEM((blocks, 8, tokens), F32)
+    if last:
+        n_copies += 2 * groups * (n_dp - 1) + blocks
+        scratch["gates"] = pltpu.VMEM((blocks, 8, tokens), F32)
+        scratch["y"] = pltpu.VMEM((slots, width), BF16)
+        scratch["d"] = pltpu.VMEM((slots, width), BF16)
+        scratch["grads_all"] = pltpu.VMEM((groups, n_dp, tokens, width), BF16)
+        scratch["sums"] = pltpu.VMEM((2, tokens, width), BF16)
+        scratch["sum_sems"] = pltpu.SemaphoreType.DMA((2,))
+        scratch["gate_sem"] = pltpu.SemaphoreType.DMA((1,))
+        scratch["rooms"], scratch["across"] = reduce_rooms(groups, n_dp, tokens, width, BF16)
+    scratch["send_sems"] = pltpu.SemaphoreType.DMA((n_copies,))
+    scratch["recv_sems"] = pltpu.SemaphoreType.DMA((n_copies,))
+    names = list(arrays) + list(outs) + list(scratch)
+
+    def kernel(*refs):
+        r = dict(zip(names, refs, strict=True))
+        dp, mp = lax.axis_index("dp"), lax.axis_index("mp")
+        me = (dp, mp)
+        other = flip(mp, 1)
+        kind = lax.rem(mp, groups)
+        copies = Copies(r["send_sems"], r["recv_sems"])
+        peers = {
+            (group, j): (flip_all(dp, j), other if group else mp)
+            for group in range(groups)
+            for j in range(n_dp)
+            if group + j
+        }
+        weights, act, pair, grad_rows = r["weights"], r["act"], r["pair"], r["grad_rows"]
+        loads = [
+            pltpu.make_async_copy(
+                r[f"part{k}"].at[c],
+                weights.at[c, pl.ds(k * hidden, hidden)],
+                r["part_sems"].at[3 * k + c],
+            )
+            for k in range(n_mp)
+            for c in range(3)
+        ]
+        for copy in loads:
+            copy.start()
+        tables = r["tables"] if first else r["tables_in"]
+        x_refs = {index: r["x_own"] if first else r["x_in"]}
+        c_refs = {index: r["c_own"] if first else r["c_in"]}
+        if first:
+            x_refs |= {i: r[f"x{i}"] for i in range(1, shared)}
+            c_refs |= {i: r[f"c{i}"] for i in range(1, shared)}
+
+        def hits(block, experts):
+            slot = lax.broadcasted_iota(jnp.int32, (CAP, tokens), 0).astype(F32)
+            found = [slot == tables[block, pl.ds(i, 1), :] for i in experts]
+            return found[0] if len(found) == 1 else jnp.concatenate(found, 0)
+
+        def rows_of(block):
+            return pl.ds(pl.multiple_of(block * CAP, 16), CAP)
+
+        if first:
+            rows_all, cots = r["tokens_all"], r["cots"]
+            keep = [
+                pltpu.make_async_copy(r["rows"], rows_all.at[0, 0], r["keep_sems"].at[0]),
+                pltpu.make_async_copy(
+                    r["own_table"].at[dp, kind], tables.at[0], r["keep_sems"].at[1]
+                ),
+            ]
+            for copy in keep:
+                copy.start()
+            order = [(group, 0) for group in range(groups)]
+            for level in range(1, n_dp.bit_length()):
+                for group in range(groups):
+                    order += [(group, j) for j in range(n_dp) if bin(j).count("1") == level]
+
+            def cot_copy(number):
+                group, j = order[number]
+                return pltpu.make_async_copy(
+                    cots.at[group, j], r["cot"].at[number % 2], r["cot_sems"].at[number % 2]
+                )
+
+            cot_copy(0).start()
+            greet(list(peers.values()))
+            across = copies.slot()
+            if groups > 1:
+                copies.start(r["rows"], rows_all.at[1, 0], peers[1, 0], across)
+            sent = {}
+            for key, device in peers.items():
+                sent[key] = copies.slot()
+                group, j = key
+                copies.start(
+                    r["own_table"].at[device[0], lax.rem(device[1], groups)],
+                    tables.at[group * n_dp + j],
+                    device,
+                    sent[key],
+                )
+            trees = [row_trees(copies, n_dp, me, rows_all, group) for group in range(groups)]
+            keep[0].wait()
+            for tree in trees[0]:
+                tree.send(0)
+            keep[1].wait()
+
+            def fill(number):
+                group, j = order[number]
+                block = group * n_dp + j
+                if number:
+                    copies.wait(tables.at[block], me, sent[group, j])
+                if number + 1 < blocks:
+                    cot_copy(number + 1).start()
+                pick = hits(block, range(shared)).astype(BF16)
+                found = dot(pick, rows_all[group, j], NN).astype(BF16)
+                for i in range(shared):
+                    x_refs[i][block * CAP : (block + 1) * CAP, :] = found[i * CAP : (i + 1) * CAP]
+                cot_copy(number).wait()
+                found = dot(pick, r["cot"][number % 2], NN).astype(BF16)
+                for i in range(shared):
+                    c_refs[i][block * CAP : (block + 1) * CAP, :] = found[i * CAP : (i + 1) * CAP]
+
+            for number, (group, j) in enumerate(order):
+                if j:
+                    for tree in sorted(trees[group], key=lambda tree: place_of(tree.order, j)):
+                        tree.receive(j)
+                        tree.send(j)
+                elif group:
+                    copies.wait(rows_all.at[1, 0], me, across)
+                    for tree in trees[1]:
+                        tree.send(0)
+                fill(number)
+        else:
+            greet(list(peers.values()))
+        if last:
+            gates = r["gates"]
+            if index:
+                gates[...] = r["gates_in"][...]
+        else:
+            gates = r["gates"]
+        for copy in loads:
+            copy.wait()
+        x_all, c_all = x_refs[index], c_refs[index]
+        y_all, d_all = r["y"], r["d"]
+
+        def work(step, carry):
+            rows = pl.ds(pl.multiple_of(step * tile, 16), tile)
+            x = x_all[rows, :]
+            gate = dot(x, weights[0], NT)
+            up = dot(x, weights[1], NT)
+            sigmoid = 1.0 / (1.0 + jnp.exp(-gate))
+            silu = gate * sigmoid
+            activation = (silu * up).astype(BF16)
+            act[rows, :] = activation
+            made = dot(activation, weights[2], NN)
+            cot = c_all[rows, :].astype(F32)
+            chosen, scores = [], []
+            dots = jnp.sum(cot * made, -1, keepdims=True)
+            for b in range(per_tile):
+                block = step * per_tile + b
+                hit = hits(block, (index,))
+                chance = tables[block, pl.ds(4 + index, 1), :]
+                chosen.append(jnp.sum(jnp.where(hit, chance, 0.0), -1, keepdims=True))
+                here = dots[b * CAP : (b + 1) * CAP]
+                gates[block, pl.ds(index, 1), :] = jnp.sum(
+                    jnp.where(hit, here, 0.0), 0, keepdims=True
+                )
+            share = jnp.concatenate(chosen, 0)
+            y_all[rows, :] = (share * made).astype(BF16)
+            back = (share * cot).astype(BF16)
+            grad_rows[rows, :] = back
+            grad_act = dot(back, weights[2], NT)
+            grad_gate = grad_act * up * sigmoid * (1.0 + gate * (1.0 - sigmoid))
+            grad_gate = grad_gate.astype(BF16)
+            grad_up = (grad_act * silu).astype(BF16)
+            pair[rows, pl.ds(0, units)] = grad_gate
+            pair[rows, pl.ds(units, units)] = grad_up
+            d_all[rows, :] = (dot(grad_gate, weights[0], NN) + dot(grad_up, weights[1], NN)).astype(
+                BF16
+            )
+            return carry
+
+        lax.fori_loop(0, blocks // per_tile, work, 0)
+
+        def weight_grad(k):
+            x, back = x_all[...], grad_rows[...]
+            for c, source in enumerate((pair, pair, act)):
+                columns = pl.ds(k * hidden + (units if c == 1 else 0), hidden)
+                rhs = back if c == 2 else x
+                r[f"grad{k}"][c] = dot(source[:, columns], rhs, TN).astype(BF16)
+
+        if not last:
+            for k in range(n_mp):
+                weight_grad(k)
+        else:
+            y_refs = [r[f"y{i}"] for i in range(index)] + [y_all]
+            d_refs = [r[f"d{i}"] for i in range(index)] + [d_all]
+            reduce = TokenReduce(copies, n_dp, me, r["grads_all"], r["rooms"], r["across"])
+            back = range(groups)[::-1]
+            order = [(g, j) for g in back for j in range(1, n_dp, 2)]
+            order += [(g, j) for g in back for j in range(0, n_dp, 2)]
+
+            def sum_copy(number):
+                group, j = order[number]
+                return pltpu.make_async_copy(
+                    r["sums"].at[number % 2], r["terms"].at[group, j], r["sum_sems"].at[number % 2]
+                )
+
+            sent = {}
+            own_gates = pltpu.make_async_copy(
+                gates.at[0], r["gate_parts"].at[dp, kind], r["gate_sem"].at[0]
+            )
+            own_gates.start()
+            for number, (group, j) in enumerate(order):
+                block = group * n_dp + j
+                if group + j:
+                    sent[group, j] = copies.slot()
+                    copies.start(
+                        gates.at[block],
+                        r["gate_parts"].at[dp, kind],
+                        peers[group, j],
+                        sent[group, j],
+                    )
+                pick = hits(block, range(shared)).astype(BF16)
+                there = rows_of(block)
+                found = jnp.concatenate([ref[there, :] for ref in d_refs], 0)
+                r["grads_all"][group, j] = dot(pick, found, TN).astype(BF16)
+                if j % 2:
+                    reduce.first(group, j)
+                found = jnp.concatenate([ref[there, :] for ref in y_refs], 0)
+                if number > 1:
+                    sum_copy(number - 2).wait()
+                r["sums"][number % 2] = dot(pick, found, TN).astype(BF16)
+                sum_copy(number).start()
+            left = list(range(n_mp))
+
+            def some(count):
+                for _ in range(count):
+                    if left:
+                        weight_grad(left.pop(0))
+
+            for p in range(reduce.last - 1, -1, -1):
+                reduce.level(1, p)
+                some(1)
+            reduce.pass_on()
+            for p in range(reduce.last - 1, -1, -1):
+                reduce.level(0, p)
+                some(1)
+            some(n_mp)
+            reduce.end(r["total"])
+            for number in (blocks - 2, blocks - 1):
+                sum_copy(number).wait()
+            own_gates.wait()
+            for (group, j), device in peers.items():
+                theirs = 1 - kind if group else kind
+                copies.wait(r["gate_parts"].at[device[0], theirs], me, sent[group, j])
+        copies.finish()
+
+    results = pl.pallas_call(
+        kernel,
+        out_shape=tuple(outs.values()),
+        in_specs=list(places.values()),
+        out_specs=tuple(out_places.values()),
+        scratch_shapes=list(scratch.values()),
+        compiler_params=params(identity, 60 << 20),
+        name=f"expert{index}",
+    )(*arrays.values())
+    return dict(zip(outs, results, strict=True))
 
 
 def reduce_weights(n_dp, n_mp, identity, grads, small):
@@ -627,27 +952,20 @@
     down_var,
 ):
     dp, mp = lax.axis_index("dp"), lax.axis_index("mp")
-    half = n_mp // 2
-    kind = mp // half
+    groups = 2 if 2 * n_dp <= 16 else 1
+    kind = mp % groups
     tokens = residual_in.shape[0]
     owned = gateup_w.shape[0]
-    shared = owned // 2
+    shared = owned // groups
     hidden_units = down_w.shape[1]
     flips = [[(i, i ^ k) for i in range(n_mp)] for k in range(n_mp)]
-
-    packed = jnp.concatenate([gateup_w, down_w[:, None]], 1).astype(BF16)
-    mine = jnp.where(kind == 0, packed[:shared], packed[shared:])
-    theirs = jnp.where(kind == 0, packed[shared:], packed[:shared])
-    expert_parts = [mine] + [
-        lax.ppermute(mine if k < half else theirs, "mp", flips[k]) for k in range(1, n_mp)
-    ]
 
     expert_range = jnp.arange(EXPERTS, dtype=jnp.int32)
     onehot = (expert_ids[:, :, None] == expert_range[None, None, :]).astype(jnp.int32)
     onehot_float = onehot.astype(F32)
     chosen = jnp.sum(onehot, 1)
     before = jnp.cumsum(chosen, 0) - chosen
-    place = jnp.where(chosen > 0, before, -1).T
+    place = jnp.where(chosen > 0, before, -1)
 
     own_gain, own_router = attn_gain.shape[0], router_w.shape[0]
     lanes = 128
@@ -660,8 +978,20 @@
     gain_two = small_all[:, :, 1, :own_gain].reshape(-1)
     router_low = small_all[:, :, 8:, :EXPERTS].reshape(MODEL_WIDTH, EXPERTS).astype(BF16)
     query_full, keyval_full, output_turned = projections[0], projections[1], projections[2]
-    cot_low = cotangent.astype(BF16)
-    cot_all, place_all = gather_tokens(n_dp, n_mp, 1, cot_low, place)
+    packed = jnp.concatenate([gateup_w, down_w[:, None]], 1)
+    packed, projections = lax.optimization_barrier((packed, projections))
+    packed = packed.astype(BF16)
+    expert_parts = []
+    for i in range(shared):
+        mine = theirs = packed[groups * i]
+        if groups > 1:
+            mine = jnp.where(kind == 0, packed[2 * i], packed[2 * i + 1])
+            theirs = jnp.where(kind == 0, packed[2 * i + 1], packed[2 * i])
+        expert_parts.append(
+            [mine]
+            + [lax.ppermute(theirs if k % 2 else mine, "mp", flips[k]) for k in range(1, n_mp)]
+        )
+    cot_all = gather_tokens(n_dp, groups, 1, cotangent.astype(BF16))
 
     inv_one = lax.rsqrt(jnp.mean(residual_in * residual_in, -1, keepdims=True) + NORM_EPS)
     normed_one = (residual_in * inv_one * gain_one).astype(BF16)
@@ -706,83 +1036,43 @@
     exp_logits = jnp.exp(logits)
     router_probs = exp_logits / jnp.sum(exp_logits, -1, keepdims=True)
 
-    token_all, probs_all = gather_tokens(n_dp, n_mp, 2, normed_two, router_probs.T)
-    blocks = 2 * n_dp
-    first_expert = dp * owned + kind * shared
-    token_all = token_all.reshape(blocks, tokens, MODEL_WIDTH)
-    cot_all = cot_all.reshape(blocks, tokens, MODEL_WIDTH)
-    own_place = lax.dynamic_slice_in_dim(
-        place_all.reshape(blocks, EXPERTS, tokens), first_expert, shared, 1
-    )
-    own_probs = lax.dynamic_slice_in_dim(
-        probs_all.reshape(blocks, EXPERTS, tokens), first_expert, shared, 1
-    )
-    hit = own_place[:, :, None, :] == jnp.arange(CAP, dtype=jnp.int32)[None, None, :, None]
-    pick = hit.astype(BF16)
-    weight = jnp.sum(jnp.where(hit, own_probs[:, :, None, :], 0.0), -1)
-    weight = weight.transpose(1, 0, 2).reshape(shared, blocks * CAP, 1)
-
-    def slots_of(rows):
-        found = jnp.einsum("best,btd->ebsd", pick, rows, preferred_element_type=F32)
-        return found.astype(BF16).reshape(shared, blocks * CAP, MODEL_WIDTH)
-
-    def sums_of(slots):
-        per_block = slots.reshape(shared, blocks, CAP, MODEL_WIDTH)
-        found = jnp.einsum("best,ebsd->btd", pick, per_block, preferred_element_type=F32)
-        return found.astype(BF16).reshape(2, n_dp, tokens, MODEL_WIDTH)
-
-    received = slots_of(token_all)
-    cot_slots = slots_of(cot_all)
-    experts = jnp.stack(expert_parts, 2)
-    gateup_full = experts[:, :2].reshape(shared, 2, n_mp * hidden_units, MODEL_WIDTH)
-    down_full = experts[:, 2].reshape(shared, n_mp * hidden_units, MODEL_WIDTH)
-    gate_up = jnp.einsum("erd,ecfd->ercf", received, gateup_full, preferred_element_type=F32)
-    gate_val, up_val = gate_up[:, :, 0], gate_up[:, :, 1]
-    sigmoid_val = jax.nn.sigmoid(gate_val)
-    silu_val = gate_val * sigmoid_val
-    activation = (silu_val * up_val).astype(BF16)
-    expert_out = jnp.einsum("erf,efd->erd", activation, down_full, preferred_element_type=F32)
-    gate_dot_slots = jnp.sum(cot_slots.astype(F32) * expert_out, -1)
-    gate_dot_slots = gate_dot_slots.reshape(shared, blocks, CAP).transpose(1, 0, 2)
-    gate_dots = jnp.sum(jnp.where(hit, gate_dot_slots[..., None], 0.0), 2)
-    gate_dots = jnp.pad(gate_dots, ((0, 0), (0, 8 - shared), (0, 0)))
-    gate_dots = gate_dots.reshape(2, n_dp, 8, tokens)
-    mixture_terms = sums_of((weight * expert_out).astype(BF16))
-    mixture, gate_parts = reduce_tokens(n_dp, n_mp, 3, mixture_terms, gate_dots)
+    table = jnp.zeros((n_dp, groups, 8, tokens), F32)
+    by_owner = place.astype(F32).T.reshape(n_dp, shared, groups, tokens).transpose(0, 2, 1, 3)
+    table = table.at[:, :, :shared].set(by_owner)
+    by_owner = router_probs.T.reshape(n_dp, shared, groups, tokens).transpose(0, 2, 1, 3)
+    table = table.at[:, :, 4 : 4 + shared].set(by_owner)
+    made = {"rows": normed_two, "table": table, "cots": cot_all, "tokens": tokens}
+    made |= {"x": {}, "c": {}, "y": {}, "d": {}}
+    expert_grads = []
+    for i in range(shared):
+        found = run_expert(n_dp, n_mp, groups, 2 + i, i, shared, expert_parts[i], made)
+        for name, value in found.items():
+            if name[0] in "xc" and name[1:].isdigit():
+                made[name[0]][int(name[1:])] = value
+            elif name in ("y", "d"):
+                made[name][i] = value
+            elif name in ("tables", "gates"):
+                made[name] = value
+        sent = [found[f"grad{k}"] for k in range(n_mp)]
+        expert_grads.append(
+            sent[:1] + [lax.ppermute(sent[k], "mp", flips[k]) for k in range(1, n_mp)]
+        )
+    grad_normed_two, gate_parts = found["total"], found["gate_parts"]
+    mixture = reduce_tokens(2 + shared, found["terms"])
     block_out = hidden + mixture
-    grad_probs = gate_parts[:, :, :shared].reshape(EXPERTS, tokens).T
-    grad_rows = (weight * cot_slots.astype(F32)).astype(BF16)
-    grad_act = jnp.einsum("erd,efd->erf", grad_rows, down_full, preferred_element_type=F32)
-    grad_down = jnp.einsum("erf,erd->efd", activation, grad_rows, preferred_element_type=F32)
-    grad_gate = grad_act * up_val * sigmoid_val * (1.0 + gate_val * (1.0 - sigmoid_val))
-    grad_up = grad_act * silu_val
-    grad_pair = jnp.stack([grad_gate, grad_up], 2).astype(BF16)
-    grad_slots = jnp.einsum(
-        "ercf,ecfd->erd", grad_pair, gateup_full, preferred_element_type=F32
-    ).astype(BF16)
-    grad_gateup = jnp.einsum("ercf,erd->ecfd", grad_pair, received, preferred_element_type=F32)
-    (grad_normed_two,) = reduce_tokens(n_dp, n_mp, 4, sums_of(grad_slots))
-
-    grad_experts = jnp.concatenate(
-        [
-            grad_gateup.reshape(shared, 2, n_mp, hidden_units, MODEL_WIDTH),
-            grad_down.reshape(shared, 1, n_mp, hidden_units, MODEL_WIDTH),
-        ],
-        1,
-    ).astype(BF16)
-    arrived = [grad_experts[:, :, 0]] + [
-        lax.ppermute(grad_experts[:, :, k], "mp", flips[k]) for k in range(1, n_mp)
-    ]
-    near_sum = sum(part.astype(F32) for part in arrived[:half])
-    far_sum = sum(part.astype(F32) for part in arrived[half:])
-    expert_grad = jnp.where(
-        kind == 0,
-        jnp.concatenate([near_sum, far_sum], 0),
-        jnp.concatenate([far_sum, near_sum], 0),
-    )
+    grad_probs = gate_parts[:, :, :shared].transpose(0, 2, 1, 3).reshape(EXPERTS, tokens).T
+    pairs = []
+    for i in range(shared):
+        if groups == 1:
+            pairs.append(sum(part.astype(F32) for part in expert_grads[i]))
+            continue
+        same = sum(part.astype(F32) for part in expert_grads[i][0::2])
+        turned = sum(part.astype(F32) for part in expert_grads[i][1::2])
+        pairs.append(jnp.where(kind == 0, same, turned))
+        pairs.append(jnp.where(kind == 0, turned, same))
+    expert_grad = jnp.stack(pairs)
     gateup_grad, down_grad = expert_grad[:, :2], expert_grad[:, 2]
 
-    grad_probs = jnp.where(chosen > 0, grad_probs, 0.0)
     grad_logits = (
         router_probs * (grad_probs - jnp.sum(router_probs * grad_probs, -1, keepdims=True))
     ).astype(BF16)
@@ -841,7 +1131,7 @@
     small_grads = small_grads.at[:, :, 8:, :EXPERTS].set(
         grad_router.reshape(n_dp, n_mp, own_router, EXPERTS)
     )
-    grads, small_grads = reduce_weights(n_dp, n_mp, 5, grads, small_grads)
+    grads, small_grads = reduce_weights(n_dp, n_mp, 3 + shared, grads, small_grads)
     query_grad, keyval_grad, output_grad = grads[0], grads[1], grads[2].T
     gain_one_grad, gain_two_grad = small_grads[0, :own_gain], small_grads[1, :own_gain]
     router_grad = small_grads[8:, :EXPERTS]

time: 900 us -> 671 us (0.75)
  matrix products: 120 us -> 43.1 us
  Pallas kernels: 497 us -> 441 us
  local copies, waits for them, and re-layouts: 84.3 us -> 44.3 us
  waiting for transfers between devices: 101 us -> 62.6 us
  other arithmetic: 71 us -> 48.9 us
    pallas_call x1, Pallas kernels: 170 us -> 49.6 us  [gather_weights(): pl.pallas_call(kernel, out_shape=(jax.ShapeDtypeStruct((n_dp, n_mp) + sma...]
    ppermute x1, waiting for transfers between devices: 101 us -> 5.38 us  [local(): grad_kv_other = lax.ppermute(grad_kv[:tokens].astype(BF16), 'mp', flips[1])]
    dot_general x10 -> x0, matrix products: 78.9 us -> none  [the longest x2 16.1 us: slots_of(): found = jnp.einsum('best,btd->ebsd', pick, rows, preferred_element_type=F32)]
    pallas_call x1, Pallas kernels: 56.7 us -> 116 us  [reduce_weights(): pl.pallas_call(kernel, out_shape=(jax.ShapeDtypeStruct((kinds, rows, cols...]
    ppermute x6 -> x12, waiting for transfers between devices: 0.02 us -> 57.3 us  [the longest x6 48.8 us: local(): lax.ppermute(theirs if k % 2 else mine, 'mp', flips[k])]
    unnamed x222 -> x157, local copies, waits for them, and re-layouts: 36.5 us -> 15.5 us
    convert_element_type x2 -> x0, local copies, waits for them, and re-layouts: 15.8 us -> none  [the longest x1 10.2 us: local(): gate_dot_slots = jnp.sum(cot_slots.astype(F32) * expert_out, -1)]
    convert_element_type x3 -> x2, other arithmetic: 12 us -> 0.95 us  [the longest x1 0.87 us: local(): cot_all = gather_tokens(n_dp, groups, 1, cotangent.astype(BF16))]
  transfers between devices with their start and end apart: 8 -> 14, of which waited for: 1 -> 3; matrix products, arithmetic and copies ran while one was open for 13% -> 12% of each run, Pallas kernels for 40% -> 41%
where the time goes in v2:
time: 671 us; the launch traced here: 661 us
  Pallas kernels  441 us (66%)
  waiting for transfers between devices  62.6 us (9%)
  other arithmetic  48.9 us (7%)
  local copies, waits for them, and re-layouts  44.3 us (7%)
  matrix products  43.1 us (6%)
  starting transfers between devices  19.5 us (3%)
    pallas_call x2, Pallas kernels, run_expert(): pl.pallas_call(kernel, out_shape=tuple(outs.values()), in_specs=list(plac...  134 us
    pallas_call x1, Pallas kernels, reduce_weights(): pl.pallas_call(kernel, out_shape=(jax.ShapeDtypeStruct((kinds, rows, cols...  116 us
    pallas_call x1, Pallas kernels, gather_tokens(): pl.pallas_call(kernel, out_shape=jax.ShapeDtypeStruct((groups, n_dp) + ro...  92.3 us
    pallas_call x1, Pallas kernels, gather_weights(): pl.pallas_call(kernel, out_shape=(jax.ShapeDtypeStruct((n_dp, n_mp) + sma...  49.6 us
    pallas_call x1, Pallas kernels, reduce_tokens(): pl.pallas_call(kernel, out_shape=jax.ShapeDtypeStruct((tokens, width), F3...  49.2 us
    ppermute x6, waiting for transfers between devices, local(): lax.ppermute(theirs if k % 2 else mine, 'mp', flips[k])  48.8 us
    unnamed x157, local copies, waits for them, and re-layouts  15.5 us
    sub x6, other arithmetic, adamw(): weight - rate_val * (first_hat / (jnp.sqrt(second_hat) + 1e-08) + decay_v...  14 us
  transfers between devices with their start and end apart: 14, of which 3 were waited for; matrix products, arithmetic and copies ran while one was open for 12% of the time, Pallas kernels for 41%

profile of v2, /device:TPU:0, one launch (start us, length us, event | category | flops | bytes accessed | tf_op | source)
XLA Modules:
  0.0 661.3 jit_solution(9313367665914153494)
XLA Ops:
  6.6 49.6 %gather_weights.1 = (f32[8,4,40,128]{3,2,1,0:T(8,128)}, bf16[3,1024,1024]{2,1,0:T(8,128)(2,1)}) custom-call(f32[40,128]{1,0:T(8,128)} %copy-done.56, bf16[3,128,256]{2,1,0:T(8,128)(2,1)} %pad_maximum_fusion.7.shard_ref), custom_call_target="tpu_custom_call" | custom-call | tf_op jit(solution)/shard_map/gather_weights/pallas_call | solution.py:288
  56.2 3.2 pad_maximum_fusion
  69.0 4.7 slice_bitcast_fusion.1
  83.1 3.9 copy.106
  88.7 92.3 %gather_tokens.1.refs_6_ = bf16[2,8,256,1024]{3,2,1,0:T(8,128)(2,1)} custom-call(bf16[256,1024]{1,0:T(8,128)(2,1)} %convert_element_type.127.rows_ref), custom_call_target="tpu_custom_call" | custom-call | tf_op jit(solution)/shard_map/gather_tokens/pallas_call | solution.py:331
  184.7 3.2 fusion.36
  206.6 48.8 %collective-permute-done.5.refs_2_ = bf16[3,128,1024]{2,1,0:T(8,128)(2,1)} collective-permute-done((bf16[3,128,1024]{2,1,0:T(8,128)(2,1)S(1)}, bf16[3,128,1024]{2,1,0:T(8,128)(2,1)}, u32[]{:S(2)}, u32[]{:S(2)}) %collective-permute-start.5) | collective-permute-done | bytes 786464 | tf_op jit(solution)/shard_map/ppermute | solution.py:992
  255.4 62.4 %expert0.1 = (bf16[3,128,1024]{2,1,0:T(8,128)(2,1)}, bf16[3,128,1024]{2,1,0:T(8,128)(2,1)}, bf16[3,128,1024]{2,1,0:T(8,128)(2,1)}, bf16[3,128,1024]{2,1,0:T(8,12...) custom-call(bf16[3,128,1024]{2,1,0:T(8,128)(2,1)} %get-tuple-element, ...), custom_call_target="tpu_custom_call" | custom-call | tf_op jit(solution)/shard_map/expert0/pallas_call | solution.py:797
  317.8 71.4 %expert1.1 = (bf16[3,128,1024]{2,1,0:T(8,128)(2,1)}, bf16[3,128,1024]{2,1,0:T(8,128)(2,1)}, bf16[3,128,1024]{2,1,0:T(8,128)(2,1)}, bf16[3,128,1024]{2,1,0:T(8,12...) custom-call(bf16[3,128,1024]{2,1,0:T(8,128)(2,1)} %get-tuple-element.322.refs_0_, ...), custom_call_target="tpu_custom_call" | custom-call | tf_op jit(solution)/shard_map/expert1/pallas_call | solution.py:797
  392.1 49.2 %reduce_tokens.1 = f32[256,1024]{1,0:T(8,128)S(1)} custom-call(bf16[2,8,256,1024]{3,2,1,0:T(8,128)(2,1)} %get-tuple-element.161.terms_ref), custom_call_target="tpu_custom_call" | custom-call | tf_op jit(solution)/shard_map/reduce_tokens/pallas_call | solution.py:457
  445.2 5.8 fusion
  461.3 3.3 convert_bitcast_fusion.2
  466.3 3.0 collective-permute-start.13
  470.7 3.1 convert_bitcast_fusion
  476.4 5.4 collective-permute-done.7
  485.7 3.2 convert_bitcast_fusion.1
  488.9 4.0 multiply_reduce_fusion.1
  493.7 3.1 scatter.39.small_ref
  496.9 6.5 pad_maximum_fusion.1.grads_ref
  503.5 115.6 %reduce_weights.1 = (f32[3,128,256]{2,1,0:T(8,128)S(1)}, f32[40,128]{1,0:T(8,128)S(1)}) custom-call(bf16[3,1024,1024]{2,1,0:T(8,128)(2,1)} %pad_maximum_fusion.1.grads_ref, f32[8,4,40,128]{3,2,1,0:T(8,128)S(1)} %scatter.39.small_ref), custom_call_target="tpu_custom_call" | custom-call | tf_op jit(solution)/shard_map/reduce_weights/pallas_call | solution.py:875
  622.4 3.1 collective-permute-start.9
  633.0 8.5 %collective-permute-done.9 = bf16[3,128,1024]{2,1,0:T(8,128)(2,1)} collective-permute-done((bf16[3,128,1024]{2,1,0:T(8,128)(2,1)}, bf16[3,128,1024]{2,1,0:T(8,128)(2,1)}, u32[]{:S(2)}, u32[]{:S(2)}) %collective-permute-start.9) | collective-permute-done | bytes 786464 | tf_op jit(solution)/shard_map/ppermute | solution.py:1058
  646.7 5.0 multiply_subtract_fusion.1
  654.2 6.7 %multiply_subtract_fusion = (f32[4,2,128,1024]{3,2,1,0:T(8,128)}, f32[4,2,128,1024]{3,2,1,0:T(8,128)}, f32[4,2,128,1024]{3,2,1,0:T(8,128)}, f32[4,2,128,1024]{3,2,1,0:T(8,128)}) fusion(f32[4,2,128,1024]{3,2,1,0:T(8,128)S(1)} %copy-done.3, f32[4,2,128,1024]{3,2,1,0:T(8,128)S(1)} %copy-done.14, f32[4,2,128,1024]{3,2,1,0:T(8,128)S(1)} %copy-done.15, ...), kind=kLoop, calls=%fused_computation.19 | loop fusion | flops 15728640 | bytes 33554432 | tf_op jit(solution)/shard_map/sub | solution.py:917
  (269 shorter events, 94.0 us)
Async XLA Ops:
  61.2 256.6 %collective-permute-start.1 = (bf16[3,128,1024]{2,1,0:T(8,128)(2,1)}, bf16[3,128,1024]{2,1,0:T(8,128)(2,1)}, u32[]{:S(2)}, u32[]{:S(2)}) collective-permute-start(bf16[3,128,1024]{2,1,0:T(8,128)(2,1)} %get-tuple-element.320), channel_id=1, source_target_pairs={{0,1},{1,0},{2,3},{3,2},{4,5},{5,4},{6,7},{7,6},{8,9},{9,8},{10,11... | collective-permute-start | bytes 2359304 | tf_op jit(solution)/shard_map/ppermute | solution.py:992
  61.2 256.6 %collective-permute-start.3 = (bf16[3,128,1024]{2,1,0:T(8,128)(2,1)}, bf16[3,128,1024]{2,1,0:T(8,128)(2,1)}, u32[]{:S(2)}, u32[]{:S(2)}) collective-permute-start(bf16[3,128,1024]{2,1,0:T(8,128)(2,1)} %get-tuple-element.320), channel_id=1, source_target_pairs={{0,3},{1,2},{2,1},{3,0},{4,7},{5,6},{6,5},{7,4},{8,11},{9,10},{10,... | collective-permute-start | bytes 2359304 | tf_op jit(solution)/shard_map/ppermute | solution.py:992
  63.3 136.2 %collective-permute-start.4 = (bf16[3,128,1024]{2,1,0:T(8,128)(2,1)}, bf16[3,128,1024]{2,1,0:T(8,128)(2,1)}, u32[]{:S(2)}, u32[]{:S(2)}) collective-permute-start(bf16[3,128,1024]{2,1,0:T(8,128)(2,1)} %get-tuple-element.319), channel_id=1, source_target_pairs={{0,1},{1,0},{2,3},{3,2},{4,5},{5,4},{6,7},{7,6},{8,9},{9,8},{10,11... | collective-permute-start | bytes 2359304 | tf_op jit(solution)/shard_map/ppermute | solution.py:992
  63.3 192.1 %collective-permute-start.6 = (bf16[3,128,1024]{2,1,0:T(8,128)(2,1)}, bf16[3,128,1024]{2,1,0:T(8,128)(2,1)}, u32[]{:S(2)}, u32[]{:S(2)}) collective-permute-start(bf16[3,128,1024]{2,1,0:T(8,128)(2,1)} %get-tuple-element.319), channel_id=1, source_target_pairs={{0,3},{1,2},{2,1},{3,0},{4,7},{5,6},{6,5},{7,4},{8,11},{9,10},{10,... | collective-permute-start | bytes 2359304 | tf_op jit(solution)/shard_map/ppermute | solution.py:992
  69.0 114.7 %collective-permute-start = (bf16[256,1024]{1,0:T(8,128)(2,1)}, bf16[256,1024]{1,0:T(8,128)(2,1)}, u32[]{:S(2)}, u32[]{:S(2)}) collective-permute-start(bf16[256,1024]{1,0:T(8,128)(2,1)} %multiply_convert_fusion.1), channel_id=1, source_target_pairs={{0,1},{1,0},{2,3},{3,2},{4,5},{5,4},{6,7},{7,6},{8,9},{9,8},{10,11... | collective-permute-start | bytes 1572872 | tf_op jit(solution)/shard_map/ppermute | solution.py:998
  183.6 134.1 %collective-permute-start.2 = (bf16[3,128,1024]{2,1,0:T(8,128)(2,1)}, bf16[3,128,1024]{2,1,0:T(8,128)(2,1)}, u32[]{:S(2)}, u32[]{:S(2)}) collective-permute-start(bf16[3,128,1024]{2,1,0:T(8,128)(2,1)} %get-tuple-element.322.refs_0_), channel_id=1, source_target_pairs={{0,2},{1,3},{2,0},{3,1},{4,6},{5,7},{6,4},{7,5},{8,10},{9,11},{10,... | collective-permute-start | bytes 2359304 | tf_op jit(solution)/shard_map/ppermute | solution.py:992
  198.9 191.4 %copy-start.5 = (f32[256,1024]{1,0:T(8,128)}, f32[256,1024]{1,0:T(8,128)S(1)}, u32[]{:S(2)}) copy-start(f32[256,1024]{1,0:T(8,128)S(1)} %get-tuple-element.356) | copy-start | bytes 3145732
  199.5 55.9 %collective-permute-start.5 = (bf16[3,128,1024]{2,1,0:T(8,128)(2,1)S(1)}, bf16[3,128,1024]{2,1,0:T(8,128)(2,1)}, u32[]{:S(2)}, u32[]{:S(2)}) collective-permute-start(bf16[3,128,1024]{2,1,0:T(8,128)(2,1)S(1)} %copy-done.18), channel_id=1, source_target_pairs={{0,2},{1,3},{2,0},{3,1},{4,6},{5,7},{6,4},{7,5},{8,10},{9,11},{10,... | collective-permute-start | bytes 2359304 | tf_op jit(solution)/shard_map/ppermute | solution.py:992
  461.1 20.7 %collective-permute-start.7 = (bf16[256,1024]{0,1:T(8,128)(2,1)}, bf16[256,1024]{0,1:T(8,128)(2,1)}, u32[]{:S(2)}, u32[]{:S(2)}) collective-permute-start(bf16[256,1024]{0,1:T(8,128)(2,1)} %bitcast.56), channel_id=1, source_target_pairs={{0,1},{1,0},{2,3},{3,2},{4,5},{5,4},{6,7},{7,6},{8,9},{9,8},{10,11... | collective-permute-start | bytes 1572872 | tf_op jit(solution)/shard_map/ppermute | solution.py:1112
  464.9 157.4 %collective-permute-start.11 = (bf16[3,128,1024]{2,1,0:T(8,128)(2,1)}, bf16[3,128,1024]{2,1,0:T(8,128)(2,1)}, u32[]{:S(2)}, u32[]{:S(2)}) collective-permute-start(bf16[3,128,1024]{2,1,0:T(8,128)(2,1)} %get-tuple-element.171), channel_id=1, source_target_pairs={{0,2},{1,3},{2,0},{3,1},{4,6},{5,7},{6,4},{7,5},{8,10},{9,11},{10,... | collective-permute-start | bytes 2359304 | tf_op jit(solution)/shard_map/ppermute | solution.py:1058
  466.3 164.3 %collective-permute-start.13 = (bf16[3,128,1024]{2,1,0:T(8,128)(2,1)}, bf16[3,128,1024]{2,1,0:T(8,128)(2,1)}, u32[]{:S(2)}, u32[]{:S(2)}) collective-permute-start(bf16[3,128,1024]{2,1,0:T(8,128)(2,1)} %get-tuple-element.173), channel_id=1, source_target_pairs={{0,3},{1,2},{2,1},{3,0},{4,7},{5,6},{6,5},{7,4},{8,11},{9,10},{10,... | collective-permute-start | bytes 2359304 | tf_op jit(solution)/shard_map/ppermute | solution.py:1058
  469.4 161.3 %collective-permute-start.12 = (bf16[3,128,1024]{2,1,0:T(8,128)(2,1)}, bf16[3,128,1024]{2,1,0:T(8,128)(2,1)}, u32[]{:S(2)}, u32[]{:S(2)}) collective-permute-start(bf16[3,128,1024]{2,1,0:T(8,128)(2,1)} %get-tuple-element.172), channel_id=1, source_target_pairs={{0,1},{1,0},{2,3},{3,2},{4,5},{5,4},{6,7},{7,6},{8,9},{9,8},{10,11... | collective-permute-start | bytes 2359304 | tf_op jit(solution)/shard_map/ppermute | solution.py:1058
  469.4 163.6 %collective-permute-start.8 = (bf16[3,128,1024]{2,1,0:T(8,128)(2,1)}, bf16[3,128,1024]{2,1,0:T(8,128)(2,1)}, u32[]{:S(2)}, u32[]{:S(2)}) collective-permute-start(bf16[3,128,1024]{2,1,0:T(8,128)(2,1)} %get-tuple-element.167), channel_id=1, source_target_pairs={{0,2},{1,3},{2,0},{3,1},{4,6},{5,7},{6,4},{7,5},{8,10},{9,11},{10,... | collective-permute-start | bytes 2359304 | tf_op jit(solution)/shard_map/ppermute | solution.py:1058
  481.8 151.3 %collective-permute-start.10 = (bf16[3,128,1024]{2,1,0:T(8,128)(2,1)}, bf16[3,128,1024]{2,1,0:T(8,128)(2,1)}, u32[]{:S(2)}, u32[]{:S(2)}) collective-permute-start(bf16[3,128,1024]{2,1,0:T(8,128)(2,1)} %get-tuple-element.169), channel_id=1, source_target_pairs={{0,3},{1,2},{2,1},{3,0},{4,7},{5,6},{6,5},{7,4},{8,11},{9,10},{10,... | collective-permute-start | bytes 2359304 | tf_op jit(solution)/shard_map/ppermute | solution.py:1058
  503.4 116.6 %copy-start.40 = (f32[128,256]{1,0:T(8,128)S(1)}, f32[128,256]{1,0:T(8,128)}, u32[]{:S(2)}) copy-start(f32[128,256]{1,0:T(8,128)} %param.48) | copy-start | bytes 393220
  503.5 117.7 %copy-start.66 = (f32[32]{0:T(128)S(1)}, f32[32]{0:T(128)}, u32[]{:S(2)}) copy-start(f32[32]{0:T(128)} %param.46) | copy-start | bytes 388
  503.5 117.7 %copy-start.67 = (f32[32]{0:T(128)S(1)}, f32[32]{0:T(128)}, u32[]{:S(2)}) copy-start(f32[32]{0:T(128)} %param.50) | copy-start | bytes 388
  503.5 117.6 %copy-start.69 = (f32[32]{0:T(128)S(1)}, f32[32]{0:T(128)}, u32[]{:S(2)}) copy-start(f32[32]{0:T(128)} %param.62) | copy-start | bytes 388
  503.5 117.6 %copy-start.70 = (f32[32]{0:T(128)S(1)}, f32[32]{0:T(128)}, u32[]{:S(2)}) copy-start(f32[32]{0:T(128)} %param.63) | copy-start | bytes 388
  503.5 117.6 %copy-start.71 = (f32[32]{0:T(128)S(1)}, f32[32]{0:T(128)}, u32[]{:S(2)}) copy-start(f32[32]{0:T(128)} %param.55) | copy-start | bytes 388
  503.5 117.6 %copy-start.72 = (f32[32]{0:T(128)S(1)}, f32[32]{0:T(128)}, u32[]{:S(2)}) copy-start(f32[32]{0:T(128)} %param.54) | copy-start | bytes 388
  503.5 121.9 %copy-start.68 = (f32[256]{0:T(256)S(1)}, f32[256]{0:T(256)}, u32[]{:S(2)}) copy-start(f32[256]{0:T(256)} %get-tuple-element.279) | copy-start | bytes 3076
  503.5 125.9 %copy-start.64 = (f32[256]{0:T(256)S(1)}, f32[256]{0:T(256)}, u32[]{:S(2)}) copy-start(f32[256]{0:T(256)} %get-tuple-element.349) | copy-start | bytes 3076
  622.4 19.1 %collective-permute-start.9 = (bf16[3,128,1024]{2,1,0:T(8,128)(2,1)}, bf16[3,128,1024]{2,1,0:T(8,128)(2,1)}, u32[]{:S(2)}, u32[]{:S(2)}) collective-permute-start(bf16[3,128,1024]{2,1,0:T(8,128)(2,1)} %get-tuple-element.168), channel_id=1, source_target_pairs={{0,1},{1,0},{2,3},{3,2},{4,5},{5,4},{6,7},{7,6},{8,9},{9,8},{10,11... | collective-permute-start | bytes 2359304 | tf_op jit(solution)/shard_map/ppermute | solution.py:1058
  (65 other events, 2292.1 us)

commit v3 on v2

v3 whole, which is shorter than its diff:
```python
import functools
import math
import types

import jax
import jax.numpy as jnp
import numpy as np
from jax import lax
from jax.experimental import pallas as pl
from jax.experimental.pallas import tpu as pltpu
from jax.sharding import PartitionSpec as P

MODEL_WIDTH = 1024
QUERY_HEADS = 16
KEY_VALUE_HEADS = 8
HEAD_SIZE = 64
EXPERTS = 32
TOPK = 8
SEQUENCE_TOKENS = 512
STEP = 3
CAP = 80

NORM_EPS = 1e-06
MESH = pl.DeviceIdType.MESH
BF16 = jnp.bfloat16
F32 = jnp.float32


def flip(index, mask):
    return index + mask * (1 - 2 * lax.rem(lax.div(index, mask), 2))


def flip_all(index, masks):
    bit = 1
    while bit <= masks:
        if masks & bit:
            index = flip(index, bit)
        bit *= 2
    return index


def bits_of(size):
    return [1 << i for i in range(size.bit_length() - 1)]


def orders_of(n_dp):
    bits = bits_of(n_dp)
    return bits[1:] + bits[:1], bits[1:][::-1] + bits[:1]


def place_of(order, j):
    place = -1
    for at, mask in enumerate(order):
        if j & mask:
            place = at
    return place


def greet(partners):
    barrier = pltpu.get_barrier_semaphore()
    for partner in partners:
        pl.semaphore_signal(barrier, inc=1, device_id=partner, device_id_type=MESH)
    pl.semaphore_wait(barrier, len(partners))


class Copies:
    def __init__(self, send_sems, recv_sems):
        self.send_sems, self.recv_sems = send_sems, recv_sems
        self.used = 0
        self.sent = []

    def slot(self):
        self.used += 1
        return self.used - 1

    def make(self, source, target, device, slot):
        return pltpu.make_async_remote_copy(
            src_ref=source,
            dst_ref=target,
            send_sem=self.send_sems.at[slot],
            recv_sem=self.recv_sems.at[slot],
            device_id=device,
            device_id_type=MESH,
        )

    def start(self, source, target, device, slot):
        copy = self.make(source, target, device, slot)
        copy.start()
        self.sent.append(copy)

    def wait(self, target, device, slot):
        self.make(target, target, device, slot).wait_recv()

    def finish(self):
        for copy in self.sent:
            copy.wait_send()


class TreeGather:
    def __init__(self, copies, order, n_dp, me, source, target):
        self.copies, self.order, self.n_dp, self.me = copies, order, n_dp, me
        self.source, self.target = source, target
        self.slots = {j: copies.slot() for j in range(1, n_dp)}

    def level(self, j):
        return bin(j).count("1")

    def send(self, j):
        dp, mp = self.me
        for mask in self.order[place_of(self.order, j) + 1 :]:
            self.copies.start(
                self.source(j), self.target(j, mask), (flip(dp, mask), mp), self.slots[j ^ mask]
            )

    def receive(self, j):
        self.copies.wait(self.source(j), self.me, self.slots[j])

    def steps(self):
        return sorted(range(1, self.n_dp), key=lambda j: (self.level(j), place_of(self.order, j)))


def run_gathers(trees):
    n_dp = trees[0].n_dp
    for level in range(1, n_dp.bit_length()):
        for tree in trees:
            for j in tree.steps():
                if tree.level(j) == level:
                    tree.receive(j)
                    tree.send(j)


class TreeReduce:
    def __init__(self, copies, order, n_dp, me, block, room, add):
        self.copies, self.order, self.n_dp, self.me = copies, order, n_dp, me
        self.block, self.room, self.add = block, room, add
        self.keys = [
            (j, q) for j in range(n_dp) for q in range(len(order) - 1, place_of(order, j), -1)
        ]
        self.slots = {key: copies.slot() for key in self.keys}

    def number(self, key):
        return self.keys.index(key)

    def send(self, j):
        dp, mp = self.me
        p = place_of(self.order, j)
        last = len(self.order) - 1
        source = self.block(j) if p == last else self.room(self.number((j, last)))
        mask = self.order[p]
        key = (j ^ mask, p)
        self.copies.start(source, self.room(self.number(key)), (flip(dp, mask), mp), self.slots[key])

    def collect(self, j):
        last = len(self.order) - 1
        for q in range(last, place_of(self.order, j), -1):
            here = self.room(self.number((j, q)))
            self.copies.wait(here, self.me, self.slots[(j, q)])
            if q == last:
                self.add(here, self.block(j))
            else:
                self.add(self.room(self.number((j, last))), here)

    def total(self):
        return self.room(self.number((0, len(self.order) - 1)))


def add_rows(step=16):
    def add(here, other):
        def body(i, carry):
            rows = pl.ds(pl.multiple_of(i * step, step), step)
            total = here[..., rows, :].astype(F32) + other[..., rows, :].astype(F32)
            here[..., rows, :] = total.astype(here.dtype)
            return carry

        lax.fori_loop(0, here.shape[-2] // step, body, 0)

    return add


def hbm():
    return pl.BlockSpec(memory_space=pl.ANY)


def vmem():
    return pl.BlockSpec(memory_space=pltpu.VMEM)


def params(identity, limit=None):
    return pltpu.CompilerParams(
        collective_id=identity, has_side_effects=True, vmem_limit_bytes=limit
    )


def launch(kernel, identity, ins, outs, scratch, n_copies, limit=None):
    def flat(entries):
        names, leaves, specs = [], [], []
        for name, (value, spec) in entries.items():
            several = isinstance(value, list)
            new = value if several else [value]
            names.append((name, len(new) if several else None))
            leaves += new
            specs += [spec] * len(new)
        return names, leaves, specs

    def unflat(names, leaves):
        leaves, found = list(leaves), {}
        for name, count in names:
            found[name] = leaves[0] if count is None else leaves[:count]
            leaves = leaves[1 if count is None else count :]
        return found

    scratch = scratch | dict(
        send_sems=pltpu.SemaphoreType.DMA((n_copies,)),
        recv_sems=pltpu.SemaphoreType.DMA((n_copies,)),
    )
    in_names, values, in_specs = flat(ins)
    out_names, shapes, out_specs = flat(outs)
    scratch_names = [(name, None) for name in scratch]

    def body(*refs):
        named = unflat(in_names + out_names + scratch_names, refs)
        kernel(types.SimpleNamespace(**named))

    results = pl.pallas_call(
        body,
        out_shape=tuple(shapes),
        in_specs=in_specs,
        out_specs=tuple(out_specs),
        scratch_shapes=list(scratch.values()),
        compiler_params=params(identity, limit),
        cost_estimate=pl.CostEstimate(flops=1, bytes_accessed=1, transcendentals=0),
        name=kernel.__name__,
    )(*values)
    return types.SimpleNamespace(**unflat(out_names, results))


def low(*shape):
    return jax.ShapeDtypeStruct(shape, BF16)


def single(*shape):
    return jax.ShapeDtypeStruct(shape, F32)


def dot(a, b, contract):
    return lax.dot_general(a, b, ((contract[:1], contract[1:]), ((), ())), preferred_element_type=F32)


NN, NT, TN = (1, 0), (1, 1), (0, 0)


def gain_rows(small_all, row):
    n_devices = math.prod(small_all.shape[:2])
    n_tiles = MODEL_WIDTH // 128
    per_tile = n_devices // n_tiles
    n_mp = small_all.shape[1]
    tiles = []
    for tile in range(n_tiles):
        total = None
        for device in range(tile * per_tile, (tile + 1) * per_tile):
            part = small_all[device // n_mp, device % n_mp, row : row + 1, :]
            total = part if total is None else total + part
        tiles.append(total)
    return tiles


def prologue(n_dp, n_mp, groups, identity, small, shards, cot, residual):
    half = n_mp // 2
    kinds, rows, cols = shards.shape
    tokens, width = cot.shape
    order_a, order_b = orders_of(n_dp)
    n_copies = 2 * (n_mp - 1) + 4 * (n_dp - 1) + 1

    def gather_line(r):
        dp, mp = lax.axis_index("dp"), lax.axis_index("mp")
        me = (dp, mp)
        neighbour = (dp, flip(mp, 1))
        copies = Copies(r.send_sems, r.recv_sems)
        own_small = r.small_all.at[dp, mp]
        own_cols = pl.ds(pl.multiple_of(mp * cols, cols), cols)
        own_part = r.row_block.at[:, :, own_cols]
        r.small_all[dp, mp] = r.small[...]
        r.row_block[:, :, own_cols] = r.shards[...]
        r.cots[0] = r.cot[...]
        greet(
            [(flip_all(dp, mask), mp) for mask in bits_of(n_dp)]
            + [(dp, flip_all(mp, k)) for k in range(1, n_mp)]
        )
        near = lax.div(mp, half)
        line = {}
        for k in range(1, n_mp):
            line[k] = (copies.slot(), copies.slot())
            copies.start(r.small, own_small, (dp, flip_all(mp, k)), line[k][0])
        for k in range(1, n_mp):
            copies.start(r.shards, own_part, (dp, flip_all(mp, k)), line[k][1])
        across = copies.slot()

        def small_tree(chunk):
            first = pl.multiple_of(chunk * half, half)

            def ref(j, mask=0):
                return r.small_all.at[flip_all(dp, j), pl.ds(first, half)]

            return TreeGather(copies, order_a, n_dp, me, ref, ref)

        small_trees = [small_tree(chunk) for chunk in (near, 1 - near)]
        cot_trees = row_trees(copies, n_dp, me, r.cots)
        for chunk in (0, 1):
            for k in range(1, half) if chunk == 0 else range(half, n_mp):
                copies.wait(r.small_all.at[dp, flip_all(mp, k)], me, line[k][0])
            small_trees[chunk].send(0)
        for one in cot_trees:
            one.send(0)
        top = n_dp.bit_length() - 1
        for level in range(1, top + 1):
            run_level(small_trees, level)
            if level < top:
                run_level(cot_trees, level)
        residual_rows = r.residual[...]
        inverse = lax.rsqrt(jnp.mean(residual_rows * residual_rows, -1, keepdims=True) + NORM_EPS)
        for number, gain in enumerate(gain_rows(r.small_all, 0)):
            lanes = slice(number * 128, (number + 1) * 128)
            r.normed[0, :, lanes] = (residual_rows[:, lanes] * inverse * gain).astype(BF16)
        copies.start(r.normed.at[0], r.normed.at[1], neighbour, across)
        run_level(cot_trees, top)
        for k in range(1, n_mp):
            other = pl.multiple_of(flip_all(mp, k) * cols, cols)
            copies.wait(r.row_block.at[:, :, pl.ds(other, cols)], me, line[k][1])
        copies.wait(r.normed.at[1], me, across)
        copies.finish()

    return launch(
        gather_line,
        identity,
        dict(
            small=(small, vmem()), shards=(shards, vmem()), cot=(cot, vmem()), residual=(residual, vmem())
        ),
        dict(
            small_all=(single(n_dp, n_mp, *small.shape), vmem()),
            row_block=(low(kinds, rows, n_mp * cols), vmem()),
            cots=(low(n_dp, tokens, width), vmem()),
            normed=(low(2, tokens, width), vmem()),
        ),
        {},
        n_copies,
        32 << 20,
    )


def run_level(trees, level):
    for one in trees:
        for j in one.steps():
            if one.level(j) == level:
                one.receive(j)
                one.send(j)


def gather_rows(n_dp, groups, identity, row_block, cot):
    kinds, rows, width = row_block.shape
    part_rows = rows // 2

    def gather_weights(r):
        dp, mp = lax.axis_index("dp"), lax.axis_index("mp")
        me = (dp, mp)
        copies = Copies(r.send_sems, r.recv_sems)
        neighbour = (dp, flip(mp, 1))
        r.full[:, pl.ds(pl.multiple_of(dp * rows, rows), rows), :] = r.row_block[...]
        greet([(flip_all(dp, mask), mp) for mask in bits_of(n_dp)] + [neighbour] * (groups - 1))
        across = copies.slot()
        if groups > 1:
            copies.start(r.cot, r.cot_other, neighbour, across)

        def tree(part, order):
            def ref(j, mask=0):
                start = flip_all(dp, j) * rows + part * part_rows
                return r.full.at[:, pl.ds(pl.multiple_of(start, part_rows), part_rows), :]

            return TreeGather(copies, order, n_dp, me, ref, ref)

        trees = [tree(part, order) for part, order in enumerate(orders_of(n_dp))]
        for one in trees:
            one.send(0)
        run_gathers(trees)
        if groups > 1:
            copies.wait(r.cot_other, me, across)
        copies.finish()

    return launch(
        gather_weights,
        identity,
        dict(row_block=(row_block, vmem()), cot=(cot, vmem())),
        dict(full=(low(kinds, n_dp * rows, width), vmem()), cot_other=(low(*cot.shape), vmem())),
        {},
        2 * (n_dp - 1) + 1,
        32 << 20,
    )


def row_trees(copies, n_dp, me, rows_all):
    tokens = rows_all.shape[1]

    def tree(part, order):
        cut = pl.ds(part * (tokens // 2), tokens // 2)
        return TreeGather(
            copies,
            order,
            n_dp,
            me,
            lambda j: rows_all.at[j, cut],
            lambda j, mask: rows_all.at[j ^ mask, cut],
        )

    return [tree(part, order) for part, order in enumerate(orders_of(n_dp))]


def rotary_constants():
    half_width = HEAD_SIZE // 2
    frequency = np.exp(
        np.float32(-math.log(10000.0)) * np.arange(half_width, dtype=np.float32) * np.float32(2.0)
        / np.float32(HEAD_SIZE)
    ).astype(np.float32)
    angles = np.arange(SEQUENCE_TOKENS, dtype=np.float32)[:, None] * frequency[None, :]
    cosine, sine = np.cos(angles), np.sin(angles)
    cosine = np.concatenate([cosine, cosine], 1)
    sine = np.concatenate([-sine, sine], 1)
    queries = np.stack([np.tile(cosine, (1, 2)), np.tile(sine, (1, 2))])
    keys = np.stack(
        [
            np.concatenate([cosine, np.ones_like(cosine)], 1),
            np.concatenate([sine, np.zeros_like(sine)], 1),
        ]
    )
    return queries.astype(np.float32), keys.astype(np.float32)


def rotate(value, cosine, sine):
    lane = lax.broadcasted_iota(jnp.int32, value.shape, 1)
    rolled = jnp.where(
        lane % HEAD_SIZE < HEAD_SIZE // 2,
        pltpu.roll(value, 128 - HEAD_SIZE // 2, 1),
        pltpu.roll(value, HEAD_SIZE // 2, 1),
    )
    return value * cosine + rolled * sine


def group_operands(queries, keyval):
    lane = lax.broadcasted_iota(jnp.int32, queries.shape, 1)
    both = jnp.concatenate(
        [jnp.where(lane < HEAD_SIZE, queries, 0.0), jnp.where(lane < HEAD_SIZE, 0.0, queries)], 0
    ).astype(BF16)
    lane = lax.broadcasted_iota(jnp.int32, keyval.shape, 1)
    turned = pltpu.roll(keyval, HEAD_SIZE, 1)
    keys = jnp.where(lane < HEAD_SIZE, keyval, turned).astype(BF16)
    values = jnp.where(lane < HEAD_SIZE, turned, keyval).astype(BF16)
    return both, keys, values


def merge_heads(both):
    tokens = both.shape[0] // 2
    lane = lax.broadcasted_iota(jnp.int32, (tokens, 128), 1)
    return jnp.where(lane < HEAD_SIZE, both[:tokens], both[tokens:])


def seen(tokens, mp):
    shape = (2 * tokens, 2 * tokens)
    row = lax.broadcasted_iota(jnp.int32, shape, 0) % tokens
    key = lax.broadcasted_iota(jnp.int32, shape, 1)
    shift = tokens - 2 * tokens * lax.rem(mp, 2)
    key = jnp.where(key < tokens, key, key - tokens + shift)
    return key <= row


def softmax_of(both, keys, mask):
    scores = dot(both, keys, NT) * (1.0 / math.sqrt(HEAD_SIZE))
    raised = jnp.exp(jnp.where(mask, scores, -1e30))
    return raised / jnp.sum(raised, -1, keepdims=True)


def attention_forward(
    n_dp, groups, shared, identity, residual, normed, full, gain_two, router, places, cot_other, rotary
):
    tokens, width = residual.shape
    query_rotary, own_rotary, other_rotary = rotary
    n_heads = width // 128
    n_copies = 2 * (n_dp - 1)

    def attention(r):
        dp, mp = lax.axis_index("dp"), lax.axis_index("mp")
        me = (dp, mp)
        copies = Copies(r.send_sems, r.recv_sems)
        loads = [
            pltpu.make_async_copy(r.full.at[c], r.weights.at[c], r.local_sems.at[c])
            for c in range(3)
        ]
        for copy in loads:
            copy.start()
        r.cots[0] = r.cot_other[...]
        greet([(flip_all(dp, mask), mp) for mask in bits_of(n_dp)])
        trees = row_trees(copies, n_dp, me, r.cots) if groups > 1 else []
        for one in trees:
            one.send(0)
        top = n_dp.bit_length() - 1
        loads[0].wait()
        r.q[...] = dot(r.normed[0], r.weights[0], NN)
        loads[1].wait()
        for part in (0, 1):
            r.kv[part] = dot(r.normed[part], r.weights[1], NN)
        run_level(trees, 1)
        mask = seen(tokens, mp)

        def head(k, carry):
            lanes = pl.ds(pl.multiple_of(k * 128, 128), 128)
            queries = rotate(r.q[:, lanes], r.query_rotary[0], r.query_rotary[1])
            r.queries[:, lanes] = queries.astype(BF16)
            parts = []
            for part, table in enumerate((r.own_rotary, r.other_rotary)):
                parts.append(rotate(r.kv[part, :, lanes], table[0], table[1]))
                r.keyval[part, :, lanes] = parts[part].astype(BF16)
            both, keys, values = group_operands(queries, jnp.concatenate(parts, 0))
            chance = softmax_of(both, keys, mask).astype(BF16)
            r.context[:, lanes] = merge_heads(dot(chance, values, NN)).astype(BF16)
            return carry

        for level in range(2, top + 1):
            first, end = [(level - 2 + i) * n_heads // (top - 1) for i in (0, 1)]
            lax.fori_loop(first, end, head, 0)
            run_level(trees, level)
        loads[2].wait()
        hidden = r.residual[...] + dot(r.context[...], r.weights[2], NT)
        r.hidden[...] = hidden
        inverse = lax.rsqrt(jnp.mean(hidden * hidden, -1, keepdims=True) + NORM_EPS)
        normed = (hidden * inverse * r.gain_two[...]).astype(BF16)
        r.normed_two[...] = normed
        logits = dot(normed, r.router[...], NN)
        lane = lax.broadcasted_iota(jnp.int32, logits.shape, 1)
        raised = jnp.where(lane < EXPERTS, jnp.exp(logits), 0.0)
        probs = raised / jnp.sum(raised, -1, keepdims=True)
        r.probs[...] = probs
        turned = probs.T
        r.table[...] = r.places[...]
        for expert in range(EXPERTS):
            owner, which = divmod(expert, groups * shared)
            r.table[owner, which % groups, 4 + which // groups, :] = turned[expert]
        copies.finish()

    return launch(
        attention,
        identity,
        dict(
            residual=(residual, vmem()),
            normed=(normed, vmem()),
            full=(full, hbm()),
            gain_two=(gain_two, vmem()),
            router=(router, vmem()),
            places=(places, vmem()),
            cot_other=(cot_other, vmem()),
            query_rotary=(query_rotary, vmem()),
            own_rotary=(own_rotary, vmem()),
            other_rotary=(other_rotary, vmem()),
        ),
        dict(
            cots=(low(n_dp, tokens, width), vmem()),
            queries=(low(tokens, width), vmem()),
            keyval=(low(2, tokens, width), vmem()),
            context=(low(tokens, width), vmem()),
            hidden=(single(tokens, width), vmem()),
            normed_two=(low(tokens, width), vmem()),
            probs=(single(tokens, 128), vmem()),
            table=(single(*places.shape), vmem()),
        ),
        dict(
            weights=pltpu.VMEM((3, width, width), BF16),
            q=pltpu.VMEM((tokens, width), F32),
            kv=pltpu.VMEM((2, tokens, width), F32),
            local_sems=pltpu.SemaphoreType.DMA((3,)),
        ),
        n_copies,
        48 << 20,
    )


def attention_backward(n_dp, n_mp, groups, shared, identity, given, first_row):
    tokens, width = given.residual.shape
    n_heads = width // 128
    n_devices = n_dp * n_mp
    own_router = width // n_devices
    per_tile = n_devices // n_heads
    rows, cols = width // n_dp, width // n_mp
    part_rows = rows // 2
    orders = orders_of(n_dp)
    n_copies = (2 * groups + 7) * (n_dp - 1) + 1 + 5 * (n_mp - 1) + 1

    rooms, across_room = reduce_rooms(groups, n_dp, tokens, width, BF16)

    def attention_back(r):
        dp, mp = lax.axis_index("dp"), lax.axis_index("mp")
        me = (dp, mp)
        neighbour = (dp, flip(mp, 1))
        copies = Copies(r.send_sems, r.recv_sems)
        loads = [
            pltpu.make_async_copy(r.full.at[c], r.weights.at[c], r.local_sems.at[c])
            for c in (2, 0, 1)
        ]
        for copy in loads:
            copy.start()
        greet(
            [(flip_all(dp, mask), mp) for mask in bits_of(n_dp)]
            + [(dp, flip_all(mp, k)) for k in range(1, n_mp)]
        )
        mixture = TokenReduce(copies, n_dp, me, r.terms, r.rooms, r.across)
        for group in range(groups)[::-1]:
            for j in range(1, n_dp, 2):
                mixture.first(group, j)
        last = mixture.last
        travels = {k: copies.slot() for k in range(1, n_mp)}

        def send_expert(k):
            copies.start(
                r.expert_grads[k - 1], r.arrived[k - 1], (dp, flip_all(mp, k)), travels[k]
            )

        for k in range(2, n_mp):
            send_expert(k)
        r.turned[...] = jnp.zeros_like(r.turned)
        for expert in range(EXPERTS):
            owner, which = divmod(expert, groups * shared)
            r.turned[expert, :] = r.gate_parts[owner, which % groups, which // groups, :]
        grad_probs = r.turned[...].T
        probs = r.probs[...]
        grad_logits = (
            probs * (grad_probs - jnp.sum(probs * grad_probs, -1, keepdims=True))
        ).astype(BF16)
        grad_normed_two = r.total[...] + dot(grad_logits, r.router[...], NT)
        r.grad_router[...] = dot(r.normed_two[...], grad_logits, TN)
        hidden = r.hidden[...]
        inverse = lax.rsqrt(jnp.mean(hidden * hidden, -1, keepdims=True) + NORM_EPS)
        scaled = r.gain_two[...] * grad_normed_two
        grad_hidden = (
            r.cotangent[...]
            + inverse * scaled
            - hidden * (inverse * inverse * inverse) * jnp.mean(scaled * hidden, -1, keepdims=True)
        )
        r.grad_hidden[...] = grad_hidden
        gain_two = jnp.sum(grad_normed_two * hidden * inverse, 0, keepdims=True)
        grad_attn = grad_hidden.astype(BF16)
        r.grad_attn[...] = grad_attn
        def weight_tree(c, part):
            def block(j):
                start = flip_all(dp, j) * rows + part * part_rows
                return r.grads.at[c, pl.ds(pl.multiple_of(start, part_rows), part_rows), :]

            return TreeReduce(
                copies,
                orders[part],
                n_dp,
                me,
                block,
                lambda number: r.weight_rooms.at[c, part, number],
                add_rows(),
            )

        weight_trees = [[weight_tree(c, part) for part in (0, 1)] for c in range(3)]

        def weight_level(c, p):
            for j in range(1, n_dp):
                for one in weight_trees[c]:
                    if place_of(one.order, j) == p:
                        if p < last:
                            one.collect(j)
                        one.send(j)

        r.grads[2] = dot(grad_attn, r.context[...], TN).astype(BF16)
        weight_level(2, last)
        mixture.level(1, last - 1)
        loads[0].wait()
        r.grad_context[...] = dot(r.grad_attn[...], r.weights[2], NN).astype(BF16)
        mask = seen(tokens, mp)

        def head(k, carry):
            lanes = pl.ds(pl.multiple_of(k * 128, 128), 128)
            keyval = jnp.concatenate([r.keyval[0, :, lanes], r.keyval[1, :, lanes]], 0)
            both, keys, values = group_operands(r.queries[:, lanes].astype(F32), keyval.astype(F32))
            grad_both = group_operands(r.grad_context[:, lanes].astype(F32), keyval.astype(F32))[0]
            chance = softmax_of(both, keys, mask)
            grad_p = dot(grad_both, values, NT)
            delta = jnp.sum(chance * grad_p, -1, keepdims=True)
            grad_s = (chance * (grad_p - delta)).astype(BF16)
            scale = 1.0 / math.sqrt(HEAD_SIZE)
            grad_q = merge_heads(dot(grad_s, keys, NN)) * scale
            r.grad_q[:, lanes] = rotate(grad_q, r.query_rotary[0], -r.query_rotary[1]).astype(BF16)
            grad_k = dot(grad_s, both, TN) * scale
            grad_v = dot(chance.astype(BF16), grad_both, TN)
            lane = lax.broadcasted_iota(jnp.int32, grad_k.shape, 1)
            grad_kv = jnp.where(
                lane < HEAD_SIZE,
                grad_k + pltpu.roll(grad_k, HEAD_SIZE, 1),
                grad_v + pltpu.roll(grad_v, HEAD_SIZE, 1),
            )
            r.grad_kv[:, lanes] = grad_kv[:tokens]
            r.swap[0, :, lanes] = grad_kv[tokens:].astype(BF16)
            return carry

        sent = {}

        def line_out(c):
            for part, one in enumerate(weight_trees[c]):
                one.collect(0)
                total = one.total()
                for k in range(n_mp):
                    there = pl.ds(pl.multiple_of(flip_all(mp, k) * cols, cols), cols)
                    r.line[0, c, k, pl.ds(part * part_rows, part_rows), :] = total[:, there]
            for k in range(1, n_mp):
                sent[c, k] = copies.slot()
                copies.start(
                    r.line.at[0, c, k], r.line.at[1, c, k], (dp, flip_all(mp, k)), sent[c, k]
                )

        stages = []
        for p in range(last - 2, -1, -1):
            stages.append([lambda p=p: mixture.level(1, p)])
        stages.append([lambda: weight_level(2, last - 1), mixture.pass_on])
        for p in range(last - 1, -1, -1):
            stages.append([lambda p=p: mixture.level(0, p)])
            if p < last - 1:
                stages[-1].append(lambda p=p: weight_level(2, p))
        loops = min(len(stages), n_heads)
        for step in range(loops):
            lax.fori_loop(step * n_heads // loops, (step + 1) * n_heads // loops, head, 0)
            if step == loops - 1:
                across = copies.slot()
                copies.start(r.swap.at[0], r.swap.at[1], neighbour, across)
                send_expert(1)
            for stage in stages.pop(0):
                stage()
        for stage in sum(stages, []):
            stage()
        r.grads[0] = dot(r.normed[0], r.grad_q[...], TN).astype(BF16)
        weight_level(0, last)
        loads[1].wait()
        r.grad_normed[...] = dot(r.grad_q[...], r.weights[0], NT)
        weight_level(0, last - 1)
        line_out(2)
        copies.wait(r.swap.at[1], me, across)

        def turn_back(k, carry):
            lanes = pl.ds(pl.multiple_of(k * 128, 128), 128)
            total = r.grad_kv[:, lanes] + r.swap[1, :, lanes].astype(F32)
            total = rotate(total, r.own_rotary[0], -r.own_rotary[1])
            r.grad_kv_low[:, lanes] = total.astype(BF16)
            return carry

        lax.fori_loop(0, n_heads, turn_back, 0)
        loads[2].wait()
        r.grads[1] = dot(r.normed[0], r.grad_kv_low[...], TN).astype(BF16)
        weight_level(1, last)
        grad_normed = r.grad_normed[...] + dot(r.grad_kv_low[...], r.weights[1], NT)
        residual = r.residual[...]
        inverse = lax.rsqrt(jnp.mean(residual * residual, -1, keepdims=True) + NORM_EPS)
        scaled = r.gain_one[...] * grad_normed
        r.input_grad[...] = (
            r.grad_hidden[...]
            + inverse * scaled
            - residual * (inverse * inverse * inverse) * jnp.mean(scaled * residual, -1, keepdims=True)
        )
        gain_one = jnp.sum(grad_normed * residual * inverse, 0, keepdims=True)
        r.small[...] = jnp.zeros_like(r.small)
        for device in range(n_devices):
            tile = device // per_tile
            owner = r.small.at[device // n_mp, device % n_mp]
            owner[0:1, :] = gain_one[:, tile * 128 : (tile + 1) * 128]
            owner[1:2, :] = gain_two[:, tile * 128 : (tile + 1) * 128]
            owner[first_row : first_row + own_router, :] = r.grad_router[
                device * own_router : (device + 1) * own_router, :
            ]

        def add_whole(here, other):
            here[...] = here[...] + other[...]

        small_tree = TreeReduce(
            copies,
            orders[0],
            n_dp,
            me,
            lambda j: r.small.at[flip_all(dp, j)],
            lambda number: r.small_rooms.at[number],
            add_whole,
        )
        for j in range(1, n_dp):
            if place_of(orders[0], j) == last:
                small_tree.send(j)
        for p in range(last - 1, -1, -1):
            if p < last - 1:
                weight_level(0, p)
            weight_level(1, p)
            for j in range(1, n_dp):
                if place_of(orders[0], j) == p:
                    small_tree.collect(j)
                    small_tree.send(j)
        for c in (0, 1):
            line_out(c)
        small_tree.collect(0)
        small_total = small_tree.total()
        for k in range(1, n_mp):
            device = (dp, flip_all(mp, k))
            sent[k] = copies.slot()
            copies.start(small_total.at[device[1]], r.small_line.at[k], device, sent[k])
        mixture.end(r.block_out)
        r.block_out[...] += r.hidden[...]
        for c in (2, 0, 1):
            r.shards[c] = r.line[0, c, 0].astype(F32)
            for k in range(1, n_mp):
                copies.wait(r.line.at[1, c, k], me, sent[c, k])
                r.shards[c] += r.line[1, c, k].astype(F32)
        r.small_shard[...] = small_total[mp]
        for k in range(1, n_mp):
            copies.wait(r.small_line.at[k], me, sent[k])
            r.small_shard[...] += r.small_line[k]
        for k in range(1, n_mp):
            copies.wait(r.arrived[k - 1], me, travels[k])
        copies.finish()

    return launch(
        attention_back,
        identity,
        dict(
            full=(given.full, hbm()),
            expert_grads=(given.expert_grads, hbm()),
            residual=(given.residual, vmem()),
            hidden=(given.hidden, vmem()),
            cotangent=(given.cotangent, vmem()),
            total=(given.total, vmem()),
            gate_parts=(given.gate_parts, vmem()),
            terms=(given.terms, vmem()),
            probs=(given.probs, vmem()),
            normed=(given.normed, vmem()),
            normed_two=(given.normed_two, vmem()),
            queries=(given.queries, vmem()),
            keyval=(given.keyval, vmem()),
            context=(given.context, vmem()),
            gain_one=(given.gain_one, vmem()),
            gain_two=(given.gain_two, vmem()),
            router=(given.router, vmem()),
            query_rotary=(given.rotary[0], vmem()),
            own_rotary=(given.rotary[1], vmem()),
        ),
        dict(
            input_grad=(single(tokens, width), vmem()),
            block_out=(single(tokens, width), vmem()),
            arrived=([low(*grad.shape) for grad in given.expert_grads], hbm()),
            shards=(single(3, rows, cols), vmem()),
            small_shard=(single(first_row + own_router, 128), vmem()),
        ),
        dict(
            grads=pltpu.VMEM((3, width, width), BF16),
            small=pltpu.VMEM((n_dp, n_mp, first_row + own_router, 128), F32),
            small_rooms=pltpu.VMEM((n_dp - 1, n_mp, first_row + own_router, 128), F32),
            small_line=pltpu.VMEM((n_mp, first_row + own_router, 128), F32),
            weight_rooms=pltpu.VMEM((3, 2, n_dp - 1, part_rows, width), BF16),
            line=pltpu.VMEM((2, 3, n_mp, rows, cols), BF16),
            rooms=rooms,
            across=across_room,
            weights=pltpu.VMEM((3, width, width), BF16),
            turned=pltpu.VMEM((128, tokens), F32),
            grad_router=pltpu.VMEM((width, 128), F32),
            grad_hidden=pltpu.VMEM((tokens, width), F32),
            grad_attn=pltpu.VMEM((tokens, width), BF16),
            grad_context=pltpu.VMEM((tokens, width), BF16),
            grad_q=pltpu.VMEM((tokens, width), BF16),
            grad_kv=pltpu.VMEM((tokens, width), F32),
            grad_kv_low=pltpu.VMEM((tokens, width), BF16),
            grad_normed=pltpu.VMEM((tokens, width), F32),
            swap=pltpu.VMEM((2, tokens, width), BF16),
            local_sems=pltpu.SemaphoreType.DMA((3,)),
        ),
        n_copies,
        62 << 20,
    )


class TokenReduce:
    def __init__(self, copies, n_dp, me, terms, rooms, across):
        dp, mp = me
        self.copies, self.me, self.across = copies, me, across
        self.partner = (dp, flip(mp, 1))
        self.tokens = terms.shape[2]
        self.n_dp = n_dp
        self.last = n_dp.bit_length() - 2
        self.groups = terms.shape[0]
        self.slot = copies.slot()

        def tree(group, part, order):
            cut = pl.ds(part * (self.tokens // 2), self.tokens // 2)
            return TreeReduce(
                copies,
                order,
                n_dp,
                me,
                lambda j: terms.at[group, j, cut],
                lambda number: rooms.at[group, part, number],
                add_rows(),
            )

        self.trees = [
            [tree(group, part, order) for part, order in enumerate(orders_of(n_dp))]
            for group in range(self.groups)
        ]

    def first(self, group, j):
        for tree in self.trees[group]:
            tree.send(j)

    def level(self, group, p):
        if group == self.groups:
            return
        for j in range(1, self.n_dp):
            for tree in self.trees[group]:
                if place_of(tree.order, j) == p:
                    tree.collect(j)
                    tree.send(j)

    def pass_on(self):
        if self.groups == 1:
            return
        for part, tree in enumerate(self.trees[1]):
            tree.collect(0)
            cut = pl.ds(part * (self.tokens // 2), self.tokens // 2)
            self.across[0, cut, :] = tree.total()[...]
        self.copies.start(self.across.at[0], self.across.at[1], self.partner, self.slot)

    def end(self, out_ref):
        for tree in self.trees[0]:
            tree.collect(0)
        if self.groups > 1:
            self.copies.wait(self.across.at[1], self.me, self.slot)
        for part, tree in enumerate(self.trees[0]):
            cut = pl.ds(part * (self.tokens // 2), self.tokens // 2)
            total = tree.total()[...].astype(F32)
            if self.groups > 1:
                total = total + self.across[1, cut, :].astype(F32)
            out_ref[cut, :] = total


def reduce_rooms(groups, n_dp, tokens, width, dtype):
    return [
        pltpu.VMEM((groups, 2, n_dp - 1, tokens // 2, width), dtype),
        pltpu.VMEM((2, tokens, width), dtype),
    ]


def run_expert(n_dp, n_mp, groups, identity, index, shared, parts, inputs):
    first, last = index == 0, index == shared - 1
    hidden, width = parts[0].shape[1:]
    units = n_mp * hidden
    blocks = groups * n_dp
    slots = blocks * CAP
    tokens = inputs.rows.shape[0]
    per_tile = 4
    tile = per_tile * CAP
    ins = dict(part=(parts, hbm()))
    outs = dict(grad=([low(3, hidden, width) for _ in range(n_mp)], vmem()))
    scratch = dict(
        weights=pltpu.VMEM((3, units, width), BF16),
        act=pltpu.VMEM((slots, units), BF16),
        pair=pltpu.VMEM((slots, 2 * units), BF16),
        grad_rows=pltpu.VMEM((slots, width), BF16),
        part_sems=pltpu.SemaphoreType.DMA((3 * n_mp,)),
    )
    n_copies = 1
    slot_rows = pltpu.VMEM((slots, width), BF16)
    if first:
        n_copies += blocks + 2 * groups * (n_dp - 1)
        ins |= dict(
            rows=(inputs.rows, hbm()), own_table=(inputs.table, hbm()), cots=(inputs.cots, hbm())
        )
        scratch |= dict(
            tokens_all=pltpu.VMEM((groups, n_dp, tokens, width), BF16),
            x_own=slot_rows,
            c_own=slot_rows,
            cot=pltpu.VMEM((2, tokens, width), BF16),
            cot_sems=pltpu.SemaphoreType.DMA((2,)),
            keep_sems=pltpu.SemaphoreType.DMA((2,)),
        )
    else:
        ins |= dict(
            tables_in=(inputs.tables, vmem()),
            gates_in=(inputs.gates, vmem()),
            x_in=(inputs.x[index], vmem()),
            c_in=(inputs.c[index], vmem()),
        )
    if first and last:
        scratch |= dict(tables=pltpu.VMEM((blocks, 8, tokens), F32))
    elif first:
        rest = [low(slots, width) for _ in range(1, shared)]
        outs |= dict(tables=(single(blocks, 8, tokens), vmem()))
        outs |= dict(x=(rest, vmem()), c=(rest, vmem()))
    if last:
        n_copies += 2 * groups * (n_dp - 1) + blocks
        ins |= dict(y_before=(inputs.y, vmem()), d_before=(inputs.d, vmem()))
        outs |= dict(
            terms=(low(groups, n_dp, tokens, width), hbm()),
            gate_parts=(single(n_dp, groups, 8, tokens), hbm()),
            total=(single(tokens, width), vmem()),
        )
        rooms, across_room = reduce_rooms(groups, n_dp, tokens, width, BF16)
        scratch |= dict(
            gates=pltpu.VMEM((blocks, 8, tokens), F32),
            y=slot_rows,
            d=slot_rows,
            grads_all=pltpu.VMEM((groups, n_dp, tokens, width), BF16),
            sums=pltpu.VMEM((2, tokens, width), BF16),
            sum_sems=pltpu.SemaphoreType.DMA((2,)),
            gate_sem=pltpu.SemaphoreType.DMA((1,)),
            rooms=rooms,
            across=across_room,
        )
    else:
        outs |= dict(
            gates=(single(blocks, 8, tokens), vmem()),
            y=(low(slots, width), vmem()),
            d=(low(slots, width), vmem()),
        )

    def expert(r):
        dp, mp = lax.axis_index("dp"), lax.axis_index("mp")
        me = (dp, mp)
        other = flip(mp, 1)
        kind = lax.rem(mp, groups)
        copies = Copies(r.send_sems, r.recv_sems)
        peers = {
            (group, j): (flip_all(dp, j), other if group else mp)
            for group in range(groups)
            for j in range(n_dp)
            if group + j
        }
        weights, act, pair, grad_rows = r.weights, r.act, r.pair, r.grad_rows
        loads = [
            pltpu.make_async_copy(
                r.part[k].at[c],
                weights.at[c, pl.ds(k * hidden, hidden)],
                r.part_sems.at[3 * k + c],
            )
            for k in range(n_mp)
            for c in range(3)
        ]
        for copy in loads:
            copy.start()
        tables = r.tables if first else r.tables_in
        x_refs = {index: r.x_own if first else r.x_in}
        c_refs = {index: r.c_own if first else r.c_in}
        if first:
            x_refs |= {i + 1: ref for i, ref in enumerate(r.x if shared > 1 else [])}
            c_refs |= {i + 1: ref for i, ref in enumerate(r.c if shared > 1 else [])}

        def hits(block, experts):
            slot = lax.broadcasted_iota(jnp.int32, (CAP, tokens), 0).astype(F32)
            found = [slot == tables[block, pl.ds(i, 1), :] for i in experts]
            return found[0] if len(found) == 1 else jnp.concatenate(found, 0)

        def rows_of(block):
            return pl.ds(pl.multiple_of(block * CAP, 16), CAP)

        if first:
            rows_all, cots = r.tokens_all, r.cots
            keep = [
                pltpu.make_async_copy(r.rows, rows_all.at[0, 0], r.keep_sems.at[0]),
                pltpu.make_async_copy(
                    r.own_table.at[dp, kind], tables.at[0], r.keep_sems.at[1]
                ),
            ]
            for copy in keep:
                copy.start()
            order = [(group, 0) for group in range(groups)]
            for level in range(1, n_dp.bit_length()):
                for group in range(groups):
                    order += [(group, j) for j in range(n_dp) if bin(j).count("1") == level]

            def cot_copy(number):
                group, j = order[number]
                return pltpu.make_async_copy(
                    cots[group].at[j], r.cot.at[number % 2], r.cot_sems.at[number % 2]
                )

            cot_copy(0).start()
            greet(list(peers.values()))
            across = copies.slot()
            if groups > 1:
                copies.start(r.rows, rows_all.at[1, 0], peers[1, 0], across)
            sent = {}
            for key, device in peers.items():
                sent[key] = copies.slot()
                group, j = key
                copies.start(
                    r.own_table.at[device[0], lax.rem(device[1], groups)],
                    tables.at[group * n_dp + j],
                    device,
                    sent[key],
                )
            trees = [row_trees(copies, n_dp, me, rows_all.at[group]) for group in range(groups)]
            keep[0].wait()
            for tree in trees[0]:
                tree.send(0)
            keep[1].wait()

            def fill(number):
                group, j = order[number]
                block = group * n_dp + j
                if number:
                    copies.wait(tables.at[block], me, sent[group, j])
                if number + 1 < blocks:
                    cot_copy(number + 1).start()
                pick = hits(block, range(shared)).astype(BF16)
                found = dot(pick, rows_all[group, j], NN).astype(BF16)
                for i in range(shared):
                    x_refs[i][block * CAP : (block + 1) * CAP, :] = found[i * CAP : (i + 1) * CAP]
                cot_copy(number).wait()
                found = dot(pick, r.cot[number % 2], NN).astype(BF16)
                for i in range(shared):
                    c_refs[i][block * CAP : (block + 1) * CAP, :] = found[i * CAP : (i + 1) * CAP]

            for number, (group, j) in enumerate(order):
                if j:
                    for tree in sorted(trees[group], key=lambda tree: place_of(tree.order, j)):
                        tree.receive(j)
                        tree.send(j)
                elif group:
                    copies.wait(rows_all.at[1, 0], me, across)
                    for tree in trees[1]:
                        tree.send(0)
                fill(number)
        else:
            greet(list(peers.values()))
        if last:
            gates = r.gates
            if index:
                gates[...] = r.gates_in[...]
        else:
            gates = r.gates
        for copy in loads:
            copy.wait()
        x_all, c_all = x_refs[index], c_refs[index]
        y_all, d_all = r.y, r.d

        def work(step, carry):
            rows = pl.ds(pl.multiple_of(step * tile, 16), tile)
            x = x_all[rows, :]
            gate = dot(x, weights[0], NT)
            up = dot(x, weights[1], NT)
            sigmoid = 1.0 / (1.0 + jnp.exp(-gate))
            silu = gate * sigmoid
            activation = (silu * up).astype(BF16)
            act[rows, :] = activation
            made = dot(activation, weights[2], NN)
            cot = c_all[rows, :].astype(F32)
            chosen, scores = [], []
            dots = jnp.sum(cot * made, -1, keepdims=True)
            for b in range(per_tile):
                block = step * per_tile + b
                hit = hits(block, (index,))
                chance = tables[block, pl.ds(4 + index, 1), :]
                chosen.append(jnp.sum(jnp.where(hit, chance, 0.0), -1, keepdims=True))
                here = dots[b * CAP : (b + 1) * CAP]
                gates[block, pl.ds(index, 1), :] = jnp.sum(
                    jnp.where(hit, here, 0.0), 0, keepdims=True
                )
            share = jnp.concatenate(chosen, 0)
            y_all[rows, :] = (share * made).astype(BF16)
            back = (share * cot).astype(BF16)
            grad_rows[rows, :] = back
            grad_act = dot(back, weights[2], NT)
            grad_gate = grad_act * up * sigmoid * (1.0 + gate * (1.0 - sigmoid))
            grad_gate = grad_gate.astype(BF16)
            grad_up = (grad_act * silu).astype(BF16)
            pair[rows, pl.ds(0, units)] = grad_gate
            pair[rows, pl.ds(units, units)] = grad_up
            d_all[rows, :] = (dot(grad_gate, weights[0], NN) + dot(grad_up, weights[1], NN)).astype(
                BF16
            )
            return carry

        lax.fori_loop(0, blocks // per_tile, work, 0)

        def weight_grad(k):
            x, back = x_all[...], grad_rows[...]
            for c, source in enumerate((pair, pair, act)):
                columns = pl.ds(k * hidden + (units if c == 1 else 0), hidden)
                rhs = back if c == 2 else x
                r.grad[k][c] = dot(source[:, columns], rhs, TN).astype(BF16)

        if not last:
            for k in range(n_mp):
                weight_grad(k)
        else:
            y_refs = r.y_before + [y_all]
            d_refs = r.d_before + [d_all]
            reduce = TokenReduce(copies, n_dp, me, r.grads_all, r.rooms, r.across)
            back = range(groups)[::-1]
            order = [(g, j) for g in back for j in range(1, n_dp, 2)]
            order += [(g, j) for g in back for j in range(0, n_dp, 2)]

            def sum_copy(number):
                group, j = order[number]
                return pltpu.make_async_copy(
                    r.sums.at[number % 2], r.terms.at[group, j], r.sum_sems.at[number % 2]
                )

            sent = {}
            own_gates = pltpu.make_async_copy(
                gates.at[0], r.gate_parts.at[dp, kind], r.gate_sem.at[0]
            )
            own_gates.start()
            for number, (group, j) in enumerate(order):
                block = group * n_dp + j
                if group + j:
                    sent[group, j] = copies.slot()
                    copies.start(
                        gates.at[block],
                        r.gate_parts.at[dp, kind],
                        peers[group, j],
                        sent[group, j],
                    )
                pick = hits(block, range(shared)).astype(BF16)
                there = rows_of(block)
                found = jnp.concatenate([ref[there, :] for ref in d_refs], 0)
                r.grads_all[group, j] = dot(pick, found, TN).astype(BF16)
                if j % 2:
                    reduce.first(group, j)
                found = jnp.concatenate([ref[there, :] for ref in y_refs], 0)
                if number > 1:
                    sum_copy(number - 2).wait()
                r.sums[number % 2] = dot(pick, found, TN).astype(BF16)
                sum_copy(number).start()
            left = list(range(n_mp))

            def some(count):
                for _ in range(count):
                    if left:
                        weight_grad(left.pop(0))

            for p in range(reduce.last - 1, -1, -1):
                reduce.level(1, p)
                some(1)
            reduce.pass_on()
            for p in range(reduce.last - 1, -1, -1):
                reduce.level(0, p)
                some(1)
            some(n_mp)
            reduce.end(r.total)
            for number in (blocks - 2, blocks - 1):
                sum_copy(number).wait()
            own_gates.wait()
            for (group, j), device in peers.items():
                theirs = 1 - kind if group else kind
                copies.wait(r.gate_parts.at[device[0], theirs], me, sent[group, j])
        copies.finish()

    return launch(expert, identity, ins, outs, scratch, n_copies, 60 << 20)


def adamw(weight, gradient, moment_one, moment_two, rate_val, decay_val):
    first_new = 0.9 * moment_one + 0.1 * gradient
    second_new = 0.95 * moment_two + 0.05 * gradient * gradient
    first_hat = first_new / (1.0 - 0.9**STEP)
    second_hat = second_new / (1.0 - 0.95**STEP)
    weight_new = weight - rate_val * (
        first_hat / (jnp.sqrt(second_hat) + 1e-08) + decay_val * weight
    )
    return (gradient, weight_new, first_new, second_new)


def local(
    n_dp,
    n_mp,
    residual_in,
    cotangent,
    expert_ids,
    attn_gain,
    query_w,
    key_value_weight,
    output_w,
    moe_gain,
    router_w,
    gateup_w,
    down_w,
    attn_gain_mean,
    attn_gain_var,
    query_mean,
    query_var,
    key_value_first_moment,
    key_value_second_moment,
    output_mean,
    output_var,
    moe_gain_mean,
    moe_gain_var,
    router_mean,
    router_var,
    gateup_mean,
    gateup_var,
    down_mean,
    down_var,
):
    mp = lax.axis_index("mp")
    place_in_all = lax.axis_index("dp") * n_mp + mp
    groups = 2 if 2 * n_dp <= 16 else 1
    kind = mp % groups
    tokens = residual_in.shape[0]
    owned = gateup_w.shape[0]
    shared = owned // groups
    hidden_units = down_w.shape[1]
    flips = [[(i, i ^ k) for i in range(n_mp)] for k in range(n_mp)]
    own_gain, own_router = attn_gain.shape[0], router_w.shape[0]
    first_row, lanes = 8, 128
    per_tile = lanes // own_gain

    def spread(gain):
        return jnp.where(jnp.arange(lanes) // own_gain == place_in_all % per_tile, jnp.tile(gain, per_tile), 0.0)

    small = jnp.concatenate(
        [
            spread(attn_gain)[None],
            spread(moe_gain)[None],
            jnp.zeros((first_row - 2, lanes), F32),
            jnp.pad(router_w, ((0, 0), (0, lanes - EXPERTS))),
        ]
    )
    shards = jnp.stack([query_w, key_value_weight, output_w.T]).astype(BF16)
    cot_low = cotangent.astype(BF16)
    start = prologue(n_dp, n_mp, groups, 0, small, shards, cot_low, residual_in)
    small_all = start.small_all
    gains = [
        jnp.sum(small_all[:, :, row].reshape(-1, per_tile, lanes), 1).reshape(1, -1) for row in (0, 1)
    ]
    router_low = small_all[:, :, first_row:].reshape(MODEL_WIDTH, lanes).astype(BF16)

    expert_range = jnp.arange(EXPERTS, dtype=jnp.int32)
    onehot = (expert_ids[:, :, None] == expert_range[None, None, :]).astype(jnp.int32)
    chosen = jnp.sum(onehot, 1)
    before = jnp.cumsum(chosen, 0) - chosen
    place = jnp.where(chosen > 0, before, -1)
    by_owner = place.astype(F32).T.reshape(n_dp, shared, groups, tokens).transpose(0, 2, 1, 3)
    places = jnp.pad(by_owner, ((0, 0), (0, 0), (0, 8 - shared), (0, 0)))

    packed = jnp.concatenate([gateup_w, down_w[:, None]], 1).astype(BF16)

    def send_weights(i, after):
        mine = theirs = packed[groups * i]
        if groups > 1:
            mine = jnp.where(kind == 0, packed[2 * i], packed[2 * i + 1])
            theirs = jnp.where(kind == 0, packed[2 * i + 1], packed[2 * i])
        mine, theirs, after = lax.optimization_barrier((mine, theirs, after))
        parts = [mine] + [
            lax.ppermute(theirs if k % 2 else mine, "mp", flips[k]) for k in range(1, n_mp)
        ]
        return parts, after

    expert_parts = [None] * shared
    expert_parts[0], row_block = send_weights(0, start.row_block)
    whole = gather_rows(n_dp, groups, 1, row_block, cot_low)
    full = whole.full

    query_table, key_table = (jnp.asarray(table) for table in rotary_constants())
    part = mp % 2
    rotary = [
        lax.dynamic_slice_in_dim(table, which * tokens, tokens, 1)
        for table, which in ((query_table, part), (key_table, part), (key_table, 1 - part))
    ]
    front = attention_forward(
        n_dp,
        groups,
        shared,
        2,
        residual_in,
        start.normed,
        full,
        gains[1],
        router_low,
        places,
        whole.cot_other,
        rotary,
    )

    rows = front.normed_two
    for i in range(1, shared):
        expert_parts[i], (rows, expert_parts[i - 1]) = send_weights(i, (rows, expert_parts[i - 1]))
    made = types.SimpleNamespace(
        rows=rows, table=front.table, cots=[start.cots, front.cots][:groups], y=[], d=[]
    )
    expert_grads = []
    for i in range(shared):
        found = run_expert(n_dp, n_mp, groups, 3 + i, i, shared, expert_parts[i], made)
        if i < shared - 1:
            made.gates = found.gates
            made.y, made.d = made.y + [found.y], made.d + [found.d]
            if i == 0:
                made.tables, made.x, made.c = found.tables, [None] + found.x, [None] + found.c
        if i < shared - 1:
            expert_grads.append(
                found.grad[:1]
                + [lax.ppermute(found.grad[k], "mp", flips[k]) for k in range(1, n_mp)]
            )
    total, expert_grads = lax.optimization_barrier((found.total, expert_grads))
    given = types.SimpleNamespace(
        full=full,
        residual=residual_in,
        hidden=front.hidden,
        cotangent=cotangent,
        total=total,
        expert_grads=found.grad[1:],
        gate_parts=found.gate_parts,
        terms=found.terms,
        probs=front.probs,
        normed=start.normed,
        normed_two=front.normed_two,
        queries=front.queries,
        keyval=front.keyval,
        context=front.context,
        gain_one=gains[0],
        gain_two=gains[1],
        router=router_low,
        rotary=rotary,
    )
    back = attention_backward(n_dp, n_mp, groups, shared, 3 + shared, given, first_row)
    input_grad, block_out = back.input_grad, back.block_out
    expert_grads = expert_grads + [found.grad[:1] + back.arrived]
    pairs = []
    for i in range(shared):
        if groups == 1:
            pairs.append(sum(part.astype(F32) for part in expert_grads[i]))
            continue
        same = sum(part.astype(F32) for part in expert_grads[i][0::2])
        turned = sum(part.astype(F32) for part in expert_grads[i][1::2])
        pairs.append(jnp.where(kind == 0, same, turned))
        pairs.append(jnp.where(kind == 0, turned, same))
    expert_grad = jnp.stack(pairs)
    gateup_grad, down_grad = expert_grad[:, :2], expert_grad[:, 2]

    grads, small_grads = back.shards, back.small_shard
    query_grad, keyval_grad, output_grad = grads[0], grads[1], grads[2].T
    first_lane = (place_in_all % per_tile) * own_gain
    gain_one_grad, gain_two_grad = (
        lax.dynamic_slice_in_dim(small_grads[row], first_lane, own_gain) for row in (0, 1)
    )
    router_grad = small_grads[first_row:, :EXPERTS]
    matrix_rate = 0.2 / math.sqrt(MODEL_WIDTH)
    gain_one_all = adamw(attn_gain, gain_one_grad, attn_gain_mean, attn_gain_var, 0.1, 0.0)
    query_all = adamw(query_w, query_grad, query_mean, query_var, matrix_rate, 0.1)
    keyval_all = adamw(
        key_value_weight,
        keyval_grad,
        key_value_first_moment,
        key_value_second_moment,
        matrix_rate,
        0.1,
    )
    output_all = adamw(output_w, output_grad, output_mean, output_var, 0.1, 0.1)
    gain_two_all = adamw(moe_gain, gain_two_grad, moe_gain_mean, moe_gain_var, 0.1, 0.0)
    router_all = adamw(router_w, router_grad, router_mean, router_var, matrix_rate, 0.1)
    gateup_all = adamw(gateup_w, gateup_grad, gateup_mean, gateup_var, matrix_rate, 0.1)
    down_all = adamw(down_w, down_grad, down_mean, down_var, 0.07, 0.1)
    return (
        block_out,
        input_grad,
        gain_one_all[0],
        gain_one_all[1],
        gain_one_all[2],
        gain_one_all[3],
        query_all[0],
        query_all[1],
        query_all[2],
        query_all[3],
        keyval_all[0],
        keyval_all[1],
        keyval_all[2],
        keyval_all[3],
        output_all[0],
        output_all[1],
        output_all[2],
        output_all[3],
        gain_two_all[0],
        gain_two_all[1],
        gain_two_all[2],
        gain_two_all[3],
        router_all[0],
        router_all[1],
        router_all[2],
        router_all[3],
        gateup_all[0],
        gateup_all[1],
        gateup_all[2],
        gateup_all[3],
        down_all[0],
        down_all[1],
        down_all[2],
        down_all[3],
    )


def solution(mesh):
    in_specs = (
        P(("dp", "mp"), None),
        P(("dp", "mp"), None),
        P(("dp", "mp"), None),
        P(("dp", "mp")),
        P("dp", "mp"),
        P("dp", "mp"),
        P("mp", "dp"),
        P(("dp", "mp")),
        P(("dp", "mp"), None),
        P("dp", None, "mp", None),
        P("dp", "mp", None),
        P(("dp", "mp")),
        P(("dp", "mp")),
        P("dp", "mp"),
        P("dp", "mp"),
        P("dp", "mp"),
        P("dp", "mp"),
        P("mp", "dp"),
        P("mp", "dp"),
        P(("dp", "mp")),
        P(("dp", "mp")),
        P(("dp", "mp"), None),
        P(("dp", "mp"), None),
        P("dp", None, "mp", None),
        P("dp", None, "mp", None),
        P("dp", "mp", None),
        P("dp", "mp", None),
    )
    out_specs = (
        P(("dp", "mp"), None),
        P(("dp", "mp"), None),
        P(("dp", "mp")),
        P(("dp", "mp")),
        P(("dp", "mp")),
        P(("dp", "mp")),
        P("dp", "mp"),
        P("dp", "mp"),
        P("dp", "mp"),
        P("dp", "mp"),
        P("dp", "mp"),
        P("dp", "mp"),
        P("dp", "mp"),
        P("dp", "mp"),
        P("mp", "dp"),
        P("mp", "dp"),
        P("mp", "dp"),
        P("mp", "dp"),
        P(("dp", "mp")),
        P(("dp", "mp")),
        P(("dp", "mp")),
        P(("dp", "mp")),
        P(("dp", "mp"), None),
        P(("dp", "mp"), None),
        P(("dp", "mp"), None),
        P(("dp", "mp"), None),
        P("dp", None, "mp", None),
        P("dp", None, "mp", None),
        P("dp", None, "mp", None),
        P("dp", None, "mp", None),
        P("dp", "mp", None),
        P("dp", "mp", None),
        P("dp", "mp", None),
        P("dp", "mp", None),
    )
    step = functools.partial(local, mesh.shape["dp"], mesh.shape["mp"])
    return jax.shard_map(step, mesh=mesh, in_specs=in_specs, out_specs=out_specs, check_vma=False)
```

time: 671 us -> 507 us (0.76)
  waiting for transfers between devices: 62.6 us -> 0.02 us
  matrix products: 43.1 us -> 0 us
  Pallas kernels: 441 us -> 407 us
  other arithmetic: 48.9 us -> 30.9 us
  local copies, waits for them, and re-layouts: 44.3 us -> 29.3 us
  starting transfers between devices: 19.5 us -> 28.3 us
    ppermute x14 -> x9, waiting for transfers between devices: 62.6 us -> 0.02 us  [the longest x6 0.02 us: send_weights(): lax.ppermute(theirs if k % 2 else mine, 'mp', flips[k])]
    dot_general x18 -> x0, matrix products: 43.1 us -> none  [the longest x1 5.83 us: local(): jnp.einsum('qkgd,skd->kgqs', grad_ctx, values, preferred_element_type=F32)]
    pallas_call x6, Pallas kernels: 441 us -> 407 us  [launch(): pl.pallas_call(body, out_shape=tuple(shapes), in_specs=in_specs, out_spec...]
    dot_general x3 -> x0, local copies, waits for them, and re-layouts: 11.5 us -> none  [the longest x2 8.6 us: local(): jnp.dot(jnp.concatenate([normed_other, normed_one]), keyval_full, preferr...]
    unnamed x157 -> x125, local copies, waits for them, and re-layouts: 15.5 us -> 24.5 us
    scatter x8 -> x0, local copies, waits for them, and re-layouts: 8.96 us -> none  [the longest x1 3.15 us: local(): small_grads.at[:, :, 8:, :EXPERTS]]
    ppermute x14 -> x9, starting transfers between devices: 19.5 us -> 28.3 us  [the longest x3 19.6 us: local(): lax.ppermute(found.grad[k], 'mp', flips[k])]
    convert_element_type x9 -> x1, other arithmetic: 8.31 us -> 1.29 us  [local(): cot_low = cotangent.astype(BF16)]
  transfers between devices with their start and end apart: 14 -> 9, of which waited for: 3 -> 0; matrix products, arithmetic and copies ran while one was open for 12% -> 1% of each run, Pallas kernels for 41% -> 50%
where the time goes in v3:
time: 507 us; the launch traced here: 498 us
  Pallas kernels  407 us (80%)
  other arithmetic  30.9 us (6%)
  local copies, waits for them, and re-layouts  29.3 us (6%)
  starting transfers between devices  28.3 us (6%)
    pallas_call x6, Pallas kernels, launch(): pl.pallas_call(body, out_shape=tuple(shapes), in_specs=in_specs, out_spec...  407 us
    unnamed x125, local copies, waits for them, and re-layouts  24.5 us
    ppermute x3, starting transfers between devices, local(): lax.ppermute(found.grad[k], 'mp', flips[k])  19.6 us
    sub x7, other arithmetic, adamw(): weight - rate_val * (first_hat / (jnp.sqrt(second_hat) + 1e-08) + decay_v...  15.6 us
  transfers between devices with their start and end apart: 9, of which 0 were waited for; matrix products, arithmetic and copies ran while one was open for 1% of the time, Pallas kernels for 50%

profile of v3, /device:TPU:0, one launch (start us, length us, event | category | flops | bytes accessed | tf_op | source)
XLA Modules:
  0.0 497.6 jit_solution(2480248587630477325)
XLA Ops:
  5.5 1.3 convert_element_type.43.refs_2_.refs_1_
  6.8 2.7 convert.23
  9.8 1.0 select_bitcast_fusion.4
  10.9 1.5 select_bitcast_fusion.5
  15.0 41.2 %gather_line.1 = (f32[8,4,40,128]{3,2,1,0:T(8,128)S(1)}, bf16[3,128,1024]{2,1,0:T(8,128)(2,1)S(1)}, bf16[8,256,1024]{2,1,0:T(8,128)(2,1)S(1)}, bf16[2,256,1024]{2,1,0:T(8,128)(2,1)S(1)}) custom-call(f32[40,128]{1,0:T(8,128)S(1)} %select_maximum_fusion.refs_0_, bf16[3,128,256]{2,1,0:T(8,128)(2,1)S(1)} %pad_maximum_fusion.2.refs_1_, ...), custom_call_target="tpu_custom_call" | custom-call | flops 1 | bytes 1 | tf_op jit(solution)/shard_map/gather_line/pallas_call | solution.py:224
  56.3 2.0 copy-done.2
  59.2 1.6 collective-permute-start
  60.8 2.4 collective-permute-start.2
  63.2 56.4 %gather_weights.1 = (bf16[3,1024,1024]{2,1,0:T(8,128)(2,1)S(1)}, bf16[256,1024]{1,0:T(8,128)(2,1)S(1)}) custom-call(bf16[3,128,1024]{2,1,0:T(8,128)(2,1)S(1)} %get-tuple-element.88.refs_0_, bf16[256,1024]{1,0:T(8,128)(2,1)S(1)} %convert_element_type.43.refs_2_.refs_1_), custom_call_target="tpu_custom_call" | custom-call | flops 1 | bytes 1 | tf_op jit(solution)/shard_map/gather_weights/pallas_call | solution.py:224
  119.6 2.7 copy-done
  124.8 31.3 %attention.1 = (bf16[8,256,1024]{2,1,0:T(8,128)(2,1)}, bf16[256,1024]{1,0:T(8,128)(2,1)S(1)}, bf16[2,256,1024]{2,1,0:T(8,128)(2,1)S(1)}, bf16[256,1024]{1,0:T(8,...) custom-call(f32[256,1024]{1,0:T(8,128)} %refs_4_.1, ...), custom_call_target="tpu_custom_call" | custom-call | flops 1 | bytes 1 | tf_op jit(solution)/shard_map/attention/pallas_call | solution.py:224
  161.8 2.5 collective-permute-start.3
  164.4 2.2 collective-permute-start.5
  166.6 89.7 %expert.2 = (bf16[3,128,1024]{2,1,0:T(8,128)(2,1)}, bf16[3,128,1024]{2,1,0:T(8,128)(2,1)}, bf16[3,128,1024]{2,1,0:T(8,128)(2,1)}, bf16[3,128,1024]{2,1,0:T(8,128...) custom-call(bf16[3,128,1024]{2,1,0:T(8,128)(2,1)} %get-tuple-element, ...), custom_call_target="tpu_custom_call" | custom-call | flops 1 | bytes 1 | tf_op jit(solution)/shard_map/expert/pallas_call | solution.py:224
  256.3 17.1 %collective-permute-start.6 = (bf16[3,128,1024]{2,1,0:T(8,128)(2,1)}, bf16[3,128,1024]{2,1,0:T(8,128)(2,1)S(1)}, u32[]{:S(2)}, u32[]{:S(2)}) collective-permute-start(bf16[3,128,1024]{2,1,0:T(8,128)(2,1)} %get-tuple-element.118), channel_id=1, source_target_pairs={{0,1},{1,0},{2,3},{3,2},{4,5},{5,4},{6,7},{7,6},{8,9},{9,8},{10,11... | collective-permute-start | bytes 2359304 | tf_op jit(solution)/shard_map/ppermute | solution.py:1398
  273.4 2.4 collective-permute-start.8
  277.0 71.5 %expert.3 = (bf16[3,128,1024]{2,1,0:T(8,128)(2,1)}, bf16[3,128,1024]{2,1,0:T(8,128)(2,1)}, bf16[3,128,1024]{2,1,0:T(8,128)(2,1)}, bf16[3,128,1024]{2,1,0:T(8,128...) custom-call(bf16[3,128,1024]{2,1,0:T(8,128)(2,1)} %get-tuple-element.96.refs_0_, ...), custom_call_target="tpu_custom_call" | custom-call | flops 1 | bytes 1 | tf_op jit(solution)/shard_map/expert/pallas_call | solution.py:224
  349.7 117.2 %attention_back.1 = (f32[256,1024]{1,0:T(8,128)}, f32[256,1024]{1,0:T(8,128)}, bf16[3,128,1024]{2,1,0:T(8,128)(2,1)}, bf16[3,128,1024]{2,1,0:T(8,128)(2,1)}, bf1...) custom-call(bf16[3,1024,1024]{2,1,0:T(8,128)(2,1)} %copy-done, ...), custom_call_target="tpu_custom_call" | custom-call | flops 1 | bytes 1 | tf_op jit(solution)/shard_map/attention_back/pallas_call | solution.py:224
  466.9 1.0 slice_bitcast_fusion
  472.8 1.9 select_bitcast_fusion.3
  478.4 5.0 multiply_subtract_fusion.1
  484.8 1.2 copy-done.19
  486.1 6.7 %multiply_subtract_fusion = (f32[4,2,128,1024]{3,2,1,0:T(8,128)}, f32[4,2,128,1024]{3,2,1,0:T(8,128)}, f32[4,2,128,1024]{3,2,1,0:T(8,128)}, f32[4,2,128,1024]{3,2,1,0:T(8,128)}) fusion(f32[4,2,128,1024]{3,2,1,0:T(8,128)S(1)} %copy-done.15, f32[4,2,128,1024]{3,2,1,0:T(8,128)S(1)} %copy-done.18, f32[4,2,128,1024]{3,2,1,0:T(8,128)S(1)} %copy-done.19, ...), kind=kLoop, calls=%fused_computation.6 | loop fusion | flops 15728640 | bytes 33554432 | tf_op jit(solution)/shard_map/sub | solution.py:1264
  494.2 1.1 multiply_subtract_fusion.3
  (166 shorter events, 32.1 us)
Async XLA Ops:
  59.2 65.5 %copy-start.41 = (f32[2,512,128]{2,1,0:T(8,128)S(1)}, f32[2,512,128]{2,1,0:T(8,128)}, u32[]{:S(2)}) copy-start(f32[2,512,128]{2,1,0:T(8,128)} %constant.155.clone) | copy-start | bytes 1572868
  59.2 65.5 %copy-start.47 = (f32[2,512,128]{2,1,0:T(8,128)S(1)}, f32[2,512,128]{2,1,0:T(8,128)}, u32[]{:S(2)}) copy-start(f32[2,512,128]{2,1,0:T(8,128)} %constant.154.clone) | copy-start | bytes 1572868
  59.2 102.6 %collective-permute-start = (bf16[3,128,1024]{2,1,0:T(8,128)(2,1)}, bf16[3,128,1024]{2,1,0:T(8,128)(2,1)}, u32[]{:S(2)}, u32[]{:S(2)}) collective-permute-start(bf16[3,128,1024]{2,1,0:T(8,128)(2,1)} %get-tuple-element.95), channel_id=1, source_target_pairs={{0,1},{1,0},{2,3},{3,2},{4,5},{5,4},{6,7},{7,6},{8,9},{9,8},{10,11... | collective-permute-start | bytes 2359304 | tf_op jit(solution)/shard_map/ppermute | solution.py:1351
  60.8 101.0 %collective-permute-start.2 = (bf16[3,128,1024]{2,1,0:T(8,128)(2,1)}, bf16[3,128,1024]{2,1,0:T(8,128)(2,1)}, u32[]{:S(2)}, u32[]{:S(2)}) collective-permute-start(bf16[3,128,1024]{2,1,0:T(8,128)(2,1)} %get-tuple-element.95), channel_id=1, source_target_pairs={{0,3},{1,2},{2,1},{3,0},{4,7},{5,6},{6,5},{7,4},{8,11},{9,10},{10,... | collective-permute-start | bytes 2359304 | tf_op jit(solution)/shard_map/ppermute | solution.py:1351
  63.2 98.6 %collective-permute-start.1 = (bf16[3,128,1024]{2,1,0:T(8,128)(2,1)}, bf16[3,128,1024]{2,1,0:T(8,128)(2,1)}, u32[]{:S(2)}, u32[]{:S(2)}) collective-permute-start(bf16[3,128,1024]{2,1,0:T(8,128)(2,1)} %get-tuple-element.98.refs_0_), channel_id=1, source_target_pairs={{0,2},{1,3},{2,0},{3,1},{4,6},{5,7},{6,4},{7,5},{8,10},{9,11},{10,... | collective-permute-start | bytes 2359304 | tf_op jit(solution)/shard_map/ppermute | solution.py:1351
  122.3 33.8 %copy-start.4 = (bf16[8,4,32,128]{3,2,1,0:T(8,128)(2,1)}, bf16[8,4,32,128]{3,2,1,0:T(8,128)(2,1)S(1)}, u32[]{:S(2)}) copy-start(bf16[8,4,32,128]{3,2,1,0:T(8,128)(2,1)S(1)} %slice.135) | copy-start | bytes 786436
  124.7 31.4 %copy-start.14 = (f32[8,128]{1,0:T(8,128)}, f32[8,128]{1,0:T(8,128)S(1)}, u32[]{:S(2)}) copy-start(f32[8,128]{1,0:T(8,128)S(1)} %get-tuple-element.243) | copy-start | bytes 12292
  124.8 31.4 %copy-start.5 = (f32[2,256,128]{2,1,0:T(8,128)}, f32[2,256,128]{2,1,0:T(8,128)S(1)}, u32[]{:S(2)}) copy-start(f32[2,256,128]{2,1,0:T(8,128)S(1)} %get-tuple-element.285.refs_8_.refs_20_) | copy-start | bytes 786436
  124.8 31.4 %copy-start.6 = (f32[2,256,128]{2,1,0:T(8,128)}, f32[2,256,128]{2,1,0:T(8,128)S(1)}, u32[]{:S(2)}) copy-start(f32[2,256,128]{2,1,0:T(8,128)S(1)} %get-tuple-element.296.refs_7_.refs_19_) | copy-start | bytes 786436
  124.8 37.0 %copy-start.27 = (bf16[3,128,1024]{2,1,0:T(8,128)(2,1)S(1)}, bf16[3,128,1024]{2,1,0:T(8,128)(2,1)}, u32[]{:S(2)}) copy-start(bf16[3,128,1024]{2,1,0:T(8,128)(2,1)} %get-tuple-element.97) | copy-start | bytes 2359300
  124.8 41.8 %copy-start.20 = (bf16[3,128,1024]{2,1,0:T(8,128)(2,1)S(1)}, bf16[3,128,1024]{2,1,0:T(8,128)(2,1)}, u32[]{:S(2)}) copy-start(bf16[3,128,1024]{2,1,0:T(8,128)(2,1)} %get-tuple-element.96.refs_0_) | copy-start | bytes 2359300
  161.8 111.6 %collective-permute-start.3 = (bf16[3,128,1024]{2,1,0:T(8,128)(2,1)S(1)}, bf16[3,128,1024]{2,1,0:T(8,128)(2,1)}, u32[]{:S(2)}, u32[]{:S(2)}) collective-permute-start(bf16[3,128,1024]{2,1,0:T(8,128)(2,1)S(1)} %copy-done.27), channel_id=1, source_target_pairs={{0,1},{1,0},{2,3},{3,2},{4,5},{5,4},{6,7},{7,6},{8,9},{9,8},{10,11... | collective-permute-start | bytes 2359304 | tf_op jit(solution)/shard_map/ppermute | solution.py:1351
  164.4 112.6 %collective-permute-start.5 = (bf16[3,128,1024]{2,1,0:T(8,128)(2,1)S(1)}, bf16[3,128,1024]{2,1,0:T(8,128)(2,1)}, u32[]{:S(2)}, u32[]{:S(2)}) collective-permute-start(bf16[3,128,1024]{2,1,0:T(8,128)(2,1)S(1)} %copy-done.27), channel_id=1, source_target_pairs={{0,3},{1,2},{2,1},{3,0},{4,7},{5,6},{6,5},{7,4},{8,11},{9,10},{10,... | collective-permute-start | bytes 2359304 | tf_op jit(solution)/shard_map/ppermute | solution.py:1351
  166.6 110.4 %collective-permute-start.4 = (bf16[3,128,1024]{2,1,0:T(8,128)(2,1)S(1)}, bf16[3,128,1024]{2,1,0:T(8,128)(2,1)}, u32[]{:S(2)}, u32[]{:S(2)}) collective-permute-start(bf16[3,128,1024]{2,1,0:T(8,128)(2,1)S(1)} %copy-done.20), channel_id=1, source_target_pairs={{0,2},{1,3},{2,0},{3,1},{4,6},{5,7},{6,4},{7,5},{8,10},{9,11},{10,... | collective-permute-start | bytes 2359304 | tf_op jit(solution)/shard_map/ppermute | solution.py:1351
  166.6 109.3 %copy-start.46 = (f32[256,128]{1,0:T(8,128)S(1)}, f32[256,128]{1,0:T(8,128)}, u32[]{:S(2)}) copy-start(f32[256,128]{1,0:T(8,128)} %param.46) | copy-start | bytes 393220
  256.3 92.2 %collective-permute-start.6 = (bf16[3,128,1024]{2,1,0:T(8,128)(2,1)}, bf16[3,128,1024]{2,1,0:T(8,128)(2,1)S(1)}, u32[]{:S(2)}, u32[]{:S(2)}) collective-permute-start(bf16[3,128,1024]{2,1,0:T(8,128)(2,1)} %get-tuple-element.118), channel_id=1, source_target_pairs={{0,1},{1,0},{2,3},{3,2},{4,5},{5,4},{6,7},{7,6},{8,9},{9,8},{10,11... | collective-permute-start | bytes 2359304 | tf_op jit(solution)/shard_map/ppermute | solution.py:1398
  273.4 75.1 %collective-permute-start.7 = (bf16[3,128,1024]{2,1,0:T(8,128)(2,1)}, bf16[3,128,1024]{2,1,0:T(8,128)(2,1)S(1)}, u32[]{:S(2)}, u32[]{:S(2)}) collective-permute-start(bf16[3,128,1024]{2,1,0:T(8,128)(2,1)} %get-tuple-element.119), channel_id=1, source_target_pairs={{0,2},{1,3},{2,0},{3,1},{4,6},{5,7},{6,4},{7,5},{8,10},{9,11},{10,... | collective-permute-start | bytes 2359304 | tf_op jit(solution)/shard_map/ppermute | solution.py:1398
  273.4 75.2 %collective-permute-start.8 = (bf16[3,128,1024]{2,1,0:T(8,128)(2,1)}, bf16[3,128,1024]{2,1,0:T(8,128)(2,1)}, u32[]{:S(2)}, u32[]{:S(2)}) collective-permute-start(bf16[3,128,1024]{2,1,0:T(8,128)(2,1)} %get-tuple-element.120), channel_id=1, source_target_pairs={{0,3},{1,2},{2,1},{3,0},{4,7},{5,6},{6,5},{7,4},{8,11},{9,10},{10,... | collective-permute-start | bytes 2359304 | tf_op jit(solution)/shard_map/ppermute | solution.py:1398
  349.7 118.3 %copy-start.24 = (f32[256,128]{0,1:T(8,128)S(1)}, f32[256,128]{0,1:T(8,128)}, u32[]{:S(2)}) copy-start(f32[256,128]{0,1:T(8,128)} %copy-done.23) | copy-start | bytes 393220
  349.7 123.1 %copy-start.32 = (bf16[3,128,1024]{2,1,0:T(8,128)(2,1)S(1)}, bf16[3,128,1024]{2,1,0:T(8,128)(2,1)}, u32[]{:S(2)}) copy-start(bf16[3,128,1024]{2,1,0:T(8,128)(2,1)} %copy-done.31) | copy-start | bytes 2359300
  486.1 8.0 %copy-start.37 = (f32[3,128,256]{2,1,0:T(8,128)S(1)}, f32[3,128,256]{2,1,0:T(8,128)}, u32[]{:S(2)}) copy-start(f32[3,128,256]{2,1,0:T(8,128)} %get-tuple-element.131) | copy-start | bytes 1179652
  486.1 8.0 %copy-start.39 = (f32[128,256]{1,0:T(8,128)S(1)}, f32[128,256]{1,0:T(8,128)}, u32[]{:S(2)}) copy-start(f32[128,256]{1,0:T(8,128)} %param.34) | copy-start | bytes 393220
  486.1 8.0 %copy-start.40 = (f32[128,256]{1,0:T(8,128)S(1)}, f32[128,256]{1,0:T(8,128)}, u32[]{:S(2)}) copy-start(f32[128,256]{1,0:T(8,128)} %param.33) | copy-start | bytes 393220
  486.1 8.0 %copy-start.42 = (f32[128,256]{1,0:T(8,128)S(1)}, f32[128,256]{1,0:T(8,128)}, u32[]{:S(2)}) copy-start(f32[128,256]{1,0:T(8,128)} %param.44) | copy-start | bytes 393220
  (43 other events, 159.2 us)

commit v4 on v3

--- a/solution.py
+++ b/solution.py
@@ -94,6 +94,7 @@
     def finish(self):
         for copy in self.sent:
             copy.wait_send()
+        self.sent = []
 
 
 class TreeGather:
@@ -249,26 +250,11 @@
 NN, NT, TN = (1, 0), (1, 1), (0, 0)
 
 
-def gain_rows(small_all, row):
-    n_devices = math.prod(small_all.shape[:2])
-    n_tiles = MODEL_WIDTH // 128
-    per_tile = n_devices // n_tiles
-    n_mp = small_all.shape[1]
-    tiles = []
-    for tile in range(n_tiles):
-        total = None
-        for device in range(tile * per_tile, (tile + 1) * per_tile):
-            part = small_all[device // n_mp, device % n_mp, row : row + 1, :]
-            total = part if total is None else total + part
-        tiles.append(total)
-    return tiles
-
-
 def prologue(n_dp, n_mp, groups, identity, small, shards, cot, residual):
     half = n_mp // 2
     kinds, rows, cols = shards.shape
     tokens, width = cot.shape
-    order_a, order_b = orders_of(n_dp)
+    order_a, _ = orders_of(n_dp)
     n_copies = 2 * (n_mp - 1) + 4 * (n_dp - 1) + 1
 
     def gather_line(r):
@@ -280,6 +266,9 @@
         own_cols = pl.ds(pl.multiple_of(mp * cols, cols), cols)
         own_part = r.row_block.at[:, :, own_cols]
         r.small_all[dp, mp] = r.small[...]
+        residual_rows = r.residual[...]
+        inverse = lax.rsqrt(jnp.mean(residual_rows * residual_rows, -1, keepdims=True) + NORM_EPS)
+        r.scaled[0] = (residual_rows * inverse).astype(BF16)
         r.row_block[:, :, own_cols] = r.shards[...]
         r.cots[0] = r.cot[...]
         greet(
@@ -291,9 +280,10 @@
         for k in range(1, n_mp):
             line[k] = (copies.slot(), copies.slot())
             copies.start(r.small, own_small, (dp, flip_all(mp, k)), line[k][0])
+        across = copies.slot()
+        copies.start(r.scaled.at[0], r.scaled.at[1], neighbour, across)
         for k in range(1, n_mp):
             copies.start(r.shards, own_part, (dp, flip_all(mp, k)), line[k][1])
-        across = copies.slot()
 
         def small_tree(chunk):
             first = pl.multiple_of(chunk * half, half)
@@ -314,19 +304,11 @@
         top = n_dp.bit_length() - 1
         for level in range(1, top + 1):
             run_level(small_trees, level)
-            if level < top:
-                run_level(cot_trees, level)
-        residual_rows = r.residual[...]
-        inverse = lax.rsqrt(jnp.mean(residual_rows * residual_rows, -1, keepdims=True) + NORM_EPS)
-        for number, gain in enumerate(gain_rows(r.small_all, 0)):
-            lanes = slice(number * 128, (number + 1) * 128)
-            r.normed[0, :, lanes] = (residual_rows[:, lanes] * inverse * gain).astype(BF16)
-        copies.start(r.normed.at[0], r.normed.at[1], neighbour, across)
-        run_level(cot_trees, top)
+            run_level(cot_trees, level)
         for k in range(1, n_mp):
             other = pl.multiple_of(flip_all(mp, k) * cols, cols)
             copies.wait(r.row_block.at[:, :, pl.ds(other, cols)], me, line[k][1])
-        copies.wait(r.normed.at[1], me, across)
+        copies.wait(r.scaled.at[1], me, across)
         copies.finish()
 
     return launch(
@@ -339,7 +321,7 @@
             small_all=(single(n_dp, n_mp, *small.shape), vmem()),
             row_block=(low(kinds, rows, n_mp * cols), vmem()),
             cots=(low(n_dp, tokens, width), vmem()),
-            normed=(low(2, tokens, width), vmem()),
+            scaled=(low(2, tokens, width), vmem()),
         ),
         {},
         n_copies,
@@ -355,7 +337,26 @@
                 one.send(j)
 
 
-def gather_rows(n_dp, groups, identity, row_block, cot):
+def send_experts(copies, me, span, packed, near, experts):
+    dp, mp = me
+    slots = {}
+    for i, expert in enumerate(experts):
+        for k in range(1, span):
+            slots[i, k] = copies.slot()
+            copies.start(
+                packed.at[expert], near[k - 1].at[i], (dp, flip_all(mp, k)), slots[i, k]
+            )
+    return slots
+
+
+def wait_experts(copies, me, near, slots):
+    for (i, k), slot in slots.items():
+        copies.wait(near[k - 1].at[i], me, slot)
+
+
+def gather_rows(n_dp, n_mp, groups, identity, row_block, cot, packed, experts):
+    span = n_mp // groups
+    n_experts = len(experts)
     kinds, rows, width = row_block.shape
     part_rows = rows // 2
 
@@ -363,12 +364,17 @@
         dp, mp = lax.axis_index("dp"), lax.axis_index("mp")
         me = (dp, mp)
         copies = Copies(r.send_sems, r.recv_sems)
-        neighbour = (dp, flip(mp, 1))
+        partner = (dp, flip_all(mp, span))
         r.full[:, pl.ds(pl.multiple_of(dp * rows, rows), rows), :] = r.row_block[...]
-        greet([(flip_all(dp, mask), mp) for mask in bits_of(n_dp)] + [neighbour] * (groups - 1))
+        greet(
+            [(flip_all(dp, mask), mp) for mask in bits_of(n_dp)]
+            + [partner] * (groups - 1)
+            + [(dp, flip_all(mp, k)) for k in range(1, span)]
+        )
         across = copies.slot()
         if groups > 1:
-            copies.start(r.cot, r.cot_other, neighbour, across)
+            copies.start(r.cot, r.cot_other, partner, across)
+        sent = send_experts(copies, me, span, r.packed, r.near, experts)
 
         def tree(part, order):
             def ref(j, mask=0):
@@ -383,15 +389,20 @@
         run_gathers(trees)
         if groups > 1:
             copies.wait(r.cot_other, me, across)
+        wait_experts(copies, me, r.near, sent)
         copies.finish()
 
     return launch(
         gather_weights,
         identity,
-        dict(row_block=(row_block, vmem()), cot=(cot, vmem())),
-        dict(full=(low(kinds, n_dp * rows, width), vmem()), cot_other=(low(*cot.shape), vmem())),
+        dict(row_block=(row_block, vmem()), cot=(cot, vmem()), packed=(packed, hbm())),
+        dict(
+            full=(low(kinds, n_dp * rows, width), vmem()),
+            cot_other=(low(*cot.shape), vmem()),
+            near=([low(n_experts, *packed.shape[1:]) for _ in range(1, span)], hbm()),
+        ),
         {},
-        2 * (n_dp - 1) + 1,
+        2 * (n_dp - 1) + 1 + n_experts * (span - 1),
         32 << 20,
     )
 
@@ -477,12 +488,15 @@
 
 
 def attention_forward(
-    n_dp, groups, shared, identity, residual, normed, full, gain_two, router, places, cot_other, rotary
+    n_dp, n_mp, groups, identity, residual, scaled, full, gains, router, places, cot_other, rotary, packed, experts
 ):
     tokens, width = residual.shape
     query_rotary, own_rotary, other_rotary = rotary
     n_heads = width // 128
-    n_copies = 2 * (n_dp - 1)
+    span = n_mp // groups
+    owned = EXPERTS // n_dp
+    n_experts = len(experts)
+    n_copies = 2 * (n_dp - 1) + n_experts * (span - 1)
 
     def attention(r):
         dp, mp = lax.axis_index("dp"), lax.axis_index("mp")
@@ -495,11 +509,20 @@
         for copy in loads:
             copy.start()
         r.cots[0] = r.cot_other[...]
-        greet([(flip_all(dp, mask), mp) for mask in bits_of(n_dp)])
+        greet(
+            [(flip_all(dp, mask), mp) for mask in bits_of(n_dp)]
+            + [(dp, flip_all(mp, k)) for k in range(1, span)]
+        )
+        sent = send_experts(copies, me, span, r.packed, r.near, experts)
         trees = row_trees(copies, n_dp, me, r.cots) if groups > 1 else []
         for one in trees:
             one.send(0)
         top = n_dp.bit_length() - 1
+        residual = r.residual[...]
+        inverse = lax.rsqrt(jnp.mean(residual * residual, -1, keepdims=True) + NORM_EPS)
+        gain_one = r.gains[0:1, :]
+        r.normed[0] = (residual * inverse * gain_one).astype(BF16)
+        r.normed[1] = (r.scaled[1].astype(F32) * gain_one).astype(BF16)
         loads[0].wait()
         r.q[...] = dot(r.normed[0], r.weights[0], NN)
         loads[1].wait()
@@ -529,7 +552,7 @@
         hidden = r.residual[...] + dot(r.context[...], r.weights[2], NT)
         r.hidden[...] = hidden
         inverse = lax.rsqrt(jnp.mean(hidden * hidden, -1, keepdims=True) + NORM_EPS)
-        normed = (hidden * inverse * r.gain_two[...]).astype(BF16)
+        normed = (hidden * inverse * r.gains[1:2, :]).astype(BF16)
         r.normed_two[...] = normed
         logits = dot(normed, r.router[...], NN)
         lane = lax.broadcasted_iota(jnp.int32, logits.shape, 1)
@@ -539,8 +562,9 @@
         turned = probs.T
         r.table[...] = r.places[...]
         for expert in range(EXPERTS):
-            owner, which = divmod(expert, groups * shared)
-            r.table[owner, which % groups, 4 + which // groups, :] = turned[expert]
+            owner, which = divmod(expert, owned)
+            r.table[owner, 4 + which, :] = turned[expert]
+        wait_experts(copies, me, r.near, sent)
         copies.finish()
 
     return launch(
@@ -548,9 +572,10 @@
         identity,
         dict(
             residual=(residual, vmem()),
-            normed=(normed, vmem()),
+            scaled=(scaled, vmem()),
             full=(full, hbm()),
-            gain_two=(gain_two, vmem()),
+            gains=(gains, vmem()),
+            packed=(packed, hbm()),
             router=(router, vmem()),
             places=(places, vmem()),
             cot_other=(cot_other, vmem()),
@@ -560,6 +585,8 @@
         ),
         dict(
             cots=(low(n_dp, tokens, width), vmem()),
+            near=([low(n_experts, *packed.shape[1:]) for _ in range(1, span)], hbm()),
+            normed=(low(2, tokens, width), vmem()),
             queries=(low(tokens, width), vmem()),
             keyval=(low(2, tokens, width), vmem()),
             context=(low(tokens, width), vmem()),
@@ -579,7 +606,7 @@
     )
 
 
-def attention_backward(n_dp, n_mp, groups, shared, identity, given, first_row):
+def attention_backward(n_dp, n_mp, groups, identity, given, first_row):
     tokens, width = given.residual.shape
     n_heads = width // 128
     n_devices = n_dp * n_mp
@@ -588,7 +615,10 @@
     rows, cols = width // n_dp, width // n_mp
     part_rows = rows // 2
     orders = orders_of(n_dp)
-    n_copies = (2 * groups + 7) * (n_dp - 1) + 1 + 5 * (n_mp - 1) + 1
+    span = n_mp // groups
+    owned = EXPERTS // n_dp
+    n_late = given.late[0].shape[0] if given.late else 0
+    n_copies = (2 * groups + 7) * (n_dp - 1) + 1 + 4 * (n_mp - 1) + 1 + n_late * (span - 1)
 
     rooms, across_room = reduce_rooms(groups, n_dp, tokens, width, BF16)
 
@@ -607,24 +637,33 @@
             [(flip_all(dp, mask), mp) for mask in bits_of(n_dp)]
             + [(dp, flip_all(mp, k)) for k in range(1, n_mp)]
         )
-        mixture = TokenReduce(copies, n_dp, me, r.terms, r.rooms, r.across)
+        partner = (dp, flip_all(mp, span))
+        mixture = TokenReduce(copies, n_dp, me, partner, r.terms, r.rooms, r.across)
         for group in range(groups)[::-1]:
             for j in range(1, n_dp, 2):
                 mixture.first(group, j)
         last = mixture.last
-        travels = {k: copies.slot() for k in range(1, n_mp)}
-
-        def send_expert(k):
-            copies.start(
-                r.expert_grads[k - 1], r.arrived[k - 1], (dp, flip_all(mp, k)), travels[k]
-            )
-
-        for k in range(2, n_mp):
-            send_expert(k)
+        travels = {}
+
+        def send_late(i):
+            if i < n_late:
+                for k in range(1, span):
+                    travels[i, k] = copies.slot()
+                    copies.start(
+                        r.late[k - 1].at[i],
+                        r.arrived[k - 1].at[i],
+                        (dp, flip_all(mp, k)),
+                        travels[i, k],
+                    )
+
+        send_late(0)
         r.turned[...] = jnp.zeros_like(r.turned)
         for expert in range(EXPERTS):
-            owner, which = divmod(expert, groups * shared)
-            r.turned[expert, :] = r.gate_parts[owner, which % groups, which // groups, :]
+            owner, which = divmod(expert, owned)
+            parts = r.gate_parts[owner, 0, which, :]
+            for group in range(1, groups):
+                parts = parts + r.gate_parts[owner, group, which, :]
+            r.turned[expert, :] = parts
         grad_probs = r.turned[...].T
         probs = r.probs[...]
         grad_logits = (
@@ -634,7 +673,7 @@
         r.grad_router[...] = dot(r.normed_two[...], grad_logits, TN)
         hidden = r.hidden[...]
         inverse = lax.rsqrt(jnp.mean(hidden * hidden, -1, keepdims=True) + NORM_EPS)
-        scaled = r.gain_two[...] * grad_normed_two
+        scaled = r.gains[1:2, :] * grad_normed_two
         grad_hidden = (
             r.cotangent[...]
             + inverse * scaled
@@ -729,7 +768,8 @@
             if step == loops - 1:
                 across = copies.slot()
                 copies.start(r.swap.at[0], r.swap.at[1], neighbour, across)
-                send_expert(1)
+                for i in range(1, n_late):
+                    send_late(i)
             for stage in stages.pop(0):
                 stage()
         for stage in sum(stages, []):
@@ -756,7 +796,7 @@
         grad_normed = r.grad_normed[...] + dot(r.grad_kv_low[...], r.weights[1], NT)
         residual = r.residual[...]
         inverse = lax.rsqrt(jnp.mean(residual * residual, -1, keepdims=True) + NORM_EPS)
-        scaled = r.gain_one[...] * grad_normed
+        scaled = r.gains[0:1, :] * grad_normed
         r.input_grad[...] = (
             r.grad_hidden[...]
             + inverse * scaled
@@ -815,8 +855,7 @@
         for k in range(1, n_mp):
             copies.wait(r.small_line.at[k], me, sent[k])
             r.small_shard[...] += r.small_line[k]
-        for k in range(1, n_mp):
-            copies.wait(r.arrived[k - 1], me, travels[k])
+        wait_experts(copies, me, r.arrived, travels)
         copies.finish()
 
     return launch(
@@ -824,7 +863,7 @@
         identity,
         dict(
             full=(given.full, hbm()),
-            expert_grads=(given.expert_grads, hbm()),
+            late=(given.late, hbm()),
             residual=(given.residual, vmem()),
             hidden=(given.hidden, vmem()),
             cotangent=(given.cotangent, vmem()),
@@ -837,8 +876,7 @@
             queries=(given.queries, vmem()),
             keyval=(given.keyval, vmem()),
             context=(given.context, vmem()),
-            gain_one=(given.gain_one, vmem()),
-            gain_two=(given.gain_two, vmem()),
+            gains=(given.gains, vmem()),
             router=(given.router, vmem()),
             query_rotary=(given.rotary[0], vmem()),
             own_rotary=(given.rotary[1], vmem()),
@@ -846,7 +884,7 @@
         dict(
             input_grad=(single(tokens, width), vmem()),
             block_out=(single(tokens, width), vmem()),
-            arrived=([low(*grad.shape) for grad in given.expert_grads], hbm()),
+            arrived=([low(*grad.shape) for grad in given.late], hbm()),
             shards=(single(3, rows, cols), vmem()),
             small_shard=(single(first_row + own_router, 128), vmem()),
         ),
@@ -878,10 +916,9 @@
 
 
 class TokenReduce:
-    def __init__(self, copies, n_dp, me, terms, rooms, across):
-        dp, mp = me
+    def __init__(self, copies, n_dp, me, partner, terms, rooms, across):
         self.copies, self.me, self.across = copies, me, across
-        self.partner = (dp, flip(mp, 1))
+        self.partner = partner
         self.tokens = terms.shape[2]
         self.n_dp = n_dp
         self.last = n_dp.bit_length() - 2
@@ -947,84 +984,31 @@
     ]
 
 
-def run_expert(n_dp, n_mp, groups, identity, index, shared, parts, inputs):
-    first, last = index == 0, index == shared - 1
-    hidden, width = parts[0].shape[1:]
-    units = n_mp * hidden
+def run_experts(n_dp, n_mp, groups, identity, rows, table, cots, packed, near):
+    owned, _, hidden, width = packed.shape
+    span = n_mp // groups
+    units = span * hidden
     blocks = groups * n_dp
     slots = blocks * CAP
-    tokens = inputs.rows.shape[0]
+    tokens = rows.shape[0]
     per_tile = 4
     tile = per_tile * CAP
-    ins = dict(part=(parts, hbm()))
-    outs = dict(grad=([low(3, hidden, width) for _ in range(n_mp)], vmem()))
-    scratch = dict(
-        weights=pltpu.VMEM((3, units, width), BF16),
-        act=pltpu.VMEM((slots, units), BF16),
-        pair=pltpu.VMEM((slots, 2 * units), BF16),
-        grad_rows=pltpu.VMEM((slots, width), BF16),
-        part_sems=pltpu.SemaphoreType.DMA((3 * n_mp,)),
-    )
-    n_copies = 1
-    slot_rows = pltpu.VMEM((slots, width), BF16)
-    if first:
-        n_copies += blocks + 2 * groups * (n_dp - 1)
-        ins |= dict(
-            rows=(inputs.rows, hbm()), own_table=(inputs.table, hbm()), cots=(inputs.cots, hbm())
-        )
-        scratch |= dict(
-            tokens_all=pltpu.VMEM((groups, n_dp, tokens, width), BF16),
-            x_own=slot_rows,
-            c_own=slot_rows,
-            cot=pltpu.VMEM((2, tokens, width), BF16),
-            cot_sems=pltpu.SemaphoreType.DMA((2,)),
-            keep_sems=pltpu.SemaphoreType.DMA((2,)),
-        )
-    else:
-        ins |= dict(
-            tables_in=(inputs.tables, vmem()),
-            gates_in=(inputs.gates, vmem()),
-            x_in=(inputs.x[index], vmem()),
-            c_in=(inputs.c[index], vmem()),
-        )
-    if first and last:
-        scratch |= dict(tables=pltpu.VMEM((blocks, 8, tokens), F32))
-    elif first:
-        rest = [low(slots, width) for _ in range(1, shared)]
-        outs |= dict(tables=(single(blocks, 8, tokens), vmem()))
-        outs |= dict(x=(rest, vmem()), c=(rest, vmem()))
-    if last:
-        n_copies += 2 * groups * (n_dp - 1) + blocks
-        ins |= dict(y_before=(inputs.y, vmem()), d_before=(inputs.d, vmem()))
-        outs |= dict(
-            terms=(low(groups, n_dp, tokens, width), hbm()),
-            gate_parts=(single(n_dp, groups, 8, tokens), hbm()),
-            total=(single(tokens, width), vmem()),
-        )
-        rooms, across_room = reduce_rooms(groups, n_dp, tokens, width, BF16)
-        scratch |= dict(
-            gates=pltpu.VMEM((blocks, 8, tokens), F32),
-            y=slot_rows,
-            d=slot_rows,
-            grads_all=pltpu.VMEM((groups, n_dp, tokens, width), BF16),
-            sums=pltpu.VMEM((2, tokens, width), BF16),
-            sum_sems=pltpu.SemaphoreType.DMA((2,)),
-            gate_sem=pltpu.SemaphoreType.DMA((1,)),
-            rooms=rooms,
-            across=across_room,
-        )
-    else:
-        outs |= dict(
-            gates=(single(blocks, 8, tokens), vmem()),
-            y=(low(slots, width), vmem()),
-            d=(low(slots, width), vmem()),
-        )
-
-    def expert(r):
+    n_tiles = blocks // per_tile
+    here = [expert for experts, _ in near for expert in experts]
+    coming = [expert for expert in range(owned) if expert not in here]
+    n_sent = min(owned, 2)
+    n_late = owned - n_sent
+    n_copies = groups + 2 * (blocks - 1) + 4 * groups * (n_dp - 1)
+    n_copies += (len(coming) + n_sent) * (span - 1)
+    order = []
+    for group in range(groups):
+        for level in range(n_dp.bit_length()):
+            order += [(group, j) for j in range(n_dp) if bin(j).count("1") == level]
+
+    def experts(r):
         dp, mp = lax.axis_index("dp"), lax.axis_index("mp")
         me = (dp, mp)
-        other = flip(mp, 1)
-        kind = lax.rem(mp, groups)
+        other = flip_all(mp, span)
         copies = Copies(r.send_sems, r.recv_sems)
         peers = {
             (group, j): (flip_all(dp, j), other if group else mp)
@@ -1032,228 +1016,298 @@
             for j in range(n_dp)
             if group + j
         }
-        weights, act, pair, grad_rows = r.weights, r.act, r.pair, r.grad_rows
+        local = iter(range(n_loads))
+
+        def load(source, target):
+            copy = pltpu.make_async_copy(source, target, r.load_sems.at[next(local)])
+            copy.start()
+            return copy
+
+        def units_of(k):
+            return pl.ds(k * hidden, hidden)
+
+        own_table = load(r.own_table.at[dp], r.tables.at[0])
+        own_rows = load(r.rows, r.rows_all.at[0, 0])
         loads = [
-            pltpu.make_async_copy(
-                r.part[k].at[c],
-                weights.at[c, pl.ds(k * hidden, hidden)],
-                r.part_sems.at[3 * k + c],
+            [load(r.packed.at[e], r.weights.at[e, :, units_of(0)])] for e in range(owned)
+        ]
+        for number, (some, _) in enumerate(near):
+            for i, e in enumerate(some):
+                for k in range(1, span):
+                    source = r.near[number * (span - 1) + k - 1].at[i]
+                    loads[e].append(load(source, r.weights.at[e, :, units_of(k)]))
+
+        def cot_copy(number):
+            group, j = order[number]
+            return pltpu.make_async_copy(
+                r.cots[group].at[j], r.cot.at[number % 2], r.cot_sems.at[number % 2]
             )
-            for k in range(n_mp)
-            for c in range(3)
-        ]
-        for copy in loads:
-            copy.start()
-        tables = r.tables if first else r.tables_in
-        x_refs = {index: r.x_own if first else r.x_in}
-        c_refs = {index: r.c_own if first else r.c_in}
-        if first:
-            x_refs |= {i + 1: ref for i, ref in enumerate(r.x if shared > 1 else [])}
-            c_refs |= {i + 1: ref for i, ref in enumerate(r.c if shared > 1 else [])}
-
-        def hits(block, experts):
+
+        cot_copy(0).start()
+        greet(list(peers.values()) + [(dp, flip_all(mp, k)) for k in range(1, span)])
+        if groups > 1:
+            across = copies.slot()
+            copies.start(r.rows, r.rows_all.at[1, 0], peers[1, 0], across)
+        sent = {}
+        for (group, j), device in peers.items():
+            sent[group, j] = copies.slot()
+            copies.start(
+                r.own_table.at[device[0]],
+                r.tables.at[order.index((group, j))],
+                device,
+                sent[group, j],
+            )
+        trees = [row_trees(copies, n_dp, me, r.rows_all.at[group]) for group in range(groups)]
+        own_rows.wait()
+        for tree in trees[0]:
+            tree.send(0)
+        own_table.wait()
+
+        def hits(number, some):
             slot = lax.broadcasted_iota(jnp.int32, (CAP, tokens), 0).astype(F32)
-            found = [slot == tables[block, pl.ds(i, 1), :] for i in experts]
+            found = [slot == r.tables[number, pl.ds(i, 1), :] for i in some]
             return found[0] if len(found) == 1 else jnp.concatenate(found, 0)
 
-        def rows_of(block):
-            return pl.ds(pl.multiple_of(block * CAP, 16), CAP)
-
-        if first:
-            rows_all, cots = r.tokens_all, r.cots
-            keep = [
-                pltpu.make_async_copy(r.rows, rows_all.at[0, 0], r.keep_sems.at[0]),
-                pltpu.make_async_copy(
-                    r.own_table.at[dp, kind], tables.at[0], r.keep_sems.at[1]
-                ),
-            ]
-            for copy in keep:
-                copy.start()
-            order = [(group, 0) for group in range(groups)]
-            for level in range(1, n_dp.bit_length()):
-                for group in range(groups):
-                    order += [(group, j) for j in range(n_dp) if bin(j).count("1") == level]
-
-            def cot_copy(number):
-                group, j = order[number]
-                return pltpu.make_async_copy(
-                    cots[group].at[j], r.cot.at[number % 2], r.cot_sems.at[number % 2]
-                )
-
-            cot_copy(0).start()
-            greet(list(peers.values()))
-            across = copies.slot()
-            if groups > 1:
-                copies.start(r.rows, rows_all.at[1, 0], peers[1, 0], across)
-            sent = {}
-            for key, device in peers.items():
-                sent[key] = copies.slot()
-                group, j = key
-                copies.start(
-                    r.own_table.at[device[0], lax.rem(device[1], groups)],
-                    tables.at[group * n_dp + j],
-                    device,
-                    sent[key],
-                )
-            trees = [row_trees(copies, n_dp, me, rows_all.at[group]) for group in range(groups)]
-            keep[0].wait()
-            for tree in trees[0]:
-                tree.send(0)
-            keep[1].wait()
-
-            def fill(number):
-                group, j = order[number]
-                block = group * n_dp + j
-                if number:
-                    copies.wait(tables.at[block], me, sent[group, j])
-                if number + 1 < blocks:
-                    cot_copy(number + 1).start()
-                pick = hits(block, range(shared)).astype(BF16)
-                found = dot(pick, rows_all[group, j], NN).astype(BF16)
-                for i in range(shared):
-                    x_refs[i][block * CAP : (block + 1) * CAP, :] = found[i * CAP : (i + 1) * CAP]
-                cot_copy(number).wait()
-                found = dot(pick, r.cot[number % 2], NN).astype(BF16)
-                for i in range(shared):
-                    c_refs[i][block * CAP : (block + 1) * CAP, :] = found[i * CAP : (i + 1) * CAP]
-
-            for number, (group, j) in enumerate(order):
-                if j:
-                    for tree in sorted(trees[group], key=lambda tree: place_of(tree.order, j)):
-                        tree.receive(j)
-                        tree.send(j)
-                elif group:
-                    copies.wait(rows_all.at[1, 0], me, across)
-                    for tree in trees[1]:
-                        tree.send(0)
-                fill(number)
-        else:
-            greet(list(peers.values()))
-        if last:
-            gates = r.gates
-            if index:
-                gates[...] = r.gates_in[...]
-        else:
-            gates = r.gates
-        for copy in loads:
-            copy.wait()
-        x_all, c_all = x_refs[index], c_refs[index]
-        y_all, d_all = r.y, r.d
-
-        def work(step, carry):
+        def fill(number):
+            group, j = order[number]
+            if number:
+                copies.wait(r.tables.at[number], me, sent[group, j])
+            if number + 1 < blocks:
+                cot_copy(number + 1).start()
+            pick = hits(number, range(owned)).astype(BF16)
+            there = slice(number * CAP, (number + 1) * CAP)
+            found = dot(pick, r.rows_all[group, j], NN).astype(BF16)
+            for i in range(owned):
+                r.x[i + 1, there, :] = found[i * CAP : (i + 1) * CAP]
+            cot_copy(number).wait()
+            found = dot(pick, r.cot[number % 2], NN).astype(BF16)
+            for i in range(owned):
+                r.y[i, there, :] = found[i * CAP : (i + 1) * CAP]
+
+        def work(e, step):
             rows = pl.ds(pl.multiple_of(step * tile, 16), tile)
-            x = x_all[rows, :]
-            gate = dot(x, weights[0], NT)
-            up = dot(x, weights[1], NT)
+            x = r.x[e + 1, rows, :]
+            gate = dot(x, r.weights[e, 0], NT)
+            up = dot(x, r.weights[e, 1], NT)
             sigmoid = 1.0 / (1.0 + jnp.exp(-gate))
             silu = gate * sigmoid
             activation = (silu * up).astype(BF16)
-            act[rows, :] = activation
-            made = dot(activation, weights[2], NN)
-            cot = c_all[rows, :].astype(F32)
-            chosen, scores = [], []
+            r.act[rows, :] = activation
+            made = dot(activation, r.weights[e, 2], NN)
+            cot = r.y[e, rows, :].astype(F32)
+            chosen = []
             dots = jnp.sum(cot * made, -1, keepdims=True)
             for b in range(per_tile):
-                block = step * per_tile + b
-                hit = hits(block, (index,))
-                chance = tables[block, pl.ds(4 + index, 1), :]
+                number = step * per_tile + b
+                hit = hits(number, (e,))
+                chance = r.tables[number, pl.ds(4 + e, 1), :]
                 chosen.append(jnp.sum(jnp.where(hit, chance, 0.0), -1, keepdims=True))
-                here = dots[b * CAP : (b + 1) * CAP]
-                gates[block, pl.ds(index, 1), :] = jnp.sum(
-                    jnp.where(hit, here, 0.0), 0, keepdims=True
+                mine = dots[b * CAP : (b + 1) * CAP]
+                r.gates[number, pl.ds(e, 1), :] = jnp.sum(
+                    jnp.where(hit, mine, 0.0), 0, keepdims=True
                 )
             share = jnp.concatenate(chosen, 0)
-            y_all[rows, :] = (share * made).astype(BF16)
+            r.y[e, rows, :] = (share * made).astype(BF16)
             back = (share * cot).astype(BF16)
-            grad_rows[rows, :] = back
-            grad_act = dot(back, weights[2], NT)
+            r.back[rows, :] = back
+            grad_act = dot(back, r.weights[e, 2], NT)
             grad_gate = grad_act * up * sigmoid * (1.0 + gate * (1.0 - sigmoid))
             grad_gate = grad_gate.astype(BF16)
             grad_up = (grad_act * silu).astype(BF16)
-            pair[rows, pl.ds(0, units)] = grad_gate
-            pair[rows, pl.ds(units, units)] = grad_up
-            d_all[rows, :] = (dot(grad_gate, weights[0], NN) + dot(grad_up, weights[1], NN)).astype(
-                BF16
+            r.pair[rows, pl.ds(0, units)] = grad_gate
+            r.pair[rows, pl.ds(units, units)] = grad_up
+            found = dot(grad_gate, r.weights[e, 0], NN) + dot(grad_up, r.weights[e, 1], NN)
+            r.x[e, rows, :] = found.astype(BF16)
+
+        def ready(e):
+            for copy in loads[e]:
+                copy.wait()
+            if e in coming:
+                for k in range(1, span):
+                    copies.wait(r.weights.at[e, :, units_of(k)], me, weights_sent[e, k])
+
+        stores = []
+
+        def weight_grad(e):
+            for c in range(3):
+                source = r.act[...] if c == 2 else r.pair[:, pl.ds(c * units, units)]
+                rhs = r.back[...] if c == 2 else r.x[e + 1]
+                r.weights[e, c] = dot(source, rhs, TN).astype(BF16)
+            stores.append(load(r.weights.at[e, :, units_of(0)], r.grad_own.at[e]))
+            for k in range(1, span):
+                source = r.weights.at[e, :, units_of(k)]
+                if e < n_sent:
+                    grads_sent[e, k] = copies.slot()
+                    copies.start(
+                        source, r.arrived[k - 1].at[e], (dp, flip_all(mp, k)), grads_sent[e, k]
+                    )
+                else:
+                    stores.append(load(source, r.late[k - 1].at[e - n_sent]))
+
+        weights_sent, grads_sent = {}, {}
+        ready(0)
+        done = 0
+        for number, (group, j) in enumerate(order):
+            if j:
+                for tree in sorted(trees[group], key=lambda tree: place_of(tree.order, j)):
+                    tree.receive(j)
+                    tree.send(j)
+            elif group:
+                copies.wait(r.rows_all.at[1, 0], me, across)
+                for tree in trees[1]:
+                    tree.send(0)
+            if group == groups - 1 and j == 0:
+                for e in coming:
+                    for k in range(1, span):
+                        weights_sent[e, k] = copies.slot()
+                        copies.start(
+                            r.packed.at[e],
+                            r.weights.at[e, :, units_of(k)],
+                            (dp, flip_all(mp, k)),
+                            weights_sent[e, k],
+                        )
+            fill(number)
+            if number % per_tile == per_tile - 1 and number < blocks - 1:
+                work(0, done)
+                done += 1
+        work(0, done)
+        weight_grad(0)
+
+        def tiles(e, first, end):
+            def step(at, carry):
+                work(e, at)
+                return carry
+
+            lax.fori_loop(first, end, step, 0)
+
+        for e in range(1, owned - 1):
+            ready(e)
+            tiles(e, 0, n_tiles)
+            weight_grad(e)
+        copies.finish()
+        partner = (dp, other)
+        reduce = TokenReduce(copies, n_dp, me, partner, r.rows_all, r.rooms, r.across)
+        last = owned - 1
+        if last:
+            ready(last)
+        scattered = []
+
+        def sum_copy(at):
+            group, j = scattered[at]
+            return pltpu.make_async_copy(
+                r.sums.at[at % 2], r.terms.at[group, j], r.sum_sems.at[at % 2]
             )
-            return carry
-
-        lax.fori_loop(0, blocks // per_tile, work, 0)
-
-        def weight_grad(k):
-            x, back = x_all[...], grad_rows[...]
-            for c, source in enumerate((pair, pair, act)):
-                columns = pl.ds(k * hidden + (units if c == 1 else 0), hidden)
-                rhs = back if c == 2 else x
-                r.grad[k][c] = dot(source[:, columns], rhs, TN).astype(BF16)
-
-        if not last:
-            for k in range(n_mp):
-                weight_grad(k)
-        else:
-            y_refs = r.y_before + [y_all]
-            d_refs = r.d_before + [d_all]
-            reduce = TokenReduce(copies, n_dp, me, r.grads_all, r.rooms, r.across)
-            back = range(groups)[::-1]
-            order = [(g, j) for g in back for j in range(1, n_dp, 2)]
-            order += [(g, j) for g in back for j in range(0, n_dp, 2)]
-
-            def sum_copy(number):
-                group, j = order[number]
-                return pltpu.make_async_copy(
-                    r.sums.at[number % 2], r.terms.at[group, j], r.sum_sems.at[number % 2]
+
+        own_gates = pltpu.make_async_copy(r.gates.at[0], r.gate_parts.at[dp, 0], r.gate_sem.at[0])
+        gates_sent = {}
+
+        def scatter(group, j):
+            number = order.index((group, j))
+            if number:
+                gates_sent[group, j] = copies.slot()
+                copies.start(
+                    r.gates.at[number],
+                    r.gate_parts.at[dp, group],
+                    peers[group, j],
+                    gates_sent[group, j],
                 )
-
-            sent = {}
-            own_gates = pltpu.make_async_copy(
-                gates.at[0], r.gate_parts.at[dp, kind], r.gate_sem.at[0]
-            )
-            own_gates.start()
-            for number, (group, j) in enumerate(order):
-                block = group * n_dp + j
-                if group + j:
-                    sent[group, j] = copies.slot()
-                    copies.start(
-                        gates.at[block],
-                        r.gate_parts.at[dp, kind],
-                        peers[group, j],
-                        sent[group, j],
-                    )
-                pick = hits(block, range(shared)).astype(BF16)
-                there = rows_of(block)
-                found = jnp.concatenate([ref[there, :] for ref in d_refs], 0)
-                r.grads_all[group, j] = dot(pick, found, TN).astype(BF16)
-                if j % 2:
-                    reduce.first(group, j)
-                found = jnp.concatenate([ref[there, :] for ref in y_refs], 0)
-                if number > 1:
-                    sum_copy(number - 2).wait()
-                r.sums[number % 2] = dot(pick, found, TN).astype(BF16)
-                sum_copy(number).start()
-            left = list(range(n_mp))
-
-            def some(count):
-                for _ in range(count):
-                    if left:
-                        weight_grad(left.pop(0))
-
-            for p in range(reduce.last - 1, -1, -1):
+            else:
+                own_gates.start()
+            there = slice(number * CAP, (number + 1) * CAP)
+            pick = hits(number, range(owned)).astype(BF16)
+            found = jnp.concatenate([r.x[e, there, :] for e in range(owned)], 0)
+            r.rows_all[group, j] = dot(pick, found, TN).astype(BF16)
+            if j % 2:
+                reduce.first(group, j)
+            found = jnp.concatenate([r.y[e, there, :] for e in range(owned)], 0)
+            at = len(scattered)
+            scattered.append((group, j))
+            if at > 1:
+                sum_copy(at - 2).wait()
+            r.sums[at % 2] = dot(pick, found, TN).astype(BF16)
+            sum_copy(at).start()
+
+        halves = [
+            (n_tiles * group // groups, n_tiles * (group + 1) // groups) for group in range(groups)
+        ]
+        levels = list(range(reduce.last - 1, -1, -1))
+        for group in range(groups)[::-1]:
+            first, end = halves[group]
+            if last == 0:
+                pass
+            elif group == groups - 1:
+                tiles(last, first, end)
+            else:
+                for at in range(first, end):
+                    tiles(last, at, at + 1)
+                    if levels:
+                        reduce.level(1, levels.pop(0))
+            for j in [j for j in range(n_dp) if j % 2] + [j for j in range(n_dp) if j % 2 == 0]:
+                scatter(group, j)
+        if groups > 1:
+            for p in levels:
                 reduce.level(1, p)
-                some(1)
-            reduce.pass_on()
-            for p in range(reduce.last - 1, -1, -1):
-                reduce.level(0, p)
-                some(1)
-            some(n_mp)
-            reduce.end(r.total)
-            for number in (blocks - 2, blocks - 1):
-                sum_copy(number).wait()
-            own_gates.wait()
-            for (group, j), device in peers.items():
-                theirs = 1 - kind if group else kind
-                copies.wait(r.gate_parts.at[device[0], theirs], me, sent[group, j])
+        reduce.pass_on()
+        for p in range(reduce.last - 1, -1, -1):
+            reduce.level(0, p)
+            if p == reduce.last - 1 and last:
+                weight_grad(last)
+        reduce.end(r.total)
+        for at in (blocks - 2, blocks - 1):
+            sum_copy(at).wait()
+        own_gates.wait()
+        for (group, j), device in peers.items():
+            copies.wait(r.gate_parts.at[device[0], group], me, gates_sent[group, j])
+        for (e, k), slot in grads_sent.items():
+            copies.wait(r.arrived[k - 1].at[e], me, slot)
+        for copy in stores:
+            copy.wait()
         copies.finish()
 
-    return launch(expert, identity, ins, outs, scratch, n_copies, 60 << 20)
+    n_loads = 2 + owned * span + owned * span
+    near_refs = [part for _, parts in near for part in parts]
+    weights = packed.shape[1:]
+    rooms, across_room = reduce_rooms(groups, n_dp, tokens, width, BF16)
+    return launch(
+        experts,
+        identity,
+        dict(
+            rows=(rows, hbm()),
+            own_table=(table, hbm()),
+            cots=(cots, hbm()),
+            packed=(packed, hbm()),
+            near=(near_refs, hbm()),
+        ),
+        dict(
+            terms=(low(groups, n_dp, tokens, width), hbm()),
+            gate_parts=(single(n_dp, groups, 8, tokens), hbm()),
+            total=(single(tokens, width), vmem()),
+            grad_own=(low(owned, *weights), hbm()),
+            arrived=([low(n_sent, *weights) for _ in range(1, span)], hbm()),
+            late=([low(n_late, *weights) for _ in range(1, span) if n_late], hbm()),
+        ),
+        dict(
+            weights=pltpu.VMEM((owned, 3, units, width), BF16),
+            rows_all=pltpu.VMEM((groups, n_dp, tokens, width), BF16),
+            x=pltpu.VMEM((owned + 1, slots, width), BF16),
+            y=pltpu.VMEM((owned, slots, width), BF16),
+            act=pltpu.VMEM((slots, units), BF16),
+            pair=pltpu.VMEM((slots, 2 * units), BF16),
+            back=pltpu.VMEM((slots, width), BF16),
+            tables=pltpu.VMEM((blocks, 8, tokens), F32),
+            gates=pltpu.VMEM((blocks, 8, tokens), F32),
+            cot=pltpu.VMEM((2, tokens, width), BF16),
+            sums=pltpu.VMEM((2, tokens, width), BF16),
+            rooms=rooms,
+            across=across_room,
+            load_sems=pltpu.SemaphoreType.DMA((n_loads,)),
+            cot_sems=pltpu.SemaphoreType.DMA((2,)),
+            sum_sems=pltpu.SemaphoreType.DMA((2,)),
+            gate_sem=pltpu.SemaphoreType.DMA((1,)),
+        ),
+        n_copies,
+        63 << 20,
+    )
 
 
 def adamw(weight, gradient, moment_one, moment_two, rate_val, decay_val):
@@ -1301,12 +1355,9 @@
     mp = lax.axis_index("mp")
     place_in_all = lax.axis_index("dp") * n_mp + mp
     groups = 2 if 2 * n_dp <= 16 else 1
-    kind = mp % groups
     tokens = residual_in.shape[0]
     owned = gateup_w.shape[0]
-    shared = owned // groups
-    hidden_units = down_w.shape[1]
-    flips = [[(i, i ^ k) for i in range(n_mp)] for k in range(n_mp)]
+    span = n_mp // groups
     own_gain, own_router = attn_gain.shape[0], router_w.shape[0]
     first_row, lanes = 8, 128
     per_tile = lanes // own_gain
@@ -1326,9 +1377,12 @@
     cot_low = cotangent.astype(BF16)
     start = prologue(n_dp, n_mp, groups, 0, small, shards, cot_low, residual_in)
     small_all = start.small_all
-    gains = [
-        jnp.sum(small_all[:, :, row].reshape(-1, per_tile, lanes), 1).reshape(1, -1) for row in (0, 1)
-    ]
+    gains = jnp.concatenate(
+        [
+            jnp.sum(small_all[:, :, row].reshape(-1, per_tile, lanes), 1).reshape(1, -1)
+            for row in (0, 1)
+        ]
+    )
     router_low = small_all[:, :, first_row:].reshape(MODEL_WIDTH, lanes).astype(BF16)
 
     expert_range = jnp.arange(EXPERTS, dtype=jnp.int32)
@@ -1336,25 +1390,13 @@
     chosen = jnp.sum(onehot, 1)
     before = jnp.cumsum(chosen, 0) - chosen
     place = jnp.where(chosen > 0, before, -1)
-    by_owner = place.astype(F32).T.reshape(n_dp, shared, groups, tokens).transpose(0, 2, 1, 3)
-    places = jnp.pad(by_owner, ((0, 0), (0, 0), (0, 8 - shared), (0, 0)))
+    places = jnp.pad(
+        place.astype(F32).T.reshape(n_dp, owned, tokens), ((0, 0), (0, 8 - owned), (0, 0))
+    )
 
     packed = jnp.concatenate([gateup_w, down_w[:, None]], 1).astype(BF16)
-
-    def send_weights(i, after):
-        mine = theirs = packed[groups * i]
-        if groups > 1:
-            mine = jnp.where(kind == 0, packed[2 * i], packed[2 * i + 1])
-            theirs = jnp.where(kind == 0, packed[2 * i + 1], packed[2 * i])
-        mine, theirs, after = lax.optimization_barrier((mine, theirs, after))
-        parts = [mine] + [
-            lax.ppermute(theirs if k % 2 else mine, "mp", flips[k]) for k in range(1, n_mp)
-        ]
-        return parts, after
-
-    expert_parts = [None] * shared
-    expert_parts[0], row_block = send_weights(0, start.row_block)
-    whole = gather_rows(n_dp, groups, 1, row_block, cot_low)
+    early = [list(range(owned))[:1], list(range(owned))[1:3]]
+    whole = gather_rows(n_dp, n_mp, groups, 1, start.row_block, cot_low, packed, early[0])
     full = whole.full
 
     query_table, key_table = (jnp.asarray(table) for table in rotary_constants())
@@ -1365,74 +1407,59 @@
     ]
     front = attention_forward(
         n_dp,
+        n_mp,
         groups,
-        shared,
         2,
         residual_in,
-        start.normed,
+        start.scaled,
         full,
-        gains[1],
+        gains,
         router_low,
         places,
         whole.cot_other,
         rotary,
-    )
-
-    rows = front.normed_two
-    for i in range(1, shared):
-        expert_parts[i], (rows, expert_parts[i - 1]) = send_weights(i, (rows, expert_parts[i - 1]))
-    made = types.SimpleNamespace(
-        rows=rows, table=front.table, cots=[start.cots, front.cots][:groups], y=[], d=[]
-    )
-    expert_grads = []
-    for i in range(shared):
-        found = run_expert(n_dp, n_mp, groups, 3 + i, i, shared, expert_parts[i], made)
-        if i < shared - 1:
-            made.gates = found.gates
-            made.y, made.d = made.y + [found.y], made.d + [found.d]
-            if i == 0:
-                made.tables, made.x, made.c = found.tables, [None] + found.x, [None] + found.c
-        if i < shared - 1:
-            expert_grads.append(
-                found.grad[:1]
-                + [lax.ppermute(found.grad[k], "mp", flips[k]) for k in range(1, n_mp)]
-            )
-    total, expert_grads = lax.optimization_barrier((found.total, expert_grads))
+        packed,
+        early[1],
+    )
+
+    found = run_experts(
+        n_dp,
+        n_mp,
+        groups,
+        3,
+        front.normed_two,
+        front.table,
+        [start.cots, front.cots][:groups],
+        packed,
+        [(early[0], whole.near), (early[1], front.near)],
+    )
+
     given = types.SimpleNamespace(
         full=full,
         residual=residual_in,
         hidden=front.hidden,
         cotangent=cotangent,
-        total=total,
-        expert_grads=found.grad[1:],
+        total=found.total,
+        late=found.late,
         gate_parts=found.gate_parts,
         terms=found.terms,
         probs=front.probs,
-        normed=start.normed,
+        normed=front.normed,
         normed_two=front.normed_two,
         queries=front.queries,
         keyval=front.keyval,
         context=front.context,
-        gain_one=gains[0],
-        gain_two=gains[1],
+        gains=gains,
         router=router_low,
         rotary=rotary,
     )
-    back = attention_backward(n_dp, n_mp, groups, shared, 3 + shared, given, first_row)
+    back = attention_backward(n_dp, n_mp, groups, 4, given, first_row)
     input_grad, block_out = back.input_grad, back.block_out
-    expert_grads = expert_grads + [found.grad[:1] + back.arrived]
-    pairs = []
-    for i in range(shared):
-        if groups == 1:
-            pairs.append(sum(part.astype(F32) for part in expert_grads[i]))
-            continue
-        same = sum(part.astype(F32) for part in expert_grads[i][0::2])
-        turned = sum(part.astype(F32) for part in expert_grads[i][1::2])
-        pairs.append(jnp.where(kind == 0, same, turned))
-        pairs.append(jnp.where(kind == 0, turned, same))
-    expert_grad = jnp.stack(pairs)
+    expert_grad = found.grad_own.astype(F32)
+    for k in range(1, span):
+        parts = [found.arrived[k - 1]] + ([back.arrived[k - 1]] if back.arrived else [])
+        expert_grad += jnp.concatenate(parts).astype(F32)
     gateup_grad, down_grad = expert_grad[:, :2], expert_grad[:, 2]
-
     grads, small_grads = back.shards, back.small_shard
     query_grad, keyval_grad, output_grad = grads[0], grads[1], grads[2].T
     first_lane = (place_in_all % per_tile) * own_gain

time: 507 us -> 417 us (0.82)
  Pallas kernels: 407 us -> 355 us
  starting transfers between devices: 28.3 us -> 0 us
    pallas_call x6 -> x5, Pallas kernels: 407 us -> 355 us  [launch(): pl.pallas_call(body, out_shape=tuple(shapes), in_specs=in_specs, out_spec...]
    ppermute x9 -> x0, starting transfers between devices: 28.3 us -> none  [the longest x3 19.6 us: local(): lax.ppermute(found.grad[k], 'mp', flips[k])]
    unnamed x125 -> x109, local copies, waits for them, and re-layouts: 24.5 us -> 22.5 us
  transfers between devices with their start and end apart: 9 -> 0, of which waited for: 0 -> 0; matrix products, arithmetic and copies ran while one was open for 1% -> 0% of each run, Pallas kernels for 50% -> 0%
where the time goes in v4:
time: 417 us; the launch traced here: 412 us
  Pallas kernels  355 us (85%)
  other arithmetic  29.1 us (7%)
  local copies, waits for them, and re-layouts  26.5 us (6%)
    pallas_call x5, Pallas kernels, launch(): pl.pallas_call(body, out_shape=tuple(shapes), in_specs=in_specs, out_spec...  355 us
    unnamed x109, local copies, waits for them, and re-layouts  22.5 us
    sub x7, other arithmetic, adamw(): weight - rate_val * (first_hat / (jnp.sqrt(second_hat) + 1e-08) + decay_v...  16.4 us

profile of v4, /device:TPU:0, one launch (start us, length us, event | category | flops | bytes accessed | tf_op | source)
XLA Modules:
  0.0 411.7 jit_solution(10295457336612362435)
XLA Ops:
  3.2 1.0 copy.85
  4.2 1.0 convert_bitcast_fusion.2
  5.3 1.3 convert_element_type.25.refs_2_.refs_1_
  6.6 33.1 %gather_line.1 = (f32[8,4,40,128]{3,2,1,0:T(8,128)S(1)}, bf16[3,128,1024]{2,1,0:T(8,128)(2,1)S(1)}, bf16[8,256,1024]{2,1,0:T(8,128)(2,1)S(1)}, bf16[2,256,1024]{2,1,0:T(8,128)(2,1)S(1)}) custom-call(f32[40,128]{1,0:T(8,128)S(1)} %select_maximum_fusion.refs_0_, bf16[3,128,256]{2,1,0:T(8,128)(2,1)S(1)} %pad_maximum_fusion.1.refs_1_, ...), custom_call_target="tpu_custom_call" | custom-call | flops 1 | bytes 1 | tf_op jit(solution)/shard_map/gather_line/pallas_call | solution.py:225
  39.7 4.4 %convert.26 = bf16[4,2,128,1024]{3,2,1,0:T(8,128)(2,1)S(1)} convert(f32[4,2,128,1024]{3,2,1,0:T(8,128)} %param.38) | non-fusion elementwise | flops 1048576 | bytes 6291456 | tf_op jit(solution)/shard_map/convert.1
  44.9 31.9 %gather_weights.1 = (bf16[3,1024,1024]{2,1,0:T(8,128)(2,1)S(1)}, bf16[256,1024]{1,0:T(8,128)(2,1)S(1)}, bf16[1,3,128,1024]{3,2,1,0:T(8,128)(2,1)S(1)}) custom-call(bf16[3,128,1024]{2,1,0:T(8,128)(2,1)S(1)} %get-tuple-element.62.refs_0_, bf16[256,1024]{1,0:T(8,128)(2,1)S(1)} %convert_element_type.25.refs_2_.refs_1_, ...), custom_call_target="tpu_custom_call" | custom-call | flops 1 | bytes 1 | tf_op jit(solution)/shard_map/gather_weights/pallas_call | solution.py:225
  76.8 2.7 copy-done.1
  81.3 2.1 constant_dynamic-slice_fusion.2
  84.4 0.9 copy-done.5
  85.3 0.9 copy-done.6
  86.3 0.9 copy-done.11
  87.2 1.0 copy-done.14
  88.3 40.5 %attention.1 = (bf16[8,256,1024]{2,1,0:T(8,128)(2,1)}, bf16[2,3,128,1024]{3,2,1,0:T(8,128)(2,1)}, bf16[2,256,1024]{2,1,0:T(8,128)(2,1)S(1)}, bf16[256,1024]{1,0:...) custom-call(f32[256,1024]{1,0:T(8,128)} %refs_2_.1, ...), custom_call_target="tpu_custom_call" | custom-call | flops 1 | bytes 1 | tf_op jit(solution)/shard_map/attention/pallas_call | solution.py:225
  129.6 1.0 copy-done.9
  130.6 1.0 copy-done.10
  134.4 152.7 %experts.1 = (bf16[2,8,256,1024]{3,2,1,0:T(8,128)(2,1)}, f32[8,2,8,256]{3,2,1,0:T(8,128)}, f32[256,1024]{1,0:T(8,128)}, bf16[4,3,128,1024]{3,2,1,0:T(8,128)(2,1)...) custom-call(bf16[256,1024]{1,0:T(8,128)(2,1)} %copy-done.7, f32[8,8,256]{2,1,0:T(8,128)} %copy-done.19, ...), custom_call_target="tpu_custom_call" | custom-call | flops 1 | bytes 1 | tf_op jit(solution)/shard_map/experts/pallas_call | solution.py:225
  287.2 96.3 %attention_back.1 = (f32[256,1024]{1,0:T(8,128)}, f32[256,1024]{1,0:T(8,128)}, bf16[2,3,128,1024]{3,2,1,0:T(8,128)(2,1)}, f32[3,128,256]{2,1,0:T(8,128)}, f32[40,128]{1,0:T(8,128)}) custom-call(bf16[3,1024,1024]{2,1,0:T(8,128)(2,1)} %copy-done.1, bf16[2,3,128,1024]{3,2,1,0:T(8,128)(2,1)} %get-tuple-element.73.refs_1_, f32[256,1024]{1,0:T(8,128)} %refs_2_.1, ...), custom_call_target="tpu_custom_call" | custom-call | flops 1 | bytes 1 | tf_op jit(solution)/shard_map/attention_back/pallas_call | solution.py:225
  383.5 4.0 convert_add_fusion
  388.4 1.2 copy-done.24
  389.6 6.9 %multiply_subtract_fusion = (f32[4,2,128,1024]{3,2,1,0:T(8,128)}, f32[4,2,128,1024]{3,2,1,0:T(8,128)}, f32[4,2,128,1024]{3,2,1,0:T(8,128)}, f32[4,2,128,1024]{3,2,1,0:T(8,128)}) fusion(f32[4,2,128,1024]{3,2,1,0:T(8,128)S(1)} %copy-done.20, f32[4,2,128,1024]{3,2,1,0:T(8,128)S(1)} %copy-done.23, f32[4,2,128,1024]{3,2,1,0:T(8,128)S(1)} %copy-done.24, ...), kind=kLoop, calls=%fused_computation.3 | loop fusion | flops 15728640 | bytes 33554432 | tf_op jit(solution)/shard_map/sub | solution.py:1318
  396.6 6.5 %multiply_subtract_fusion.1 = (f32[4,128,1024]{2,1,0:T(8,128)}, f32[4,128,1024]{2,1,0:T(8,128)}, f32[4,128,1024]{2,1,0:T(8,128)}, f32[4,128,1024]{2,1,0:T(8,128)}) fusion(f32[4,128,1024]{2,1,0:T(8,128)S(1)} %copy-done.22, f32[4,128,1024]{2,1,0:T(8,128)} %param.54, f32[4,128,1024]{2,1,0:T(8,128)} %param.55, f32[4,3,128,1024]{3,2,1,0:T(8,128)S(1)} %convert_add_fusion), kind=kLoop, calls=%fused_computation.9 | loop fusion | flops 7864320 | bytes 16777216 | tf_op jit(solution)/shard_map/sub | solution.py:1318
  403.2 1.1 multiply_subtract_fusion.3
  409.6 1.0 copy.102
  410.6 1.0 copy.103
  (128 shorter events, 15.8 us)
Async XLA Ops:
  0.7 5.9 %copy-start.2 = (f32[256,1024]{1,0:T(8,128)S(1)}, f32[256,1024]{1,0:T(8,128)}, u32[]{:S(2)}) copy-start(f32[256,1024]{1,0:T(8,128)} %refs_2_.1) | copy-start | bytes 3145732
  4.2 39.9 %copy-start.26 = (f32[256,128]{0,1:T(8,128)}, f32[256,128]{0,1:T(8,128)S(1)}, u32[]{:S(2)}) copy-start(f32[256,128]{0,1:T(8,128)S(1)} %copy.85) | copy-start | bytes 393220
  44.8 38.5 %copy-start = (bf16[4,3,128,1024]{3,2,1,0:T(8,128)(2,1)}, bf16[4,3,128,1024]{3,2,1,0:T(8,128)(2,1)S(1)}, u32[]{:S(2)}) copy-start(bf16[4,3,128,1024]{3,2,1,0:T(8,128)(2,1)S(1)} %pad_maximum_fusion.refs_2_.refs_4_) | copy-start | bytes 9437188
  44.8 38.5 %copy-start.43 = (s32[256,8]{0,1:T(8,128)S(1)}, s32[256,8]{0,1:T(8,128)}, u32[]{:S(2)}) copy-start(s32[256,8]{0,1:T(8,128)} %param.31) | copy-start | bytes 24580
  81.2 47.6 %copy-start.18 = (f32[2,1024]{1,0:T(2,128)}, f32[2,1024]{1,0:T(2,128)S(1)}, u32[]{:S(2)}) copy-start(f32[2,1024]{1,0:T(2,128)S(1)} %pad_maximum_fusion.2.refs_3_.refs_14_) | copy-start | bytes 24580
  81.3 47.6 %copy-start.4 = (bf16[8,4,32,128]{3,2,1,0:T(8,128)(2,1)}, bf16[8,4,32,128]{3,2,1,0:T(8,128)(2,1)S(1)}, u32[]{:S(2)}) copy-start(bf16[8,4,32,128]{3,2,1,0:T(8,128)(2,1)S(1)} %slice.69) | copy-start | bytes 786436
  287.1 96.4 %copy-start.25 = (bf16[2,3,128,1024]{3,2,1,0:T(8,128)(2,1)S(1)}, bf16[2,3,128,1024]{3,2,1,0:T(8,128)(2,1)}, u32[]{:S(2)}) copy-start(bf16[2,3,128,1024]{3,2,1,0:T(8,128)(2,1)} %get-tuple-element.88) | copy-start | bytes 4718596
  383.5 6.1 %copy-start.24 = (f32[4,2,128,1024]{3,2,1,0:T(8,128)S(1)}, f32[4,2,128,1024]{3,2,1,0:T(8,128)}, u32[]{:S(2)}) copy-start(f32[4,2,128,1024]{3,2,1,0:T(8,128)} %param.53) | copy-start | bytes 12582916
  389.6 6.9 %copy-start.22 = (f32[4,128,1024]{2,1,0:T(8,128)S(1)}, f32[4,128,1024]{2,1,0:T(8,128)}, u32[]{:S(2)}) copy-start(f32[4,128,1024]{2,1,0:T(8,128)} %param.39) | copy-start | bytes 6291460
  396.5 6.7 %copy-start.30 = (f32[3,128,256]{2,1,0:T(8,128)S(1)}, f32[3,128,256]{2,1,0:T(8,128)}, u32[]{:S(2)}) copy-start(f32[3,128,256]{2,1,0:T(8,128)} %get-tuple-element.86) | copy-start | bytes 1179652
  396.5 6.7 %copy-start.31 = (f32[128,256]{1,0:T(8,128)S(1)}, f32[128,256]{1,0:T(8,128)}, u32[]{:S(2)}) copy-start(f32[128,256]{1,0:T(8,128)} %param.34) | copy-start | bytes 393220
  396.5 6.7 %copy-start.32 = (f32[128,256]{1,0:T(8,128)S(1)}, f32[128,256]{1,0:T(8,128)}, u32[]{:S(2)}) copy-start(f32[128,256]{1,0:T(8,128)} %param.33) | copy-start | bytes 393220
  396.5 6.7 %copy-start.33 = (f32[128,256]{1,0:T(8,128)S(1)}, f32[128,256]{1,0:T(8,128)}, u32[]{:S(2)}) copy-start(f32[128,256]{1,0:T(8,128)} %param.44) | copy-start | bytes 393220
  396.5 6.7 %copy-start.34 = (f32[128,256]{1,0:T(8,128)S(1)}, f32[128,256]{1,0:T(8,128)}, u32[]{:S(2)}) copy-start(f32[128,256]{1,0:T(8,128)} %param.45) | copy-start | bytes 393220
  396.5 6.7 %copy-start.35 = (f32[128,256]{1,0:T(8,128)S(1)}, f32[128,256]{1,0:T(8,128)}, u32[]{:S(2)}) copy-start(f32[128,256]{1,0:T(8,128)} %param.43) | copy-start | bytes 393220
  396.5 6.7 %copy-start.36 = (f32[128,256]{1,0:T(8,128)S(1)}, f32[128,256]{1,0:T(8,128)}, u32[]{:S(2)}) copy-start(f32[128,256]{1,0:T(8,128)} %param.42) | copy-start | bytes 393220
  396.5 7.8 %copy-start.37 = (f32[256,128]{1,0:T(8,128)S(1)}, f32[256,128]{1,0:T(8,128)}, u32[]{:S(2)}) copy-start(f32[256,128]{1,0:T(8,128)} %param.46) | copy-start | bytes 393220
  396.5 7.8 %copy-start.38 = (f32[256,128]{1,0:T(8,128)S(1)}, f32[256,128]{1,0:T(8,128)}, u32[]{:S(2)}) copy-start(f32[256,128]{1,0:T(8,128)} %param.47) | copy-start | bytes 393220
  396.6 7.9 %copy-start.27 = (f32[256,128]{0,1:T(8,128)S(1)}, f32[256,128]{0,1:T(8,128)}, u32[]{:S(2)}) copy-start(f32[256,128]{0,1:T(8,128)} %copy-done.26) | copy-start | bytes 393220
  403.1 5.9 %copy-start.45 = (f32[32]{0:T(128)S(1)}, f32[32]{0:T(128)}, u32[]{:S(2)}) copy-start(f32[32]{0:T(128)} %param.36) | copy-start | bytes 388
  403.1 5.8 %copy-start.48 = (f32[32]{0:T(128)S(1)}, f32[32]{0:T(128)}, u32[]{:S(2)}) copy-start(f32[32]{0:T(128)} %param.48) | copy-start | bytes 388
  403.1 5.8 %copy-start.49 = (f32[32]{0:T(128)S(1)}, f32[32]{0:T(128)}, u32[]{:S(2)}) copy-start(f32[32]{0:T(128)} %param.49) | copy-start | bytes 388
  403.1 6.4 %copy-start.29 = (f32[256,1024]{1,0:T(8,128)S(1)}, f32[256,1024]{1,0:T(8,128)}, u32[]{:S(2)}) copy-start(f32[256,1024]{1,0:T(8,128)} %get-tuple-element.272) | copy-start | bytes 3145732
  403.2 7.3 %copy-start.28 = (f32[256,1024]{1,0:T(8,128)S(1)}, f32[256,1024]{1,0:T(8,128)}, u32[]{:S(2)}) copy-start(f32[256,1024]{1,0:T(8,128)} %get-tuple-element.273) | copy-start | bytes 3145732
  (26 other events, 70.7 us)

commit v5 on v4

--- a/solution.py
+++ b/solution.py
@@ -91,10 +91,13 @@
     def wait(self, target, device, slot):
         self.make(target, target, device, slot).wait_recv()
 
-    def finish(self):
-        for copy in self.sent:
+    def split(self):
+        before, self.sent = self.sent, []
+        return before
+
+    def finish(self, some=None):
+        for copy in self.sent if some is None else some:
             copy.wait_send()
-        self.sent = []
 
 
 class TreeGather:
@@ -192,7 +195,7 @@
     )
 
 
-def launch(kernel, identity, ins, outs, scratch, n_copies, limit=None):
+def launch(kernel, identity, ins, outs, scratch, n_copies, limit=None, kept=None):
     def flat(entries):
         names, leaves, specs = [], [], []
         for name, (value, spec) in entries.items():
@@ -216,6 +219,18 @@
     )
     in_names, values, in_specs = flat(ins)
     out_names, shapes, out_specs = flat(outs)
+
+    def numbers(names, wanted):
+        at = 0
+        for name, count in names:
+            size = 1 if count is None else count
+            if name == wanted:
+                return range(at, at + size)
+            at += size
+
+    aliases = {}
+    for output, source in (kept or {}).items():
+        aliases |= dict(zip(numbers(in_names, source), numbers(out_names, output)))
     scratch_names = [(name, None) for name in scratch]
 
     def body(*refs):
@@ -228,6 +243,7 @@
         in_specs=in_specs,
         out_specs=tuple(out_specs),
         scratch_shapes=list(scratch.values()),
+        input_output_aliases=aliases,
         compiler_params=params(identity, limit),
         cost_estimate=pl.CostEstimate(flops=1, bytes_accessed=1, transcendentals=0),
         name=kernel.__name__,
@@ -250,11 +266,14 @@
 NN, NT, TN = (1, 0), (1, 1), (0, 0)
 
 
-def prologue(n_dp, n_mp, groups, identity, small, shards, cot, residual):
+def prologue(n_dp, n_mp, identity, first_row, small, shards, cot, residual, gateup, down):
     half = n_mp // 2
     kinds, rows, cols = shards.shape
     tokens, width = cot.shape
     order_a, _ = orders_of(n_dp)
+    owned, _, hidden, _ = gateup.shape
+    n_devices = n_dp * n_mp
+    own_router = small.shape[0] - first_row
     n_copies = 2 * (n_mp - 1) + 4 * (n_dp - 1) + 1
 
     def gather_line(r):
@@ -262,6 +281,12 @@
         me = (dp, mp)
         neighbour = (dp, flip(mp, 1))
         copies = Copies(r.send_sems, r.recv_sems)
+        loads = [
+            pltpu.make_async_copy(r.gateup, r.wide.at[:, pl.ds(0, 2)], r.local_sems.at[0]),
+            pltpu.make_async_copy(r.down, r.wide.at[:, 2], r.local_sems.at[1]),
+        ]
+        for copy in loads:
+            copy.start()
         own_small = r.small_all.at[dp, mp]
         own_cols = pl.ds(pl.multiple_of(mp * cols, cols), cols)
         own_part = r.row_block.at[:, :, own_cols]
@@ -301,29 +326,62 @@
             small_trees[chunk].send(0)
         for one in cot_trees:
             one.send(0)
+        for copy in loads:
+            copy.wait()
+        for e in range(owned):
+            r.narrow[e] = r.wide[e].astype(BF16)
+        store = pltpu.make_async_copy(r.narrow, r.packed, r.local_sems.at[2])
+        store.start()
         top = n_dp.bit_length() - 1
         for level in range(1, top + 1):
             run_level(small_trees, level)
             run_level(cot_trees, level)
+        n_tiles = width // 128
+        for row in (0, 1):
+            for tile in range(n_tiles):
+                total = None
+                for at in range(tile * n_devices // n_tiles, (tile + 1) * n_devices // n_tiles):
+                    part = r.small_all[at // n_mp, at % n_mp, row : row + 1, :]
+                    total = part if total is None else total + part
+                r.gains[row : row + 1, tile * 128 : (tile + 1) * 128] = total
+        for at in range(n_devices):
+            r.router_wide[at * own_router : (at + 1) * own_router, :] = r.small_all[
+                at // n_mp, at % n_mp, first_row:, :
+            ]
+        r.router[...] = r.router_wide[...].astype(BF16)
         for k in range(1, n_mp):
             other = pl.multiple_of(flip_all(mp, k) * cols, cols)
             copies.wait(r.row_block.at[:, :, pl.ds(other, cols)], me, line[k][1])
         copies.wait(r.scaled.at[1], me, across)
+        store.wait()
         copies.finish()
 
     return launch(
         gather_line,
         identity,
         dict(
-            small=(small, vmem()), shards=(shards, vmem()), cot=(cot, vmem()), residual=(residual, vmem())
+            small=(small, vmem()),
+            shards=(shards, vmem()),
+            cot=(cot, vmem()),
+            residual=(residual, vmem()),
+            gateup=(gateup, hbm()),
+            down=(down, hbm()),
         ),
         dict(
-            small_all=(single(n_dp, n_mp, *small.shape), vmem()),
+            gains=(single(2, width), vmem()),
+            router=(low(width, 128), vmem()),
+            packed=(low(owned, 3, hidden, width), hbm()),
             row_block=(low(kinds, rows, n_mp * cols), vmem()),
             cots=(low(n_dp, tokens, width), vmem()),
             scaled=(low(2, tokens, width), vmem()),
         ),
-        {},
+        dict(
+            small_all=pltpu.VMEM((n_dp, n_mp) + small.shape, F32),
+            router_wide=pltpu.VMEM((width, 128), F32),
+            wide=pltpu.VMEM((owned, 3, hidden, width), F32),
+            narrow=pltpu.VMEM((owned, 3, hidden, width), BF16),
+            local_sems=pltpu.SemaphoreType.DMA((3,)),
+        ),
         n_copies,
         32 << 20,
     )
@@ -352,59 +410,6 @@
 def wait_experts(copies, me, near, slots):
     for (i, k), slot in slots.items():
         copies.wait(near[k - 1].at[i], me, slot)
-
-
-def gather_rows(n_dp, n_mp, groups, identity, row_block, cot, packed, experts):
-    span = n_mp // groups
-    n_experts = len(experts)
-    kinds, rows, width = row_block.shape
-    part_rows = rows // 2
-
-    def gather_weights(r):
-        dp, mp = lax.axis_index("dp"), lax.axis_index("mp")
-        me = (dp, mp)
-        copies = Copies(r.send_sems, r.recv_sems)
-        partner = (dp, flip_all(mp, span))
-        r.full[:, pl.ds(pl.multiple_of(dp * rows, rows), rows), :] = r.row_block[...]
-        greet(
-            [(flip_all(dp, mask), mp) for mask in bits_of(n_dp)]
-            + [partner] * (groups - 1)
-            + [(dp, flip_all(mp, k)) for k in range(1, span)]
-        )
-        across = copies.slot()
-        if groups > 1:
-            copies.start(r.cot, r.cot_other, partner, across)
-        sent = send_experts(copies, me, span, r.packed, r.near, experts)
-
-        def tree(part, order):
-            def ref(j, mask=0):
-                start = flip_all(dp, j) * rows + part * part_rows
-                return r.full.at[:, pl.ds(pl.multiple_of(start, part_rows), part_rows), :]
-
-            return TreeGather(copies, order, n_dp, me, ref, ref)
-
-        trees = [tree(part, order) for part, order in enumerate(orders_of(n_dp))]
-        for one in trees:
-            one.send(0)
-        run_gathers(trees)
-        if groups > 1:
-            copies.wait(r.cot_other, me, across)
-        wait_experts(copies, me, r.near, sent)
-        copies.finish()
-
-    return launch(
-        gather_weights,
-        identity,
-        dict(row_block=(row_block, vmem()), cot=(cot, vmem()), packed=(packed, hbm())),
-        dict(
-            full=(low(kinds, n_dp * rows, width), vmem()),
-            cot_other=(low(*cot.shape), vmem()),
-            near=([low(n_experts, *packed.shape[1:]) for _ in range(1, span)], hbm()),
-        ),
-        {},
-        2 * (n_dp - 1) + 1 + n_experts * (span - 1),
-        32 << 20,
-    )
 
 
 def row_trees(copies, n_dp, me, rows_all):
@@ -488,56 +493,86 @@
 
 
 def attention_forward(
-    n_dp, n_mp, groups, identity, residual, scaled, full, gains, router, places, cot_other, rotary, packed, experts
+    n_dp, n_mp, groups, identity, residual, ids, start, cot, tables, experts
 ):
     tokens, width = residual.shape
-    query_rotary, own_rotary, other_rotary = rotary
+    kinds, rows, _ = start.row_block.shape
+    part_rows = rows // 2
     n_heads = width // 128
     span = n_mp // groups
     owned = EXPERTS // n_dp
     n_experts = len(experts)
-    n_copies = 2 * (n_dp - 1) + n_experts * (span - 1)
+    n_copies = 4 * (n_dp - 1) + n_experts * (span - 1) + 1
 
     def attention(r):
         dp, mp = lax.axis_index("dp"), lax.axis_index("mp")
         me = (dp, mp)
+        partner = (dp, flip_all(mp, span))
         copies = Copies(r.send_sems, r.recv_sems)
-        loads = [
-            pltpu.make_async_copy(r.full.at[c], r.weights.at[c], r.local_sems.at[c])
-            for c in range(3)
-        ]
-        for copy in loads:
-            copy.start()
-        r.cots[0] = r.cot_other[...]
+        r.full[:, pl.ds(pl.multiple_of(dp * rows, rows), rows), :] = r.row_block[...]
         greet(
             [(flip_all(dp, mask), mp) for mask in bits_of(n_dp)]
+            + [partner] * (groups - 1)
             + [(dp, flip_all(mp, k)) for k in range(1, span)]
         )
+        across = copies.slot()
+        if groups > 1:
+            copies.start(r.cot, r.cots.at[0], partner, across)
+
+        def tree(part, order):
+            def ref(j, mask=0):
+                start = flip_all(dp, j) * rows + part * part_rows
+                return r.full.at[:, pl.ds(pl.multiple_of(start, part_rows), part_rows), :]
+
+            return TreeGather(copies, order, n_dp, me, ref, ref)
+
+        weight_trees = [tree(part, order) for part, order in enumerate(orders_of(n_dp))]
+        cot_trees = row_trees(copies, n_dp, me, r.cots) if groups > 1 else []
+        for one in weight_trees:
+            one.send(0)
         sent = send_experts(copies, me, span, r.packed, r.near, experts)
-        trees = row_trees(copies, n_dp, me, r.cots) if groups > 1 else []
-        for one in trees:
-            one.send(0)
-        top = n_dp.bit_length() - 1
+        named = lax.broadcasted_iota(jnp.int32, (EXPERTS, tokens), 0)
+        chosen = jnp.zeros((EXPERTS, tokens), F32)
+        for k in range(TOPK):
+            chosen += jnp.where(named == r.ids[k : k + 1, :], 1.0, 0.0)
+        shape = (tokens, tokens)
+        earlier = lax.broadcasted_iota(jnp.int32, shape, 0) < lax.broadcasted_iota(jnp.int32, shape, 1)
+        before = dot(chosen.astype(BF16), jnp.where(earlier, 1.0, 0.0).astype(BF16), NN)
+        place = jnp.where(chosen > 0.0, before, -1.0)
+        r.table[...] = jnp.zeros_like(r.table)
+        for expert in range(EXPERTS):
+            owner, which = divmod(expert, owned)
+            r.table[owner, which, :] = place[expert]
         residual = r.residual[...]
         inverse = lax.rsqrt(jnp.mean(residual * residual, -1, keepdims=True) + NORM_EPS)
         gain_one = r.gains[0:1, :]
         r.normed[0] = (residual * inverse * gain_one).astype(BF16)
         r.normed[1] = (r.scaled[1].astype(F32) * gain_one).astype(BF16)
-        loads[0].wait()
-        r.q[...] = dot(r.normed[0], r.weights[0], NN)
-        loads[1].wait()
+        mask = seen(tokens, mp)
+        top = n_dp.bit_length() - 1
+        for level in range(1, top + 1):
+            if level == top and groups > 1:
+                copies.wait(r.cots.at[0], me, across)
+                for one in cot_trees:
+                    one.send(0)
+            run_level(weight_trees, level)
+        r.q[...] = dot(r.normed[0], r.full[0], NN)
         for part in (0, 1):
-            r.kv[part] = dot(r.normed[part], r.weights[1], NN)
-        run_level(trees, 1)
-        mask = seen(tokens, mp)
+            r.kv[part] = dot(r.normed[part], r.full[1], NN)
+        run_level(cot_trees, 1)
+        which = lax.rem(mp, 2)
+
+        def table(ref, at):
+            there = pl.ds(pl.multiple_of(at * tokens, tokens), tokens)
+            return ref[0, there, :], ref[1, there, :]
 
         def head(k, carry):
             lanes = pl.ds(pl.multiple_of(k * 128, 128), 128)
-            queries = rotate(r.q[:, lanes], r.query_rotary[0], r.query_rotary[1])
+            queries = rotate(r.q[:, lanes], *table(r.query_table, which))
             r.queries[:, lanes] = queries.astype(BF16)
             parts = []
-            for part, table in enumerate((r.own_rotary, r.other_rotary)):
-                parts.append(rotate(r.kv[part, :, lanes], table[0], table[1]))
+            for part, at in enumerate((which, 1 - which)):
+                parts.append(rotate(r.kv[part, :, lanes], *table(r.key_table, at)))
                 r.keyval[part, :, lanes] = parts[part].astype(BF16)
             both, keys, values = group_operands(queries, jnp.concatenate(parts, 0))
             chance = softmax_of(both, keys, mask).astype(BF16)
@@ -547,9 +582,8 @@
         for level in range(2, top + 1):
             first, end = [(level - 2 + i) * n_heads // (top - 1) for i in (0, 1)]
             lax.fori_loop(first, end, head, 0)
-            run_level(trees, level)
-        loads[2].wait()
-        hidden = r.residual[...] + dot(r.context[...], r.weights[2], NT)
+            run_level(cot_trees, level)
+        hidden = r.residual[...] + dot(r.context[...], r.full[2], NT)
         r.hidden[...] = hidden
         inverse = lax.rsqrt(jnp.mean(hidden * hidden, -1, keepdims=True) + NORM_EPS)
         normed = (hidden * inverse * r.gains[1:2, :]).astype(BF16)
@@ -560,7 +594,6 @@
         probs = raised / jnp.sum(raised, -1, keepdims=True)
         r.probs[...] = probs
         turned = probs.T
-        r.table[...] = r.places[...]
         for expert in range(EXPERTS):
             owner, which = divmod(expert, owned)
             r.table[owner, 4 + which, :] = turned[expert]
@@ -572,20 +605,20 @@
         identity,
         dict(
             residual=(residual, vmem()),
-            scaled=(scaled, vmem()),
-            full=(full, hbm()),
-            gains=(gains, vmem()),
-            packed=(packed, hbm()),
-            router=(router, vmem()),
-            places=(places, vmem()),
-            cot_other=(cot_other, vmem()),
-            query_rotary=(query_rotary, vmem()),
-            own_rotary=(own_rotary, vmem()),
-            other_rotary=(other_rotary, vmem()),
+            ids=(ids, vmem()),
+            scaled=(start.scaled, vmem()),
+            row_block=(start.row_block, vmem()),
+            cot=(cot, vmem()),
+            gains=(start.gains, vmem()),
+            router=(start.router, vmem()),
+            packed=(start.packed, hbm()),
+            query_table=(tables[0], vmem()),
+            key_table=(tables[1], vmem()),
         ),
         dict(
+            full=(low(kinds, n_dp * rows, width), vmem()),
             cots=(low(n_dp, tokens, width), vmem()),
-            near=([low(n_experts, *packed.shape[1:]) for _ in range(1, span)], hbm()),
+            near=([low(n_experts, *start.packed.shape[1:]) for _ in range(1, span)], hbm()),
             normed=(low(2, tokens, width), vmem()),
             queries=(low(tokens, width), vmem()),
             keyval=(low(2, tokens, width), vmem()),
@@ -593,13 +626,11 @@
             hidden=(single(tokens, width), vmem()),
             normed_two=(low(tokens, width), vmem()),
             probs=(single(tokens, 128), vmem()),
-            table=(single(*places.shape), vmem()),
+            table=(single(n_dp, 8, tokens), vmem()),
         ),
         dict(
-            weights=pltpu.VMEM((3, width, width), BF16),
             q=pltpu.VMEM((tokens, width), F32),
             kv=pltpu.VMEM((2, tokens, width), F32),
-            local_sems=pltpu.SemaphoreType.DMA((3,)),
         ),
         n_copies,
         48 << 20,
@@ -618,7 +649,7 @@
     span = n_mp // groups
     owned = EXPERTS // n_dp
     n_late = given.late[0].shape[0] if given.late else 0
-    n_copies = (2 * groups + 7) * (n_dp - 1) + 1 + 4 * (n_mp - 1) + 1 + n_late * (span - 1)
+    n_copies = (2 * groups + 7) * (n_dp - 1) + 2 + 4 * (n_mp - 1) + 2 + n_late * (span - 1)
 
     rooms, across_room = reduce_rooms(groups, n_dp, tokens, width, BF16)
 
@@ -633,16 +664,37 @@
         ]
         for copy in loads:
             copy.start()
+        even_loads = [
+            pltpu.make_async_copy(
+                r.terms.at[g, j], r.terms_even.at[g, j // 2], r.term_sems.at[g, j // 2]
+            )
+            for g in range(groups)
+            for j in range(0, n_dp, 2)
+        ]
+        for copy in even_loads:
+            copy.start()
         greet(
             [(flip_all(dp, mask), mp) for mask in bits_of(n_dp)]
             + [(dp, flip_all(mp, k)) for k in range(1, n_mp)]
         )
         partner = (dp, flip_all(mp, span))
-        mixture = TokenReduce(copies, n_dp, me, partner, r.terms, r.rooms, r.across)
+        mixture = TokenReduce(
+            copies,
+            n_dp,
+            me,
+            partner,
+            groups,
+            lambda g, j: r.terms.at[g, j] if j % 2 else r.terms_even.at[g, j // 2],
+            r.rooms,
+            r.across,
+        )
         for group in range(groups)[::-1]:
             for j in range(1, n_dp, 2):
                 mixture.first(group, j)
         last = mixture.last
+        for copy in even_loads:
+            copy.wait()
+        mixture.level(1, last - 1)
         travels = {}
 
         def send_late(i):
@@ -651,7 +703,7 @@
                     travels[i, k] = copies.slot()
                     copies.start(
                         r.late[k - 1].at[i],
-                        r.arrived[k - 1].at[i],
+                        r.arrived[k - 1].at[owned - n_late + i],
                         (dp, flip_all(mp, k)),
                         travels[i, k],
                     )
@@ -671,6 +723,7 @@
         ).astype(BF16)
         grad_normed_two = r.total[...] + dot(grad_logits, r.router[...], NT)
         r.grad_router[...] = dot(r.normed_two[...], grad_logits, TN)
+        mixture.level(0, last - 1)
         hidden = r.hidden[...]
         inverse = lax.rsqrt(jnp.mean(hidden * hidden, -1, keepdims=True) + NORM_EPS)
         scaled = r.gains[1:2, :] * grad_normed_two
@@ -710,10 +763,13 @@
 
         r.grads[2] = dot(grad_attn, r.context[...], TN).astype(BF16)
         weight_level(2, last)
-        mixture.level(1, last - 1)
         loads[0].wait()
         r.grad_context[...] = dot(r.grad_attn[...], r.weights[2], NN).astype(BF16)
         mask = seen(tokens, mp)
+
+        def table(ref):
+            there = pl.ds(pl.multiple_of(lax.rem(mp, 2) * tokens, tokens), tokens)
+            return ref[0, there, :], ref[1, there, :]
 
         def head(k, carry):
             lanes = pl.ds(pl.multiple_of(k * 128, 128), 128)
@@ -726,7 +782,8 @@
             grad_s = (chance * (grad_p - delta)).astype(BF16)
             scale = 1.0 / math.sqrt(HEAD_SIZE)
             grad_q = merge_heads(dot(grad_s, keys, NN)) * scale
-            r.grad_q[:, lanes] = rotate(grad_q, r.query_rotary[0], -r.query_rotary[1]).astype(BF16)
+            cosine, sine = table(r.query_table)
+            r.grad_q[:, lanes] = rotate(grad_q, cosine, -sine).astype(BF16)
             grad_k = dot(grad_s, both, TN) * scale
             grad_v = dot(chance.astype(BF16), grad_both, TN)
             lane = lax.broadcasted_iota(jnp.int32, grad_k.shape, 1)
@@ -754,38 +811,48 @@
                     r.line.at[0, c, k], r.line.at[1, c, k], (dp, flip_all(mp, k)), sent[c, k]
                 )
 
-        stages = []
+        across = [copies.slot() for _ in range(2)]
+        swaps = [pl.ds(half * (width // 2), width // 2) for half in range(2)]
+
+        def heads(first, end):
+            lax.fori_loop(first * n_heads // 4, end * n_heads // 4, head, 0)
+
+        def swap(half):
+            copies.start(
+                r.swap.at[0, :, swaps[half]],
+                r.swap.at[1, :, swaps[half]],
+                neighbour,
+                across[half],
+            )
+
+        heads(0, 2)
+        swap(0)
         for p in range(last - 2, -1, -1):
-            stages.append([lambda p=p: mixture.level(1, p)])
-        stages.append([lambda: weight_level(2, last - 1), mixture.pass_on])
-        for p in range(last - 1, -1, -1):
-            stages.append([lambda p=p: mixture.level(0, p)])
-            if p < last - 1:
-                stages[-1].append(lambda p=p: weight_level(2, p))
-        loops = min(len(stages), n_heads)
-        for step in range(loops):
-            lax.fori_loop(step * n_heads // loops, (step + 1) * n_heads // loops, head, 0)
-            if step == loops - 1:
-                across = copies.slot()
-                copies.start(r.swap.at[0], r.swap.at[1], neighbour, across)
-                for i in range(1, n_late):
-                    send_late(i)
-            for stage in stages.pop(0):
-                stage()
-        for stage in sum(stages, []):
-            stage()
+            mixture.level(1, p)
+        heads(2, 3)
+        weight_level(2, last - 1)
+        heads(3, 4)
+        swap(1)
+        for p in range(last - 2, -1, -1):
+            mixture.level(0, p)
+        mixture.pass_on()
+        for i in range(1, n_late):
+            send_late(i)
         r.grads[0] = dot(r.normed[0], r.grad_q[...], TN).astype(BF16)
         weight_level(0, last)
         loads[1].wait()
         r.grad_normed[...] = dot(r.grad_q[...], r.weights[0], NT)
         weight_level(0, last - 1)
-        line_out(2)
-        copies.wait(r.swap.at[1], me, across)
+        for p in range(last - 2, -1, -1):
+            weight_level(2, p)
+        for half in range(2):
+            copies.wait(r.swap.at[1, :, swaps[half]], me, across[half])
 
         def turn_back(k, carry):
             lanes = pl.ds(pl.multiple_of(k * 128, 128), 128)
             total = r.grad_kv[:, lanes] + r.swap[1, :, lanes].astype(F32)
-            total = rotate(total, r.own_rotary[0], -r.own_rotary[1])
+            cosine, sine = table(r.key_table)
+            total = rotate(total, cosine, -sine)
             r.grad_kv_low[:, lanes] = total.astype(BF16)
             return carry
 
@@ -836,6 +903,8 @@
                 if place_of(orders[0], j) == p:
                     small_tree.collect(j)
                     small_tree.send(j)
+            if p == last - 1:
+                line_out(2)
         for c in (0, 1):
             line_out(c)
         small_tree.collect(0)
@@ -855,7 +924,8 @@
         for k in range(1, n_mp):
             copies.wait(r.small_line.at[k], me, sent[k])
             r.small_shard[...] += r.small_line[k]
-        wait_experts(copies, me, r.arrived, travels)
+        for (i, k), slot in travels.items():
+            copies.wait(r.arrived[k - 1].at[owned - n_late + i], me, slot)
         copies.finish()
 
     return launch(
@@ -864,12 +934,13 @@
         dict(
             full=(given.full, hbm()),
             late=(given.late, hbm()),
+            begun=(given.arrived, hbm()),
             residual=(given.residual, vmem()),
             hidden=(given.hidden, vmem()),
             cotangent=(given.cotangent, vmem()),
             total=(given.total, vmem()),
             gate_parts=(given.gate_parts, vmem()),
-            terms=(given.terms, vmem()),
+            terms=(given.terms, hbm()),
             probs=(given.probs, vmem()),
             normed=(given.normed, vmem()),
             normed_two=(given.normed_two, vmem()),
@@ -878,13 +949,13 @@
             context=(given.context, vmem()),
             gains=(given.gains, vmem()),
             router=(given.router, vmem()),
-            query_rotary=(given.rotary[0], vmem()),
-            own_rotary=(given.rotary[1], vmem()),
+            query_table=(given.tables[0], vmem()),
+            key_table=(given.tables[1], vmem()),
         ),
         dict(
             input_grad=(single(tokens, width), vmem()),
             block_out=(single(tokens, width), vmem()),
-            arrived=([low(*grad.shape) for grad in given.late], hbm()),
+            arrived=([low(*grad.shape) for grad in given.arrived], hbm()),
             shards=(single(3, rows, cols), vmem()),
             small_shard=(single(first_row + own_router, 128), vmem()),
         ),
@@ -893,6 +964,8 @@
             small=pltpu.VMEM((n_dp, n_mp, first_row + own_router, 128), F32),
             small_rooms=pltpu.VMEM((n_dp - 1, n_mp, first_row + own_router, 128), F32),
             small_line=pltpu.VMEM((n_mp, first_row + own_router, 128), F32),
+            terms_even=pltpu.VMEM((groups, n_dp // 2, tokens, width), BF16),
+            term_sems=pltpu.SemaphoreType.DMA((groups, n_dp // 2)),
             weight_rooms=pltpu.VMEM((3, 2, n_dp - 1, part_rows, width), BF16),
             line=pltpu.VMEM((2, 3, n_mp, rows, cols), BF16),
             rooms=rooms,
@@ -912,18 +985,19 @@
         ),
         n_copies,
         62 << 20,
+        dict(arrived="begun"),
     )
 
 
 class TokenReduce:
-    def __init__(self, copies, n_dp, me, partner, terms, rooms, across):
+    def __init__(self, copies, n_dp, me, partner, groups, block, rooms, across):
         self.copies, self.me, self.across = copies, me, across
         self.partner = partner
-        self.tokens = terms.shape[2]
+        self.tokens = across.shape[1]
         self.n_dp = n_dp
         self.last = n_dp.bit_length() - 2
-        self.groups = terms.shape[0]
-        self.slot = copies.slot()
+        self.groups = groups
+        self.halves = [copies.slot(), copies.slot()]
 
         def tree(group, part, order):
             cut = pl.ds(part * (self.tokens // 2), self.tokens // 2)
@@ -932,7 +1006,7 @@
                 order,
                 n_dp,
                 me,
-                lambda j: terms.at[group, j, cut],
+                lambda j: block(group, j).at[cut],
                 lambda number: rooms.at[group, part, number],
                 add_rows(),
             )
@@ -961,26 +1035,26 @@
         for part, tree in enumerate(self.trees[1]):
             tree.collect(0)
             cut = pl.ds(part * (self.tokens // 2), self.tokens // 2)
-            self.across[0, cut, :] = tree.total()[...]
-        self.copies.start(self.across.at[0], self.across.at[1], self.partner, self.slot)
+            self.copies.start(
+                tree.total(), self.across.at[0, cut], self.partner, self.halves[part]
+            )
 
     def end(self, out_ref):
         for tree in self.trees[0]:
             tree.collect(0)
-        if self.groups > 1:
-            self.copies.wait(self.across.at[1], self.me, self.slot)
         for part, tree in enumerate(self.trees[0]):
             cut = pl.ds(part * (self.tokens // 2), self.tokens // 2)
             total = tree.total()[...].astype(F32)
             if self.groups > 1:
-                total = total + self.across[1, cut, :].astype(F32)
+                self.copies.wait(self.across.at[0, cut], self.me, self.halves[part])
+                total = total + self.across[0, cut, :].astype(F32)
             out_ref[cut, :] = total
 
 
 def reduce_rooms(groups, n_dp, tokens, width, dtype):
     return [
         pltpu.VMEM((groups, 2, n_dp - 1, tokens // 2, width), dtype),
-        pltpu.VMEM((2, tokens, width), dtype),
+        pltpu.VMEM((1, tokens, width), dtype),
     ]
 
 
@@ -998,7 +1072,7 @@
     coming = [expert for expert in range(owned) if expert not in here]
     n_sent = min(owned, 2)
     n_late = owned - n_sent
-    n_copies = groups + 2 * (blocks - 1) + 4 * groups * (n_dp - 1)
+    n_copies = groups + 1 + 2 * (blocks - 1) + 4 * groups * (n_dp - 1)
     n_copies += (len(coming) + n_sent) * (span - 1)
     order = []
     for group in range(groups):
@@ -1147,6 +1221,7 @@
         weights_sent, grads_sent = {}, {}
         ready(0)
         done = 0
+        leaving = []
         for number, (group, j) in enumerate(order):
             if j:
                 for tree in sorted(trees[group], key=lambda tree: place_of(tree.order, j)):
@@ -1157,6 +1232,7 @@
                 for tree in trees[1]:
                     tree.send(0)
             if group == groups - 1 and j == 0:
+                leaving += copies.split()
                 for e in coming:
                     for k in range(1, span):
                         weights_sent[e, k] = copies.slot()
@@ -1166,11 +1242,14 @@
                             (dp, flip_all(mp, k)),
                             weights_sent[e, k],
                         )
+                staying = copies.split()
             fill(number)
             if number % per_tile == per_tile - 1 and number < blocks - 1:
                 work(0, done)
                 done += 1
         work(0, done)
+        leaving += copies.split()
+        copies.sent = staying
         weight_grad(0)
 
         def tiles(e, first, end):
@@ -1184,9 +1263,11 @@
             ready(e)
             tiles(e, 0, n_tiles)
             weight_grad(e)
-        copies.finish()
+        copies.finish(leaving)
         partner = (dp, other)
-        reduce = TokenReduce(copies, n_dp, me, partner, r.rows_all, r.rooms, r.across)
+        reduce = TokenReduce(
+            copies, n_dp, me, partner, groups, lambda g, j: r.rows_all.at[g, j], r.rooms, r.across
+        )
         last = owned - 1
         if last:
             ready(last)
@@ -1283,7 +1364,7 @@
             gate_parts=(single(n_dp, groups, 8, tokens), hbm()),
             total=(single(tokens, width), vmem()),
             grad_own=(low(owned, *weights), hbm()),
-            arrived=([low(n_sent, *weights) for _ in range(1, span)], hbm()),
+            arrived=([low(owned, *weights) for _ in range(1, span)], hbm()),
             late=([low(n_late, *weights) for _ in range(1, span) if n_late], hbm()),
         ),
         dict(
@@ -1375,72 +1456,35 @@
     )
     shards = jnp.stack([query_w, key_value_weight, output_w.T]).astype(BF16)
     cot_low = cotangent.astype(BF16)
-    start = prologue(n_dp, n_mp, groups, 0, small, shards, cot_low, residual_in)
-    small_all = start.small_all
-    gains = jnp.concatenate(
-        [
-            jnp.sum(small_all[:, :, row].reshape(-1, per_tile, lanes), 1).reshape(1, -1)
-            for row in (0, 1)
-        ]
-    )
-    router_low = small_all[:, :, first_row:].reshape(MODEL_WIDTH, lanes).astype(BF16)
-
-    expert_range = jnp.arange(EXPERTS, dtype=jnp.int32)
-    onehot = (expert_ids[:, :, None] == expert_range[None, None, :]).astype(jnp.int32)
-    chosen = jnp.sum(onehot, 1)
-    before = jnp.cumsum(chosen, 0) - chosen
-    place = jnp.where(chosen > 0, before, -1)
-    places = jnp.pad(
-        place.astype(F32).T.reshape(n_dp, owned, tokens), ((0, 0), (0, 8 - owned), (0, 0))
-    )
-
-    packed = jnp.concatenate([gateup_w, down_w[:, None]], 1).astype(BF16)
-    early = [list(range(owned))[:1], list(range(owned))[1:3]]
-    whole = gather_rows(n_dp, n_mp, groups, 1, start.row_block, cot_low, packed, early[0])
-    full = whole.full
-
-    query_table, key_table = (jnp.asarray(table) for table in rotary_constants())
-    part = mp % 2
-    rotary = [
-        lax.dynamic_slice_in_dim(table, which * tokens, tokens, 1)
-        for table, which in ((query_table, part), (key_table, part), (key_table, 1 - part))
-    ]
+    start = prologue(
+        n_dp, n_mp, 0, first_row, small, shards, cot_low, residual_in, gateup_w, down_w
+    )
+    tables = [jnp.asarray(table) for table in rotary_constants()]
+    early = list(range(owned))[:1]
     front = attention_forward(
+        n_dp, n_mp, groups, 1, residual_in, expert_ids.T, start, cot_low, tables, early
+    )
+
+    found = run_experts(
         n_dp,
         n_mp,
         groups,
         2,
-        residual_in,
-        start.scaled,
-        full,
-        gains,
-        router_low,
-        places,
-        whole.cot_other,
-        rotary,
-        packed,
-        early[1],
-    )
-
-    found = run_experts(
-        n_dp,
-        n_mp,
-        groups,
-        3,
         front.normed_two,
         front.table,
         [start.cots, front.cots][:groups],
-        packed,
-        [(early[0], whole.near), (early[1], front.near)],
+        start.packed,
+        [(early, front.near)],
     )
 
     given = types.SimpleNamespace(
-        full=full,
+        full=front.full,
         residual=residual_in,
         hidden=front.hidden,
         cotangent=cotangent,
         total=found.total,
         late=found.late,
+        arrived=found.arrived,
         gate_parts=found.gate_parts,
         terms=found.terms,
         probs=front.probs,
@@ -1449,17 +1493,16 @@
         queries=front.queries,
         keyval=front.keyval,
         context=front.context,
-        gains=gains,
-        router=router_low,
-        rotary=rotary,
-    )
-    back = attention_backward(n_dp, n_mp, groups, 4, given, first_row)
+        gains=start.gains,
+        router=start.router,
+        tables=tables,
+    )
+    back = attention_backward(n_dp, n_mp, groups, 3, given, first_row)
     input_grad, block_out = back.input_grad, back.block_out
-    expert_grad = found.grad_own.astype(F32)
-    for k in range(1, span):
-        parts = [found.arrived[k - 1]] + ([back.arrived[k - 1]] if back.arrived else [])
-        expert_grad += jnp.concatenate(parts).astype(F32)
-    gateup_grad, down_grad = expert_grad[:, :2], expert_grad[:, 2]
+    gateup_grad, down_grad = (
+        sum(part[:, cut].astype(F32) for part in [found.grad_own] + back.arrived)
+        for cut in (slice(0, 2), 2)
+    )
     grads, small_grads = back.shards, back.small_shard
     query_grad, keyval_grad, output_grad = grads[0], grads[1], grads[2].T
     first_lane = (place_in_all % per_tile) * own_gain

time: 417 us -> 379 us (0.909)
  Pallas kernels: 355 us -> 325 us
  other arithmetic: 29.1 us -> 23.3 us
    pallas_call x5 -> x4, Pallas kernels: 355 us -> 325 us  [launch(): pl.pallas_call(body, out_shape=tuple(shapes), in_specs=in_specs, out_spec...]
    another operation x3 -> x0, other arithmetic: 5.04 us -> none
    unnamed x109 -> x93, local copies, waits for them, and re-layouts: 22.5 us -> 21.6 us
where the time goes in v5:
time: 379 us; the launch traced here: 374 us
  Pallas kernels  325 us (86%)
  other arithmetic  23.3 us (6%)
  local copies, waits for them, and re-layouts  23.2 us (6%)
    pallas_call x4, Pallas kernels, launch(): pl.pallas_call(body, out_shape=tuple(shapes), in_specs=in_specs, out_spec...  325 us
    unnamed x93, local copies, waits for them, and re-layouts  21.6 us
    sub x7, other arithmetic, adamw(): weight - rate_val * (first_hat / (jnp.sqrt(second_hat) + 1e-08) + decay_v...  20.2 us

profile of v5, /device:TPU:0, one launch (start us, length us, event | category | flops | bytes accessed | tf_op | source)
XLA Modules:
  0.0 373.6 jit_solution(4783781830907322421)
XLA Ops:
  2.4 0.8 select_maximum_fusion.refs_0_
  3.2 1.0 copy.64
  4.2 1.0 convert_bitcast_fusion.1
  5.2 1.3 convert_element_type.20.refs_2_.refs_4_
  6.5 2.2 copy-done
  8.7 1.6 copy-done.4
  10.3 33.5 %gather_line.1 = (f32[2,1024]{1,0:T(2,128)S(1)}, bf16[1024,128]{1,0:T(8,128)(2,1)S(1)}, bf16[4,3,128,1024]{3,2,1,0:T(8,128)(2,1)S(1)}, bf16[3,128,1024]{2,1,0:T(...) custom-call(f32[40,128]{1,0:T(8,128)S(1)} %select_maximum_fusion.refs_0_, ...), custom_call_target="tpu_custom_call" | custom-call | flops 1 | bytes 1 | tf_op jit(solution)/shard_map/gather_line/pallas_call | solution.py:240
  43.8 1.7 copy-done.2
  45.5 2.0 copy-done.5
  47.5 1.0 copy-done.10
  48.5 60.4 %attention.1 = (bf16[3,1024,1024]{2,1,0:T(8,128)(2,1)}, bf16[8,256,1024]{2,1,0:T(8,128)(2,1)}, bf16[1,3,128,1024]{3,2,1,0:T(8,128)(2,1)S(1)}, bf16[2,256,1024]{2...) custom-call(f32[256,1024]{1,0:T(8,128)} %refs_3_.3, ...), custom_call_target="tpu_custom_call" | custom-call | flops 1 | bytes 1 | tf_op jit(solution)/shard_map/attention/pallas_call | solution.py:240
  108.9 0.8 copy-done.6
  109.7 0.9 copy-done.11
  110.6 0.8 copy-done.12
  111.4 0.8 copy-done.13
  113.4 144.2 %experts.1 = (bf16[2,8,256,1024]{3,2,1,0:T(8,128)(2,1)}, f32[8,2,8,256]{3,2,1,0:T(8,128)}, f32[256,1024]{1,0:T(8,128)}, bf16[4,3,128,1024]{3,2,1,0:T(8,128)(2,1)...) custom-call(bf16[256,1024]{1,0:T(8,128)(2,1)} %copy-done.6, f32[8,8,256]{2,1,0:T(8,128)} %copy-done.15, ...), custom_call_target="tpu_custom_call" | custom-call | flops 1 | bytes 1 | tf_op jit(solution)/shard_map/experts/pallas_call | solution.py:240
  257.7 87.4 %attention_back.1 = (f32[256,1024]{1,0:T(8,128)}, f32[256,1024]{1,0:T(8,128)}, bf16[4,3,128,1024]{3,2,1,0:T(8,128)(2,1)}, f32[3,128,256]{2,1,0:T(8,128)}, f32[40,128]{1,0:T(8,128)}) custom-call(bf16[3,1024,1024]{2,1,0:T(8,128)(2,1)} %get-tuple-element.67.refs_0_, ...), custom_call_target="tpu_custom_call", output_to_operand_aliasing={{2}: (2, {})} | custom-call | flops 1 | bytes 1 | tf_op jit(solution)/shard_map/attention_back/pallas_call | solution.py:240
  345.1 8.5 %multiply_subtract_fusion.1 = (f32[4,128,1024]{2,1,0:T(8,128)}, f32[4,128,1024]{2,1,0:T(8,128)}, f32[4,128,1024]{2,1,0:T(8,128)}, f32[4,128,1024]{2,1,0:T(8,128)}) fusion(f32[4,128,1024]{2,1,0:T(8,128)} %refs_5_.2, f32[4,128,1024]{2,1,0:T(8,128)} %param.54, f32[4,128,1024]{2,1,0:T(8,128)} %param.55, bf16[4,3,128,1024]{3,2,1,0:T(8,128)(2,1)} %get-tuple-element.89, ...), kind=kLoop, calls=%fused_computation.7 | loop fusion | flops 9437184 | bytes 16777216 | tf_op jit(solution)/shard_map/sub | solution.py:1399
  353.7 1.1 copy-done.19
  354.8 1.2 copy-done.20
  356.1 8.6 %multiply_subtract_fusion = (f32[4,2,128,1024]{3,2,1,0:T(8,128)}, f32[4,2,128,1024]{3,2,1,0:T(8,128)}, f32[4,2,128,1024]{3,2,1,0:T(8,128)}, f32[4,2,128,1024]{3,2,1,0:T(8,128)}) fusion(f32[4,2,128,1024]{3,2,1,0:T(8,128)S(1)} %copy-done.1, f32[4,2,128,1024]{3,2,1,0:T(8,128)S(1)} %copy-done.19, f32[4,2,128,1024]{3,2,1,0:T(8,128)S(1)} %copy-done.20, ...), kind=kLoop, calls=%fused_computation.2 | loop fusion | flops 18874368 | bytes 33554432 | tf_op jit(solution)/shard_map/sub | solution.py:1399
  364.9 1.1 multiply_subtract_fusion.3
  371.2 1.0 copy.76
  372.2 1.0 copy.77
  (94 shorter events, 8.3 us)
Async XLA Ops:
  0.7 5.8 %copy-start.3 = (f32[256,1024]{1,0:T(8,128)S(1)}, f32[256,1024]{1,0:T(8,128)}, u32[]{:S(2)}) copy-start(f32[256,1024]{1,0:T(8,128)} %refs_3_.3) | copy-start | bytes 3145732
  10.3 38.2 %copy-start.7 = (f32[2,512,128]{2,1,0:T(8,128)S(1)}, f32[2,512,128]{2,1,0:T(8,128)}, u32[]{:S(2)}) copy-start(f32[2,512,128]{2,1,0:T(8,128)} %constant.133.clone.refs_8_.refs_17_) | copy-start | bytes 1572868
  10.3 38.2 %copy-start.8 = (f32[2,512,128]{2,1,0:T(8,128)S(1)}, f32[2,512,128]{2,1,0:T(8,128)}, u32[]{:S(2)}) copy-start(f32[2,512,128]{2,1,0:T(8,128)} %constant.134.clone.refs_9_.refs_18_) | copy-start | bytes 1572868
  10.3 38.2 %copy-start.17 = (s32[256,8]{0,1:T(8,128)S(1)}, s32[256,8]{0,1:T(8,128)}, u32[]{:S(2)}) copy-start(s32[256,8]{0,1:T(8,128)} %param.31) | copy-start | bytes 24580
  48.5 60.4 %copy-start.9 = (bf16[1024,128]{1,0:T(8,128)(2,1)}, bf16[1024,128]{1,0:T(8,128)(2,1)S(1)}, u32[]{:S(2)}) copy-start(bf16[1024,128]{1,0:T(8,128)(2,1)S(1)} %get-tuple-element.65.refs_6_.refs_16_) | copy-start | bytes 786436
  48.5 60.4 %copy-start.16 = (f32[2,1024]{1,0:T(2,128)}, f32[2,1024]{1,0:T(2,128)S(1)}, u32[]{:S(2)}) copy-start(f32[2,1024]{1,0:T(2,128)S(1)} %get-tuple-element.64.refs_5_.refs_15_) | copy-start | bytes 24580
  345.1 8.6 %copy-start.1 = (f32[4,2,128,1024]{3,2,1,0:T(8,128)S(1)}, f32[4,2,128,1024]{3,2,1,0:T(8,128)}, u32[]{:S(2)}) copy-start(f32[4,2,128,1024]{3,2,1,0:T(8,128)} %refs_4_.1) | copy-start | bytes 12582916
  345.1 8.6 %copy-start.18 = (bf16[4,3,128,1024]{3,2,1,0:T(8,128)(2,1)S(1)}, bf16[4,3,128,1024]{3,2,1,0:T(8,128)(2,1)}, u32[]{:S(2)}) copy-start(bf16[4,3,128,1024]{3,2,1,0:T(8,128)(2,1)} %get-tuple-element.89) | copy-start | bytes 9437188
  345.1 9.7 %copy-start.19 = (f32[4,2,128,1024]{3,2,1,0:T(8,128)S(1)}, f32[4,2,128,1024]{3,2,1,0:T(8,128)}, u32[]{:S(2)}) copy-start(f32[4,2,128,1024]{3,2,1,0:T(8,128)} %param.52) | copy-start | bytes 12582916
  345.1 10.9 %copy-start.20 = (f32[4,2,128,1024]{3,2,1,0:T(8,128)S(1)}, f32[4,2,128,1024]{3,2,1,0:T(8,128)}, u32[]{:S(2)}) copy-start(f32[4,2,128,1024]{3,2,1,0:T(8,128)} %param.53) | copy-start | bytes 12582916
  356.0 8.8 %copy-start.23 = (f32[3,128,256]{2,1,0:T(8,128)S(1)}, f32[3,128,256]{2,1,0:T(8,128)}, u32[]{:S(2)}) copy-start(f32[3,128,256]{2,1,0:T(8,128)} %get-tuple-element.87) | copy-start | bytes 1179652
  356.0 8.8 %copy-start.24 = (f32[128,256]{1,0:T(8,128)S(1)}, f32[128,256]{1,0:T(8,128)}, u32[]{:S(2)}) copy-start(f32[128,256]{1,0:T(8,128)} %param.34) | copy-start | bytes 393220
  356.0 8.8 %copy-start.25 = (f32[128,256]{1,0:T(8,128)S(1)}, f32[128,256]{1,0:T(8,128)}, u32[]{:S(2)}) copy-start(f32[128,256]{1,0:T(8,128)} %param.33) | copy-start | bytes 393220
  356.0 8.8 %copy-start.26 = (f32[128,256]{1,0:T(8,128)S(1)}, f32[128,256]{1,0:T(8,128)}, u32[]{:S(2)}) copy-start(f32[128,256]{1,0:T(8,128)} %param.44) | copy-start | bytes 393220
  356.0 8.8 %copy-start.27 = (f32[128,256]{1,0:T(8,128)S(1)}, f32[128,256]{1,0:T(8,128)}, u32[]{:S(2)}) copy-start(f32[128,256]{1,0:T(8,128)} %param.45) | copy-start | bytes 393220
  356.0 8.8 %copy-start.28 = (f32[128,256]{1,0:T(8,128)S(1)}, f32[128,256]{1,0:T(8,128)}, u32[]{:S(2)}) copy-start(f32[128,256]{1,0:T(8,128)} %param.43) | copy-start | bytes 393220
  356.0 8.8 %copy-start.29 = (f32[128,256]{1,0:T(8,128)S(1)}, f32[128,256]{1,0:T(8,128)}, u32[]{:S(2)}) copy-start(f32[128,256]{1,0:T(8,128)} %param.42) | copy-start | bytes 393220
  356.0 9.9 %copy-start.30 = (f32[256,128]{1,0:T(8,128)S(1)}, f32[256,128]{1,0:T(8,128)}, u32[]{:S(2)}) copy-start(f32[256,128]{1,0:T(8,128)} %param.46) | copy-start | bytes 393220
  356.1 10.0 %copy-start.31 = (f32[256,128]{1,0:T(8,128)S(1)}, f32[256,128]{1,0:T(8,128)}, u32[]{:S(2)}) copy-start(f32[256,128]{1,0:T(8,128)} %param.47) | copy-start | bytes 393220
  364.8 5.8 %copy-start.37 = (f32[32]{0:T(128)S(1)}, f32[32]{0:T(128)}, u32[]{:S(2)}) copy-start(f32[32]{0:T(128)} %param.36) | copy-start | bytes 388
  364.8 5.8 %copy-start.40 = (f32[32]{0:T(128)S(1)}, f32[32]{0:T(128)}, u32[]{:S(2)}) copy-start(f32[32]{0:T(128)} %param.48) | copy-start | bytes 388
  364.8 5.8 %copy-start.41 = (f32[32]{0:T(128)S(1)}, f32[32]{0:T(128)}, u32[]{:S(2)}) copy-start(f32[32]{0:T(128)} %param.49) | copy-start | bytes 388
  364.8 6.4 %copy-start.22 = (f32[256,1024]{1,0:T(8,128)S(1)}, f32[256,1024]{1,0:T(8,128)}, u32[]{:S(2)}) copy-start(f32[256,1024]{1,0:T(8,128)} %get-tuple-element.199) | copy-start | bytes 3145732
  364.9 7.3 %copy-start.21 = (f32[256,1024]{1,0:T(8,128)S(1)}, f32[256,1024]{1,0:T(8,128)}, u32[]{:S(2)}) copy-start(f32[256,1024]{1,0:T(8,128)} %get-tuple-element.200) | copy-start | bytes 3145732
  (18 other events, 47.2 us)

commit v6 on v5

--- a/solution.py
+++ b/solution.py
@@ -264,127 +264,6 @@
 
 
 NN, NT, TN = (1, 0), (1, 1), (0, 0)
-
-
-def prologue(n_dp, n_mp, identity, first_row, small, shards, cot, residual, gateup, down):
-    half = n_mp // 2
-    kinds, rows, cols = shards.shape
-    tokens, width = cot.shape
-    order_a, _ = orders_of(n_dp)
-    owned, _, hidden, _ = gateup.shape
-    n_devices = n_dp * n_mp
-    own_router = small.shape[0] - first_row
-    n_copies = 2 * (n_mp - 1) + 4 * (n_dp - 1) + 1
-
-    def gather_line(r):
-        dp, mp = lax.axis_index("dp"), lax.axis_index("mp")
-        me = (dp, mp)
-        neighbour = (dp, flip(mp, 1))
-        copies = Copies(r.send_sems, r.recv_sems)
-        loads = [
-            pltpu.make_async_copy(r.gateup, r.wide.at[:, pl.ds(0, 2)], r.local_sems.at[0]),
-            pltpu.make_async_copy(r.down, r.wide.at[:, 2], r.local_sems.at[1]),
-        ]
-        for copy in loads:
-            copy.start()
-        own_small = r.small_all.at[dp, mp]
-        own_cols = pl.ds(pl.multiple_of(mp * cols, cols), cols)
-        own_part = r.row_block.at[:, :, own_cols]
-        r.small_all[dp, mp] = r.small[...]
-        residual_rows = r.residual[...]
-        inverse = lax.rsqrt(jnp.mean(residual_rows * residual_rows, -1, keepdims=True) + NORM_EPS)
-        r.scaled[0] = (residual_rows * inverse).astype(BF16)
-        r.row_block[:, :, own_cols] = r.shards[...]
-        r.cots[0] = r.cot[...]
-        greet(
-            [(flip_all(dp, mask), mp) for mask in bits_of(n_dp)]
-            + [(dp, flip_all(mp, k)) for k in range(1, n_mp)]
-        )
-        near = lax.div(mp, half)
-        line = {}
-        for k in range(1, n_mp):
-            line[k] = (copies.slot(), copies.slot())
-            copies.start(r.small, own_small, (dp, flip_all(mp, k)), line[k][0])
-        across = copies.slot()
-        copies.start(r.scaled.at[0], r.scaled.at[1], neighbour, across)
-        for k in range(1, n_mp):
-            copies.start(r.shards, own_part, (dp, flip_all(mp, k)), line[k][1])
-
-        def small_tree(chunk):
-            first = pl.multiple_of(chunk * half, half)
-
-            def ref(j, mask=0):
-                return r.small_all.at[flip_all(dp, j), pl.ds(first, half)]
-
-            return TreeGather(copies, order_a, n_dp, me, ref, ref)
-
-        small_trees = [small_tree(chunk) for chunk in (near, 1 - near)]
-        cot_trees = row_trees(copies, n_dp, me, r.cots)
-        for chunk in (0, 1):
-            for k in range(1, half) if chunk == 0 else range(half, n_mp):
-                copies.wait(r.small_all.at[dp, flip_all(mp, k)], me, line[k][0])
-            small_trees[chunk].send(0)
-        for one in cot_trees:
-            one.send(0)
-        for copy in loads:
-            copy.wait()
-        for e in range(owned):
-            r.narrow[e] = r.wide[e].astype(BF16)
-        store = pltpu.make_async_copy(r.narrow, r.packed, r.local_sems.at[2])
-        store.start()
-        top = n_dp.bit_length() - 1
-        for level in range(1, top + 1):
-            run_level(small_trees, level)
-            run_level(cot_trees, level)
-        n_tiles = width // 128
-        for row in (0, 1):
-            for tile in range(n_tiles):
-                total = None
-                for at in range(tile * n_devices // n_tiles, (tile + 1) * n_devices // n_tiles):
-                    part = r.small_all[at // n_mp, at % n_mp, row : row + 1, :]
-                    total = part if total is None else total + part
-                r.gains[row : row + 1, tile * 128 : (tile + 1) * 128] = total
-        for at in range(n_devices):
-            r.router_wide[at * own_router : (at + 1) * own_router, :] = r.small_all[
-                at // n_mp, at % n_mp, first_row:, :
-            ]
-        r.router[...] = r.router_wide[...].astype(BF16)
-        for k in range(1, n_mp):
-            other = pl.multiple_of(flip_all(mp, k) * cols, cols)
-            copies.wait(r.row_block.at[:, :, pl.ds(other, cols)], me, line[k][1])
-        copies.wait(r.scaled.at[1], me, across)
-        store.wait()
-        copies.finish()
-
-    return launch(
-        gather_line,
-        identity,
-        dict(
-            small=(small, vmem()),
-            shards=(shards, vmem()),
-            cot=(cot, vmem()),
-            residual=(residual, vmem()),
-            gateup=(gateup, hbm()),
-            down=(down, hbm()),
-        ),
-        dict(
-            gains=(single(2, width), vmem()),
-            router=(low(width, 128), vmem()),
-            packed=(low(owned, 3, hidden, width), hbm()),
-            row_block=(low(kinds, rows, n_mp * cols), vmem()),
-            cots=(low(n_dp, tokens, width), vmem()),
-            scaled=(low(2, tokens, width), vmem()),
-        ),
-        dict(
-            small_all=pltpu.VMEM((n_dp, n_mp) + small.shape, F32),
-            router_wide=pltpu.VMEM((width, 128), F32),
-            wide=pltpu.VMEM((owned, 3, hidden, width), F32),
-            narrow=pltpu.VMEM((owned, 3, hidden, width), BF16),
-            local_sems=pltpu.SemaphoreType.DMA((3,)),
-        ),
-        n_copies,
-        32 << 20,
-    )
 
 
 def run_level(trees, level):
@@ -492,45 +371,118 @@
     return raised / jnp.sum(raised, -1, keepdims=True)
 
 
+def store_blocks(trees, level, source, target, sems):
+    stores = []
+    for j in range(source.shape[0]) if trees else []:
+        if trees[0].level(j) == level:
+            stores.append(pltpu.make_async_copy(source.at[j], target.at[j], sems.at[j]))
+            stores[-1].start()
+    return stores
+
+
 def attention_forward(
-    n_dp, n_mp, groups, identity, residual, ids, start, cot, tables, experts
+    n_dp, n_mp, groups, identity, first_row, small, shards, cot, residual, gateup, down, ids, tables, experts
 ):
     tokens, width = residual.shape
-    kinds, rows, _ = start.row_block.shape
+    half = n_mp // 2
+    kinds, rows, cols = shards.shape
     part_rows = rows // 2
+    half_cols = half * cols
     n_heads = width // 128
     span = n_mp // groups
-    owned = EXPERTS // n_dp
+    owned, _, hidden, _ = gateup.shape
+    n_devices = n_dp * n_mp
+    own_router = small.shape[0] - first_row
     n_experts = len(experts)
-    n_copies = 4 * (n_dp - 1) + n_experts * (span - 1) + 1
+    order_a, _ = orders_of(n_dp)
+    n_copies = 2 * (n_mp - 1) + 10 * (n_dp - 1) + 2 + n_experts * (span - 1)
 
     def attention(r):
         dp, mp = lax.axis_index("dp"), lax.axis_index("mp")
         me = (dp, mp)
+        neighbour = (dp, flip(mp, 1))
         partner = (dp, flip_all(mp, span))
         copies = Copies(r.send_sems, r.recv_sems)
-        r.full[:, pl.ds(pl.multiple_of(dp * rows, rows), rows), :] = r.row_block[...]
+        loads = [
+            pltpu.make_async_copy(r.gateup, r.wide.at[:, pl.ds(0, 2)], r.local_sems.at[0]),
+            pltpu.make_async_copy(r.down, r.wide.at[:, 2], r.local_sems.at[1]),
+        ]
+        for copy in loads:
+            copy.start()
+        own_small = r.small_all.at[dp, mp]
+        own_rows = pl.ds(pl.multiple_of(dp * rows, rows), rows)
+        own_cols = pl.ds(pl.multiple_of(mp * cols, cols), cols)
+        own_part = r.full.at[:, own_rows, own_cols]
+        r.small_all[dp, mp] = r.small[...]
+        residual = r.residual[...]
+        inverse = lax.rsqrt(jnp.mean(residual * residual, -1, keepdims=True) + NORM_EPS)
+        r.scaled[0] = (residual * inverse).astype(BF16)
+        r.full[:, own_rows, own_cols] = r.shards[...]
+        r.cots[0] = r.cot[...]
         greet(
             [(flip_all(dp, mask), mp) for mask in bits_of(n_dp)]
-            + [partner] * (groups - 1)
-            + [(dp, flip_all(mp, k)) for k in range(1, span)]
+            + [(dp, flip_all(mp, k)) for k in range(1, n_mp)]
         )
-        across = copies.slot()
+        line = {}
+        for k in range(1, n_mp):
+            line[k] = (copies.slot(), copies.slot())
+            copies.start(r.small, own_small, (dp, flip_all(mp, k)), line[k][0])
+        for k in range(1, n_mp):
+            copies.start(r.shards, own_part, (dp, flip_all(mp, k)), line[k][1])
+        across = (copies.slot(), copies.slot())
+        copies.start(r.scaled.at[0], r.scaled.at[1], neighbour, across[0])
         if groups > 1:
-            copies.start(r.cot, r.cots.at[0], partner, across)
-
-        def tree(part, order):
+            copies.start(r.cot, r.other_cots.at[0], partner, across[1])
+        near = lax.div(mp, half)
+        chunks = (near, 1 - near)
+        chunk_cols = [
+            pl.ds(pl.multiple_of(chunk * half_cols, half_cols), half_cols) for chunk in chunks
+        ]
+
+        def small_tree(chunk):
+            first = pl.multiple_of(chunk * half, half)
+
+            def ref(j, mask=0):
+                return r.small_all.at[flip_all(dp, j), pl.ds(first, half)]
+
+            return TreeGather(copies, order_a, n_dp, me, ref, ref)
+
+        def weight_tree(chunk, part, order):
             def ref(j, mask=0):
                 start = flip_all(dp, j) * rows + part * part_rows
-                return r.full.at[:, pl.ds(pl.multiple_of(start, part_rows), part_rows), :]
+                there = pl.ds(pl.multiple_of(start, part_rows), part_rows)
+                return r.full.at[:, there, chunk_cols[chunk]]
 
             return TreeGather(copies, order, n_dp, me, ref, ref)
 
-        weight_trees = [tree(part, order) for part, order in enumerate(orders_of(n_dp))]
-        cot_trees = row_trees(copies, n_dp, me, r.cots) if groups > 1 else []
-        for one in weight_trees:
-            one.send(0)
-        sent = send_experts(copies, me, span, r.packed, r.near, experts)
+        def wait_line(first, end, which):
+            for k in range(first, end):
+                other = flip_all(mp, k)
+                if which:
+                    there = pl.ds(pl.multiple_of(other * cols, cols), cols)
+                    copies.wait(r.full.at[:, own_rows, there], me, line[k][1])
+                else:
+                    copies.wait(r.small_all.at[dp, other], me, line[k][0])
+
+        small_trees = [small_tree(chunk) for chunk in chunks]
+        weight_trees = [
+            [weight_tree(chunk, part, order) for part, order in enumerate(orders_of(n_dp))]
+            for chunk in (0, 1)
+        ]
+        cot_trees = row_trees(copies, n_dp, me, r.cots)
+        other_trees = row_trees(copies, n_dp, me, r.other_cots) if groups > 1 else []
+
+        def send_own(trees):
+            for one in trees:
+                one.send(0)
+
+        top = n_dp.bit_length() - 1
+        wait_line(1, half, 0)
+        send_own(small_trees[:1])
+        wait_line(half, n_mp, 0)
+        send_own(small_trees[1:])
+        send_own(cot_trees)
+        stores = store_blocks(cot_trees, 0, r.cots, r.cots_out, r.cot_sems)
         named = lax.broadcasted_iota(jnp.int32, (EXPERTS, tokens), 0)
         chosen = jnp.zeros((EXPERTS, tokens), F32)
         for k in range(TOPK):
@@ -543,50 +495,96 @@
         for expert in range(EXPERTS):
             owner, which = divmod(expert, owned)
             r.table[owner, which, :] = place[expert]
+        wait_line(1, half, 1)
+        send_own(weight_trees[0])
+        for copy in loads:
+            copy.wait()
+        for e in range(owned):
+            r.narrow[e] = r.wide[e].astype(BF16)
+        stores.append(pltpu.make_async_copy(r.narrow, r.packed, r.local_sems.at[2]))
+        stores[-1].start()
+        for level in range(1, top + 1):
+            if level == top:
+                wait_line(half, n_mp, 1)
+                send_own(weight_trees[1])
+            run_level(small_trees, level)
+            run_level(cot_trees, level)
+            stores += store_blocks(cot_trees, level, r.cots, r.cots_out, r.cot_sems)
+            run_level(weight_trees[0], level)
+        n_tiles = width // 128
+        for row in (0, 1):
+            for tile in range(n_tiles):
+                total = None
+                for at in range(tile * n_devices // n_tiles, (tile + 1) * n_devices // n_tiles):
+                    part = r.small_all[at // n_mp, at % n_mp, row : row + 1, :]
+                    total = part if total is None else total + part
+                r.gains[row : row + 1, tile * 128 : (tile + 1) * 128] = total
+        for at in range(n_devices):
+            r.router_wide[at * own_router : (at + 1) * own_router, :] = r.small_all[
+                at // n_mp, at % n_mp, first_row:, :
+            ]
+        r.router[...] = r.router_wide[...].astype(BF16)
+        copies.wait(r.scaled.at[1], me, across[0])
         residual = r.residual[...]
         inverse = lax.rsqrt(jnp.mean(residual * residual, -1, keepdims=True) + NORM_EPS)
         gain_one = r.gains[0:1, :]
         r.normed[0] = (residual * inverse * gain_one).astype(BF16)
         r.normed[1] = (r.scaled[1].astype(F32) * gain_one).astype(BF16)
         mask = seen(tokens, mp)
-        top = n_dp.bit_length() - 1
-        for level in range(1, top + 1):
-            if level == top and groups > 1:
-                copies.wait(r.cots.at[0], me, across)
-                for one in cot_trees:
-                    one.send(0)
-            run_level(weight_trees, level)
-        r.q[...] = dot(r.normed[0], r.full[0], NN)
-        for part in (0, 1):
-            r.kv[part] = dot(r.normed[part], r.full[1], NN)
-        run_level(cot_trees, 1)
         which = lax.rem(mp, 2)
 
         def table(ref, at):
             there = pl.ds(pl.multiple_of(at * tokens, tokens), tokens)
             return ref[0, there, :], ref[1, there, :]
 
-        def head(k, carry):
-            lanes = pl.ds(pl.multiple_of(k * 128, 128), 128)
-            queries = rotate(r.q[:, lanes], *table(r.query_table, which))
-            r.queries[:, lanes] = queries.astype(BF16)
-            parts = []
-            for part, at in enumerate((which, 1 - which)):
-                parts.append(rotate(r.kv[part, :, lanes], *table(r.key_table, at)))
-                r.keyval[part, :, lanes] = parts[part].astype(BF16)
-            both, keys, values = group_operands(queries, jnp.concatenate(parts, 0))
-            chance = softmax_of(both, keys, mask).astype(BF16)
-            r.context[:, lanes] = merge_heads(dot(chance, values, NN)).astype(BF16)
-            return carry
-
+        def project(chunk):
+            there = chunk_cols[chunk]
+            r.q[:, there] = dot(r.normed[0], r.full[0, :, there], NN)
+            for part in (0, 1):
+                r.kv[part, :, there] = dot(r.normed[part], r.full[1, :, there], NN)
+
+        def heads(chunk, first, end):
+            def head(k, carry):
+                number = chunks[chunk] * (n_heads // 2) + k
+                lanes = pl.ds(pl.multiple_of(number * 128, 128), 128)
+                queries = rotate(r.q[:, lanes], *table(r.query_table, which))
+                r.queries[:, lanes] = queries.astype(BF16)
+                parts = []
+                for part, at in enumerate((which, 1 - which)):
+                    parts.append(rotate(r.kv[part, :, lanes], *table(r.key_table, at)))
+                    r.keyval[part, :, lanes] = parts[part].astype(BF16)
+                both, keys, values = group_operands(queries, jnp.concatenate(parts, 0))
+                chance = softmax_of(both, keys, mask).astype(BF16)
+                r.context[:, lanes] = merge_heads(dot(chance, values, NN)).astype(BF16)
+                return carry
+
+            lax.fori_loop(first, end, head, 0)
+
+        run_level(weight_trees[1], 1)
+        if groups > 1:
+            copies.wait(r.other_cots.at[0], me, across[1])
+        send_own(other_trees)
+        stores += store_blocks(other_trees, 0, r.other_cots, r.other_out, r.other_sems)
+        sent = send_experts(copies, me, span, r.narrow, r.near, experts)
+        project(0)
+        heads(0, 0, 2)
         for level in range(2, top + 1):
-            first, end = [(level - 2 + i) * n_heads // (top - 1) for i in (0, 1)]
-            lax.fori_loop(first, end, head, 0)
-            run_level(cot_trees, level)
-        hidden = r.residual[...] + dot(r.context[...], r.full[2], NT)
-        r.hidden[...] = hidden
-        inverse = lax.rsqrt(jnp.mean(hidden * hidden, -1, keepdims=True) + NORM_EPS)
-        normed = (hidden * inverse * r.gains[1:2, :]).astype(BF16)
+            run_level(weight_trees[1], level)
+        stores.append(pltpu.make_async_copy(r.full, r.full_out, r.local_sems.at[3]))
+        stores[-1].start()
+        heads(0, 2, n_heads // 2)
+        project(1)
+        n_left = n_heads // 2
+        for level in range(1, top + 1):
+            run_level(other_trees, level)
+            stores += store_blocks(other_trees, level, r.other_cots, r.other_out, r.other_sems)
+            if level < top:
+                first, end = [(level - 1 + i) * n_left // (top - 1) for i in (0, 1)]
+                heads(1, first, end)
+        hidden_rows = r.residual[...] + dot(r.context[...], r.full[2], NT)
+        r.hidden[...] = hidden_rows
+        inverse = lax.rsqrt(jnp.mean(hidden_rows * hidden_rows, -1, keepdims=True) + NORM_EPS)
+        normed = (hidden_rows * inverse * r.gains[1:2, :]).astype(BF16)
         r.normed_two[...] = normed
         logits = dot(normed, r.router[...], NN)
         lane = lax.broadcasted_iota(jnp.int32, logits.shape, 1)
@@ -598,27 +596,32 @@
             owner, which = divmod(expert, owned)
             r.table[owner, 4 + which, :] = turned[expert]
         wait_experts(copies, me, r.near, sent)
+        for copy in stores:
+            copy.wait()
         copies.finish()
 
     return launch(
         attention,
         identity,
         dict(
+            small=(small, vmem()),
+            shards=(shards, vmem()),
+            cot=(cot, vmem()),
             residual=(residual, vmem()),
+            gateup=(gateup, hbm()),
+            down=(down, hbm()),
             ids=(ids, vmem()),
-            scaled=(start.scaled, vmem()),
-            row_block=(start.row_block, vmem()),
-            cot=(cot, vmem()),
-            gains=(start.gains, vmem()),
-            router=(start.router, vmem()),
-            packed=(start.packed, hbm()),
             query_table=(tables[0], vmem()),
             key_table=(tables[1], vmem()),
         ),
         dict(
-            full=(low(kinds, n_dp * rows, width), vmem()),
-            cots=(low(n_dp, tokens, width), vmem()),
-            near=([low(n_experts, *start.packed.shape[1:]) for _ in range(1, span)], hbm()),
+            gains=(single(2, width), vmem()),
+            router=(low(width, 128), vmem()),
+            packed=(low(owned, 3, hidden, width), hbm()),
+            full_out=(low(kinds, n_dp * rows, width), hbm()),
+            cots_out=(low(n_dp, tokens, width), hbm()),
+            other_out=(low(n_dp, tokens, width), hbm()),
+            near=([low(n_experts, 3, hidden, width) for _ in range(1, span)], hbm()),
             normed=(low(2, tokens, width), vmem()),
             queries=(low(tokens, width), vmem()),
             keyval=(low(2, tokens, width), vmem()),
@@ -629,11 +632,22 @@
             table=(single(n_dp, 8, tokens), vmem()),
         ),
         dict(
+            full=pltpu.VMEM((kinds, n_dp * rows, width), BF16),
+            cots=pltpu.VMEM((n_dp, tokens, width), BF16),
+            other_cots=pltpu.VMEM((n_dp, tokens, width), BF16),
+            scaled=pltpu.VMEM((2, tokens, width), BF16),
+            small_all=pltpu.VMEM((n_dp, n_mp) + small.shape, F32),
+            router_wide=pltpu.VMEM((width, 128), F32),
+            wide=pltpu.VMEM((owned, 3, hidden, width), F32),
+            narrow=pltpu.VMEM((owned, 3, hidden, width), BF16),
             q=pltpu.VMEM((tokens, width), F32),
             kv=pltpu.VMEM((2, tokens, width), F32),
+            local_sems=pltpu.SemaphoreType.DMA((4,)),
+            cot_sems=pltpu.SemaphoreType.DMA((n_dp,)),
+            other_sems=pltpu.SemaphoreType.DMA((n_dp,)),
         ),
         n_copies,
-        48 << 20,
+        60 << 20,
     )
 
 
@@ -1455,30 +1469,39 @@
         ]
     )
     shards = jnp.stack([query_w, key_value_weight, output_w.T]).astype(BF16)
-    cot_low = cotangent.astype(BF16)
-    start = prologue(
-        n_dp, n_mp, 0, first_row, small, shards, cot_low, residual_in, gateup_w, down_w
-    )
     tables = [jnp.asarray(table) for table in rotary_constants()]
     early = list(range(owned))[:1]
     front = attention_forward(
-        n_dp, n_mp, groups, 1, residual_in, expert_ids.T, start, cot_low, tables, early
+        n_dp,
+        n_mp,
+        groups,
+        0,
+        first_row,
+        small,
+        shards,
+        cotangent.astype(BF16),
+        residual_in,
+        gateup_w,
+        down_w,
+        expert_ids.T,
+        tables,
+        early,
     )
 
     found = run_experts(
         n_dp,
         n_mp,
         groups,
-        2,
+        1,
         front.normed_two,
         front.table,
-        [start.cots, front.cots][:groups],
-        start.packed,
+        [front.cots_out, front.other_out][:groups],
+        front.packed,
         [(early, front.near)],
     )
 
     given = types.SimpleNamespace(
-        full=front.full,
+        full=front.full_out,
         residual=residual_in,
         hidden=front.hidden,
         cotangent=cotangent,
@@ -1493,11 +1516,11 @@
         queries=front.queries,
         keyval=front.keyval,
         context=front.context,
-        gains=start.gains,
-        router=start.router,
+        gains=front.gains,
+        router=front.router,
         tables=tables,
     )
-    back = attention_backward(n_dp, n_mp, groups, 3, given, first_row)
+    back = attention_backward(n_dp, n_mp, groups, 2, given, first_row)
     input_grad, block_out = back.input_grad, back.block_out
     gateup_grad, down_grad = (
         sum(part[:, cut].astype(F32) for part in [found.grad_own] + back.arrived)

time: 379 us -> 356 us (0.939)
  local copies, waits for them, and re-layouts: 23.2 us -> 10.2 us
  Pallas kernels: 325 us -> 313 us
    unnamed x93 -> x59, local copies, waits for them, and re-layouts: 21.6 us -> 8.61 us
    pallas_call x4 -> x3, Pallas kernels: 325 us -> 313 us  [launch(): pl.pallas_call(body, out_shape=tuple(shapes), in_specs=in_specs, out_spec...]
where the time goes in v6:
time: 356 us; the launch traced here: 350 us
  Pallas kernels  313 us (88%)
  other arithmetic  25.4 us (7%)
  local copies, waits for them, and re-layouts  10.2 us (3%)
    pallas_call x3, Pallas kernels, launch(): pl.pallas_call(body, out_shape=tuple(shapes), in_specs=in_specs, out_spec...  313 us
    sub x7, other arithmetic, adamw(): weight - rate_val * (first_hat / (jnp.sqrt(second_hat) + 1e-08) + decay_v...  20.2 us
    unnamed x59, local copies, waits for them, and re-layouts  8.61 us

profile of v6, /device:TPU:0, one launch (start us, length us, event | category | flops | bytes accessed | tf_op | source)
XLA Modules:
  0.0 350.1 jit_solution(7461147086313214322)
XLA Ops:
  0.7 0.7 tile.20
  1.4 0.7 tile.8
  2.3 1.4 select_maximum_fusion.refs_0_
  3.7 1.0 copy.64
  4.7 1.0 convert_bitcast_fusion.1
  5.7 0.7 pad_maximum_fusion.refs_1_
  6.4 2.1 convert_element_type.20.refs_2_
  8.5 81.5 %attention.1 = (f32[2,1024]{1,0:T(2,128)}, bf16[1024,128]{1,0:T(8,128)(2,1)}, bf16[4,3,128,1024]{3,2,1,0:T(8,128)(2,1)}, bf16[3,1024,1024]{2,1,0:T(8,128)(2,1)},...) custom-call(f32[40,128]{1,0:T(8,128)} %select_maximum_fusion.refs_0_, ...), custom_call_target="tpu_custom_call" | custom-call | flops 1 | bytes 1 | tf_op jit(solution)/shard_map/attention/pallas_call | solution.py:240
  89.9 144.1 %experts.1 = (bf16[2,8,256,1024]{3,2,1,0:T(8,128)(2,1)}, f32[8,2,8,256]{3,2,1,0:T(8,128)}, f32[256,1024]{1,0:T(8,128)}, bf16[4,3,128,1024]{3,2,1,0:T(8,128)(2,1)...) custom-call(bf16[256,1024]{1,0:T(8,128)(2,1)} %get-tuple-element.61.refs_0_.refs_11_, ...), custom_call_target="tpu_custom_call" | custom-call | flops 1 | bytes 1 | tf_op jit(solution)/shard_map/experts/pallas_call | solution.py:240
  234.0 87.5 %attention_back.1 = (f32[256,1024]{1,0:T(8,128)}, f32[256,1024]{1,0:T(8,128)}, bf16[4,3,128,1024]{3,2,1,0:T(8,128)(2,1)}, f32[3,128,256]{2,1,0:T(8,128)}, f32[40,128]{1,0:T(8,128)}) custom-call(bf16[3,1024,1024]{2,1,0:T(8,128)(2,1)} %get-tuple-element.60.refs_0_, ...), custom_call_target="tpu_custom_call", output_to_operand_aliasing={{2}: (2, {})} | custom-call | flops 1 | bytes 1 | tf_op jit(solution)/shard_map/attention_back/pallas_call | solution.py:240
  321.5 8.5 %multiply_subtract_fusion.1 = (f32[4,128,1024]{2,1,0:T(8,128)}, f32[4,128,1024]{2,1,0:T(8,128)}, f32[4,128,1024]{2,1,0:T(8,128)}, f32[4,128,1024]{2,1,0:T(8,128)}) fusion(f32[4,128,1024]{2,1,0:T(8,128)} %refs_5_.2, f32[4,128,1024]{2,1,0:T(8,128)} %param.54, f32[4,128,1024]{2,1,0:T(8,128)} %param.55, bf16[4,3,128,1024]{3,2,1,0:T(8,128)(2,1)} %get-tuple-element.85, ...), kind=kLoop, calls=%fused_computation.7 | loop fusion | flops 9437184 | bytes 16777216 | tf_op jit(solution)/shard_map/sub | solution.py:1413
  330.1 1.1 copy-done.2
  331.2 1.2 copy-done.3
  332.5 8.6 %multiply_subtract_fusion = (f32[4,2,128,1024]{3,2,1,0:T(8,128)}, f32[4,2,128,1024]{3,2,1,0:T(8,128)}, f32[4,2,128,1024]{3,2,1,0:T(8,128)}, f32[4,2,128,1024]{3,2,1,0:T(8,128)}) fusion(f32[4,2,128,1024]{3,2,1,0:T(8,128)S(1)} %copy-done, f32[4,2,128,1024]{3,2,1,0:T(8,128)S(1)} %copy-done.2, f32[4,2,128,1024]{3,2,1,0:T(8,128)S(1)} %copy-done.3, ...), kind=kLoop, calls=%fused_computation.2 | loop fusion | flops 18874368 | bytes 33554432 | tf_op jit(solution)/shard_map/sub | solution.py:1413
  341.3 1.1 multiply_subtract_fusion.3
  342.7 0.8 copy.70
  343.5 0.8 copy.71
  344.2 0.8 copy.72
  345.0 0.8 copy.69
  345.8 0.6 multiply_subtract_fusion.5
  346.4 0.6 multiply_subtract_fusion.7
  347.1 0.6 multiply_subtract_fusion.6
  347.7 1.0 copy.76
  348.6 1.0 copy.77
  (59 shorter events, 0.7 us)
Async XLA Ops:
  321.5 8.6 %copy-start = (f32[4,2,128,1024]{3,2,1,0:T(8,128)S(1)}, f32[4,2,128,1024]{3,2,1,0:T(8,128)}, u32[]{:S(2)}) copy-start(f32[4,2,128,1024]{3,2,1,0:T(8,128)} %refs_4_.1) | copy-start | bytes 12582916
  321.5 8.6 %copy-start.1 = (bf16[4,3,128,1024]{3,2,1,0:T(8,128)(2,1)S(1)}, bf16[4,3,128,1024]{3,2,1,0:T(8,128)(2,1)}, u32[]{:S(2)}) copy-start(bf16[4,3,128,1024]{3,2,1,0:T(8,128)(2,1)} %get-tuple-element.85) | copy-start | bytes 9437188
  321.5 9.7 %copy-start.2 = (f32[4,2,128,1024]{3,2,1,0:T(8,128)S(1)}, f32[4,2,128,1024]{3,2,1,0:T(8,128)}, u32[]{:S(2)}) copy-start(f32[4,2,128,1024]{3,2,1,0:T(8,128)} %param.52) | copy-start | bytes 12582916
  321.5 10.9 %copy-start.3 = (f32[4,2,128,1024]{3,2,1,0:T(8,128)S(1)}, f32[4,2,128,1024]{3,2,1,0:T(8,128)}, u32[]{:S(2)}) copy-start(f32[4,2,128,1024]{3,2,1,0:T(8,128)} %param.53) | copy-start | bytes 12582916
  332.4 8.8 %copy-start.6 = (f32[3,128,256]{2,1,0:T(8,128)S(1)}, f32[3,128,256]{2,1,0:T(8,128)}, u32[]{:S(2)}) copy-start(f32[3,128,256]{2,1,0:T(8,128)} %get-tuple-element.83) | copy-start | bytes 1179652
  332.4 8.8 %copy-start.7 = (f32[128,256]{1,0:T(8,128)S(1)}, f32[128,256]{1,0:T(8,128)}, u32[]{:S(2)}) copy-start(f32[128,256]{1,0:T(8,128)} %param.34) | copy-start | bytes 393220
  332.4 8.8 %copy-start.8 = (f32[128,256]{1,0:T(8,128)S(1)}, f32[128,256]{1,0:T(8,128)}, u32[]{:S(2)}) copy-start(f32[128,256]{1,0:T(8,128)} %param.33) | copy-start | bytes 393220
  332.4 8.8 %copy-start.9 = (f32[128,256]{1,0:T(8,128)S(1)}, f32[128,256]{1,0:T(8,128)}, u32[]{:S(2)}) copy-start(f32[128,256]{1,0:T(8,128)} %param.44) | copy-start | bytes 393220
  332.4 8.8 %copy-start.10 = (f32[128,256]{1,0:T(8,128)S(1)}, f32[128,256]{1,0:T(8,128)}, u32[]{:S(2)}) copy-start(f32[128,256]{1,0:T(8,128)} %param.45) | copy-start | bytes 393220
  332.5 8.8 %copy-start.11 = (f32[128,256]{1,0:T(8,128)S(1)}, f32[128,256]{1,0:T(8,128)}, u32[]{:S(2)}) copy-start(f32[128,256]{1,0:T(8,128)} %param.43) | copy-start | bytes 393220
  332.5 8.8 %copy-start.12 = (f32[128,256]{1,0:T(8,128)S(1)}, f32[128,256]{1,0:T(8,128)}, u32[]{:S(2)}) copy-start(f32[128,256]{1,0:T(8,128)} %param.42) | copy-start | bytes 393220
  332.5 9.9 %copy-start.13 = (f32[256,128]{1,0:T(8,128)S(1)}, f32[256,128]{1,0:T(8,128)}, u32[]{:S(2)}) copy-start(f32[256,128]{1,0:T(8,128)} %param.46) | copy-start | bytes 393220
  332.5 10.0 %copy-start.14 = (f32[256,128]{1,0:T(8,128)S(1)}, f32[256,128]{1,0:T(8,128)}, u32[]{:S(2)}) copy-start(f32[256,128]{1,0:T(8,128)} %param.47) | copy-start | bytes 393220
  341.1 4.6 %copy-start.15 = (f32[32,32]{1,0:T(8,128)S(1)}, f32[32,32]{1,0:T(8,128)}, u32[]{:S(2)}) copy-start(f32[32,32]{1,0:T(8,128)} %param.37) | copy-start | bytes 12292
  341.1 4.6 %copy-start.16 = (f32[32,32]{1,0:T(8,128)S(1)}, f32[32,32]{1,0:T(8,128)}, u32[]{:S(2)}) copy-start(f32[32,32]{1,0:T(8,128)} %param.50) | copy-start | bytes 12292
  341.1 4.6 %copy-start.17 = (f32[32,32]{1,0:T(8,128)S(1)}, f32[32,32]{1,0:T(8,128)}, u32[]{:S(2)}) copy-start(f32[32,32]{1,0:T(8,128)} %param.51) | copy-start | bytes 12292
  341.2 5.3 %copy-start.19 = (f32[32]{0:T(128)S(1)}, f32[32]{0:T(128)}, u32[]{:S(2)}) copy-start(f32[32]{0:T(128)} %param.32) | copy-start | bytes 388
  341.2 5.2 %copy-start.21 = (f32[32]{0:T(128)S(1)}, f32[32]{0:T(128)}, u32[]{:S(2)}) copy-start(f32[32]{0:T(128)} %param.40) | copy-start | bytes 388
  341.2 5.2 %copy-start.22 = (f32[32]{0:T(128)S(1)}, f32[32]{0:T(128)}, u32[]{:S(2)}) copy-start(f32[32]{0:T(128)} %param.41) | copy-start | bytes 388
  341.2 5.8 %copy-start.20 = (f32[32]{0:T(128)S(1)}, f32[32]{0:T(128)}, u32[]{:S(2)}) copy-start(f32[32]{0:T(128)} %param.36) | copy-start | bytes 388
  341.2 5.8 %copy-start.23 = (f32[32]{0:T(128)S(1)}, f32[32]{0:T(128)}, u32[]{:S(2)}) copy-start(f32[32]{0:T(128)} %param.48) | copy-start | bytes 388
  341.2 5.8 %copy-start.24 = (f32[32]{0:T(128)S(1)}, f32[32]{0:T(128)}, u32[]{:S(2)}) copy-start(f32[32]{0:T(128)} %param.49) | copy-start | bytes 388
  341.2 6.4 %copy-start.5 = (f32[256,1024]{1,0:T(8,128)S(1)}, f32[256,1024]{1,0:T(8,128)}, u32[]{:S(2)}) copy-start(f32[256,1024]{1,0:T(8,128)} %get-tuple-element.195) | copy-start | bytes 3145732
  341.3 7.3 %copy-start.4 = (f32[256,1024]{1,0:T(8,128)S(1)}, f32[256,1024]{1,0:T(8,128)}, u32[]{:S(2)}) copy-start(f32[256,1024]{1,0:T(8,128)} %get-tuple-element.196) | copy-start | bytes 3145732
  (1 other events, 4.6 us)

commit v7 on v6

--- a/solution.py
+++ b/solution.py
@@ -1136,6 +1136,20 @@
         if groups > 1:
             across = copies.slot()
             copies.start(r.rows, r.rows_all.at[1, 0], peers[1, 0], across)
+        weights_sent, grads_sent = {}, {}
+
+        def send_weights(e):
+            for k in range(1, span):
+                weights_sent[e, k] = copies.slot()
+                copies.start(
+                    r.packed.at[e],
+                    r.weights.at[e, :, units_of(k)],
+                    (dp, flip_all(mp, k)),
+                    weights_sent[e, k],
+                )
+
+        for e in coming[:1]:
+            send_weights(e)
         sent = {}
         for (group, j), device in peers.items():
             sent[group, j] = copies.slot()
@@ -1232,7 +1246,6 @@
                 else:
                     stores.append(load(source, r.late[k - 1].at[e - n_sent]))
 
-        weights_sent, grads_sent = {}, {}
         ready(0)
         done = 0
         leaving = []
@@ -1247,15 +1260,8 @@
                     tree.send(0)
             if group == groups - 1 and j == 0:
                 leaving += copies.split()
-                for e in coming:
-                    for k in range(1, span):
-                        weights_sent[e, k] = copies.slot()
-                        copies.start(
-                            r.packed.at[e],
-                            r.weights.at[e, :, units_of(k)],
-                            (dp, flip_all(mp, k)),
-                            weights_sent[e, k],
-                        )
+                for e in coming[1:]:
+                    send_weights(e)
                 staying = copies.split()
             fill(number)
             if number % per_tile == per_tile - 1 and number < blocks - 1:

time: 356 us -> 354 us (level)
  no operation moved by 1% of the time
where the time goes in v7:
time: 354 us; the launch traced here: 348 us
  Pallas kernels  311 us (88%)
  other arithmetic  25.4 us (7%)
  local copies, waits for them, and re-layouts  10.2 us (3%)
    pallas_call x3, Pallas kernels, launch(): pl.pallas_call(body, out_shape=tuple(shapes), in_specs=in_specs, out_spec...  311 us
    sub x7, other arithmetic, adamw(): weight - rate_val * (first_hat / (jnp.sqrt(second_hat) + 1e-08) + decay_v...  20.2 us
    unnamed x59, local copies, waits for them, and re-layouts  8.61 us

profile of v7, /device:TPU:0, one launch (start us, length us, event | category | flops | bytes accessed | tf_op | source)
XLA Modules:
  0.0 348.5 jit_solution(18301537387910831081)
XLA Ops:
  0.7 0.7 tile.20
  1.4 0.7 tile.8
  2.3 1.4 select_maximum_fusion.refs_0_
  3.7 1.0 copy.64
  4.7 1.0 convert_bitcast_fusion.1
  5.7 0.7 pad_maximum_fusion.refs_1_
  6.4 2.1 convert_element_type.20.refs_2_
  8.5 81.5 %attention.1 = (f32[2,1024]{1,0:T(2,128)}, bf16[1024,128]{1,0:T(8,128)(2,1)}, bf16[4,3,128,1024]{3,2,1,0:T(8,128)(2,1)}, bf16[3,1024,1024]{2,1,0:T(8,128)(2,1)},...) custom-call(f32[40,128]{1,0:T(8,128)} %select_maximum_fusion.refs_0_, ...), custom_call_target="tpu_custom_call" | custom-call | flops 1 | bytes 1 | tf_op jit(solution)/shard_map/attention/pallas_call | solution.py:240
  89.9 140.2 %experts.1 = (bf16[2,8,256,1024]{3,2,1,0:T(8,128)(2,1)}, f32[8,2,8,256]{3,2,1,0:T(8,128)}, f32[256,1024]{1,0:T(8,128)}, bf16[4,3,128,1024]{3,2,1,0:T(8,128)(2,1)...) custom-call(bf16[256,1024]{1,0:T(8,128)(2,1)} %get-tuple-element.61.refs_0_.refs_11_, ...), custom_call_target="tpu_custom_call" | custom-call | flops 1 | bytes 1 | tf_op jit(solution)/shard_map/experts/pallas_call | solution.py:240
  230.1 89.8 %attention_back.1 = (f32[256,1024]{1,0:T(8,128)}, f32[256,1024]{1,0:T(8,128)}, bf16[4,3,128,1024]{3,2,1,0:T(8,128)(2,1)}, f32[3,128,256]{2,1,0:T(8,128)}, f32[40,128]{1,0:T(8,128)}) custom-call(bf16[3,1024,1024]{2,1,0:T(8,128)(2,1)} %get-tuple-element.60.refs_0_, ...), custom_call_target="tpu_custom_call", output_to_operand_aliasing={{2}: (2, {})} | custom-call | flops 1 | bytes 1 | tf_op jit(solution)/shard_map/attention_back/pallas_call | solution.py:240
  320.0 8.5 %multiply_subtract_fusion.1 = (f32[4,128,1024]{2,1,0:T(8,128)}, f32[4,128,1024]{2,1,0:T(8,128)}, f32[4,128,1024]{2,1,0:T(8,128)}, f32[4,128,1024]{2,1,0:T(8,128)}) fusion(f32[4,128,1024]{2,1,0:T(8,128)} %refs_5_.2, f32[4,128,1024]{2,1,0:T(8,128)} %param.54, f32[4,128,1024]{2,1,0:T(8,128)} %param.55, bf16[4,3,128,1024]{3,2,1,0:T(8,128)(2,1)} %get-tuple-element.85, ...), kind=kLoop, calls=%fused_computation.7 | loop fusion | flops 9437184 | bytes 16777216 | tf_op jit(solution)/shard_map/sub | solution.py:1419
  328.5 1.1 copy-done.2
  329.7 1.2 copy-done.3
  330.9 8.6 %multiply_subtract_fusion = (f32[4,2,128,1024]{3,2,1,0:T(8,128)}, f32[4,2,128,1024]{3,2,1,0:T(8,128)}, f32[4,2,128,1024]{3,2,1,0:T(8,128)}, f32[4,2,128,1024]{3,2,1,0:T(8,128)}) fusion(f32[4,2,128,1024]{3,2,1,0:T(8,128)S(1)} %copy-done, f32[4,2,128,1024]{3,2,1,0:T(8,128)S(1)} %copy-done.2, f32[4,2,128,1024]{3,2,1,0:T(8,128)S(1)} %copy-done.3, ...), kind=kLoop, calls=%fused_computation.2 | loop fusion | flops 18874368 | bytes 33554432 | tf_op jit(solution)/shard_map/sub | solution.py:1419
  339.8 1.1 multiply_subtract_fusion.3
  341.2 0.8 copy.70
  341.9 0.8 copy.71
  342.7 0.8 copy.72
  343.4 0.8 copy.69
  344.2 0.6 multiply_subtract_fusion.5
  344.9 0.6 multiply_subtract_fusion.7
  345.5 0.6 multiply_subtract_fusion.6
  346.1 1.0 copy.76
  347.1 1.0 copy.77
  (59 shorter events, 0.7 us)
Async XLA Ops:
  319.9 8.6 %copy-start = (f32[4,2,128,1024]{3,2,1,0:T(8,128)S(1)}, f32[4,2,128,1024]{3,2,1,0:T(8,128)}, u32[]{:S(2)}) copy-start(f32[4,2,128,1024]{3,2,1,0:T(8,128)} %refs_4_.1) | copy-start | bytes 12582916
  319.9 8.6 %copy-start.1 = (bf16[4,3,128,1024]{3,2,1,0:T(8,128)(2,1)S(1)}, bf16[4,3,128,1024]{3,2,1,0:T(8,128)(2,1)}, u32[]{:S(2)}) copy-start(bf16[4,3,128,1024]{3,2,1,0:T(8,128)(2,1)} %get-tuple-element.85) | copy-start | bytes 9437188
  320.0 9.7 %copy-start.2 = (f32[4,2,128,1024]{3,2,1,0:T(8,128)S(1)}, f32[4,2,128,1024]{3,2,1,0:T(8,128)}, u32[]{:S(2)}) copy-start(f32[4,2,128,1024]{3,2,1,0:T(8,128)} %param.52) | copy-start | bytes 12582916
  320.0 10.9 %copy-start.3 = (f32[4,2,128,1024]{3,2,1,0:T(8,128)S(1)}, f32[4,2,128,1024]{3,2,1,0:T(8,128)}, u32[]{:S(2)}) copy-start(f32[4,2,128,1024]{3,2,1,0:T(8,128)} %param.53) | copy-start | bytes 12582916
  330.9 8.8 %copy-start.6 = (f32[3,128,256]{2,1,0:T(8,128)S(1)}, f32[3,128,256]{2,1,0:T(8,128)}, u32[]{:S(2)}) copy-start(f32[3,128,256]{2,1,0:T(8,128)} %get-tuple-element.83) | copy-start | bytes 1179652
  330.9 8.8 %copy-start.7 = (f32[128,256]{1,0:T(8,128)S(1)}, f32[128,256]{1,0:T(8,128)}, u32[]{:S(2)}) copy-start(f32[128,256]{1,0:T(8,128)} %param.34) | copy-start | bytes 393220
  330.9 8.8 %copy-start.8 = (f32[128,256]{1,0:T(8,128)S(1)}, f32[128,256]{1,0:T(8,128)}, u32[]{:S(2)}) copy-start(f32[128,256]{1,0:T(8,128)} %param.33) | copy-start | bytes 393220
  330.9 8.8 %copy-start.9 = (f32[128,256]{1,0:T(8,128)S(1)}, f32[128,256]{1,0:T(8,128)}, u32[]{:S(2)}) copy-start(f32[128,256]{1,0:T(8,128)} %param.44) | copy-start | bytes 393220
  330.9 8.8 %copy-start.10 = (f32[128,256]{1,0:T(8,128)S(1)}, f32[128,256]{1,0:T(8,128)}, u32[]{:S(2)}) copy-start(f32[128,256]{1,0:T(8,128)} %param.45) | copy-start | bytes 393220
  330.9 8.8 %copy-start.11 = (f32[128,256]{1,0:T(8,128)S(1)}, f32[128,256]{1,0:T(8,128)}, u32[]{:S(2)}) copy-start(f32[128,256]{1,0:T(8,128)} %param.43) | copy-start | bytes 393220
  330.9 8.8 %copy-start.12 = (f32[128,256]{1,0:T(8,128)S(1)}, f32[128,256]{1,0:T(8,128)}, u32[]{:S(2)}) copy-start(f32[128,256]{1,0:T(8,128)} %param.42) | copy-start | bytes 393220
  330.9 9.9 %copy-start.13 = (f32[256,128]{1,0:T(8,128)S(1)}, f32[256,128]{1,0:T(8,128)}, u32[]{:S(2)}) copy-start(f32[256,128]{1,0:T(8,128)} %param.46) | copy-start | bytes 393220
  330.9 10.0 %copy-start.14 = (f32[256,128]{1,0:T(8,128)S(1)}, f32[256,128]{1,0:T(8,128)}, u32[]{:S(2)}) copy-start(f32[256,128]{1,0:T(8,128)} %param.47) | copy-start | bytes 393220
  339.6 4.6 %copy-start.15 = (f32[32,32]{1,0:T(8,128)S(1)}, f32[32,32]{1,0:T(8,128)}, u32[]{:S(2)}) copy-start(f32[32,32]{1,0:T(8,128)} %param.37) | copy-start | bytes 12292
  339.6 4.6 %copy-start.16 = (f32[32,32]{1,0:T(8,128)S(1)}, f32[32,32]{1,0:T(8,128)}, u32[]{:S(2)}) copy-start(f32[32,32]{1,0:T(8,128)} %param.50) | copy-start | bytes 12292
  339.6 4.6 %copy-start.17 = (f32[32,32]{1,0:T(8,128)S(1)}, f32[32,32]{1,0:T(8,128)}, u32[]{:S(2)}) copy-start(f32[32,32]{1,0:T(8,128)} %param.51) | copy-start | bytes 12292
  339.6 5.3 %copy-start.19 = (f32[32]{0:T(128)S(1)}, f32[32]{0:T(128)}, u32[]{:S(2)}) copy-start(f32[32]{0:T(128)} %param.32) | copy-start | bytes 388
  339.6 5.2 %copy-start.21 = (f32[32]{0:T(128)S(1)}, f32[32]{0:T(128)}, u32[]{:S(2)}) copy-start(f32[32]{0:T(128)} %param.40) | copy-start | bytes 388
  339.6 5.2 %copy-start.22 = (f32[32]{0:T(128)S(1)}, f32[32]{0:T(128)}, u32[]{:S(2)}) copy-start(f32[32]{0:T(128)} %param.41) | copy-start | bytes 388
  339.6 5.8 %copy-start.20 = (f32[32]{0:T(128)S(1)}, f32[32]{0:T(128)}, u32[]{:S(2)}) copy-start(f32[32]{0:T(128)} %param.36) | copy-start | bytes 388
  339.6 5.8 %copy-start.23 = (f32[32]{0:T(128)S(1)}, f32[32]{0:T(128)}, u32[]{:S(2)}) copy-start(f32[32]{0:T(128)} %param.48) | copy-start | bytes 388
  339.7 5.8 %copy-start.24 = (f32[32]{0:T(128)S(1)}, f32[32]{0:T(128)}, u32[]{:S(2)}) copy-start(f32[32]{0:T(128)} %param.49) | copy-start | bytes 388
  339.7 6.4 %copy-start.5 = (f32[256,1024]{1,0:T(8,128)S(1)}, f32[256,1024]{1,0:T(8,128)}, u32[]{:S(2)}) copy-start(f32[256,1024]{1,0:T(8,128)} %get-tuple-element.195) | copy-start | bytes 3145732
  339.7 7.3 %copy-start.4 = (f32[256,1024]{1,0:T(8,128)S(1)}, f32[256,1024]{1,0:T(8,128)}, u32[]{:S(2)}) copy-start(f32[256,1024]{1,0:T(8,128)} %get-tuple-element.196) | copy-start | bytes 3145732
  (1 other events, 4.6 us)
